TPU v7x, 256 devices: a whole 4x4x8 slice. The times are simulated.
256 devices in a mesh: slab: 16 (over z_hi, y, core), dir: 16 (over z_lo, x).
Axes of the slice: x: 4, y: 4, z: 8 (z_hi: 2, z_lo: 4; z = z_hi * 4 + z_lo), core: 2. Of those that a mesh axis runs over, the one named last changes fastest.
Arguments:
- currents: float32 [32, 32, 6, 8, 2, 128], P('slab', 'dir'), may hold values from -6 to 6
- near_tiles: float32 [27, 2, 128, 128], replicated, may hold values from -0.078125 to 0.078125
- radiation: float32 [2, 1024, 128], replicated, may hold values from -0.5 to 0.5
- child_phase: float32 [8, 1024], replicated, may hold values from -3.140625 to 3.140625
- translators: float32 [316, 2, 1024], P(None, None, 'dir'), may hold values from -0.0625 to 0.0625
- far_targets: int32 [768, 16], replicated, may hold values from 0 to 767, as said below
- far_offsets: int32 [768, 16], replicated, may hold values from 0 to 315, as said below
Outputs:
- applied: float32 [32, 32, 6, 8, 2, 128], P('slab', 'dir')
Inputs may be any that keep to these rules, and one draw needn't show every extreme that they name: For each source parent s, far_targets[s] holds 16 different parent numbers t inside the grid; along every grid dimension the parent coordinates of t and s differ by at most 3, and along at least one by 2 or more. far_offsets[s, f] names the translation operator of the coordinate difference between far_targets[s, f] and s; equal differences have equal operators and each of the 316 differences has its own.
All inputs are finite; a program needn't handle non-finite values.
Results may differ from a plain program's by a relative error of at most 0.0001.
Values sent between devices are 32-bit elements; how exact they have to be, the bound alone decides.
No kernel may reach another device: no remote copies, remote signals or barrier semaphores. Data moves between devices by JAX's collectives and lax.ppermute only.
A program may use at most 192 MiB of HBM per device.

v0:
```python
import functools

import jax
import jax.numpy as jnp
from jax import lax
from jax.experimental import pallas as pl
from jax.experimental.pallas import tpu as pltpu
from jax.sharding import PartitionSpec as P

F32 = jnp.float32
BF16 = jnp.bfloat16
AXES = ("slab", "dir")
VMEM_BYTES = 32 * 1024 * 1024
NT = (((1,), (1,)), ((), ()))
NN = (((1,), (0,)), ((), ()))


def linear(z_hi, y, core, d):
    return (z_hi * 8 + y * 2 + core) * 16 + d


def route_of(move):
    pairs = []
    for s in range(16):
        for d in range(16):
            to = move(s // 8, s // 2 % 4, s % 2, d)
            if to is not None:
                pairs.append((s * 16 + d, linear(*to)))
    return pairs


def exchange_groups():
    return [
        [linear(z_hi, j // 2, j % 2, d) for z_hi in range(2) for d in range(16)] for j in range(8)
    ]


def split(x):
    hi = x.astype(BF16)
    lo = (x - hi.astype(F32)).astype(BF16)
    return hi, lo


def dot3(a, b, dims):
    a_hi, a_lo = a
    b_hi, b_lo = b
    dot = functools.partial(lax.dot_general, dimension_numbers=dims, preferred_element_type=F32)
    return dot(a_hi, b_hi) + (dot(a_lo, b_hi) + dot(a_hi, b_lo))


def lane_sign(shape):
    lane = lax.broadcasted_iota(jnp.int32, shape, len(shape) - 1) % 128
    return jnp.where(lane < 64, -1.0, 1.0).astype(F32)


def times_i(x):
    return lane_sign(x.shape) * pltpu.roll(x, 64, 1)


def swap_bits(x):
    row = lax.broadcasted_iota(jnp.int32, x.shape, 0) // 4 % 2
    lane = lax.broadcasted_iota(jnp.int32, x.shape, 1) // 32 % 2
    other = pltpu.roll(x, 4, 0)
    moved = jnp.where(lane == 1, pltpu.roll(other, 32, 1), pltpu.roll(other, 96, 1))
    return jnp.where(row == lane, x, moved)


def radiation_block(rad_ref, start):
    re = rad_ref[0, pl.ds(start, 128), :]
    im = rad_ref[1, pl.ds(start, 128), :]
    top = jnp.concatenate([re, -im], axis=1)
    low = jnp.concatenate([im, re], axis=1)
    return split(jnp.concatenate([top[:64], low[:64], top[64:], low[64:]], axis=0))


def phase_block(phase_ref, start):
    phase = phase_ref[:, pl.ds(start, 128)]
    lane = lax.broadcasted_iota(jnp.int32, phase.shape, 1)

    def doubled(v):
        turned = pltpu.roll(v, 64, 1)
        return jnp.concatenate(
            [jnp.where(lane < 64, v, turned), jnp.where(lane < 64, turned, v)], axis=1
        )

    return doubled(jnp.cos(phase)), doubled(jnp.sin(phase))


def leaf_row(child, parent):
    i, j, l = child // 4, child // 2 % 2, child % 2
    return ((i * 2 + j) * 6 + parent * 2 + l) * 8


def aggregate_kernel(cur_ref, rad_ref, phase_ref, out_ref):
    rows = cur_ref.shape[0] // 2
    x = jnp.concatenate(
        [cur_ref[pl.ds(0, rows, stride=2), :], cur_ref[pl.ds(1, rows, stride=2), :]], axis=1
    )
    x = split(x)

    @pl.loop(0, 8)
    def _(step):
        start = pl.multiple_of(step * 128, 128)
        leaf = dot3(x, radiation_block(rad_ref, start), NT)
        cos, sin = phase_block(phase_ref, start)
        for parent in range(3):
            a = jnp.zeros((8, 256), F32)
            b = jnp.zeros((8, 256), F32)
            for child in range(8):
                row = leaf_row(child, parent)
                part = leaf[row : row + 8]
                a = a + cos[child : child + 1] * part
                b = b + sin[child : child + 1] * part
            for pair in range(2):
                lanes = slice(pair * 128, pair * 128 + 128)
                block = swap_bits(a[:, lanes] + times_i(b[:, lanes]))
                d = step * 2 + pair
                out_ref[d, parent] = block[:4]
                out_ref[16 + d, parent] = block[4:]


def disaggregate_kernel(in_ref, rad_ref, phase_ref, near_ref, out_ref, acc_ref):
    acc_ref[...] = near_ref[...]

    @pl.loop(0, 8)
    def _(step):
        start = pl.multiple_of(step * 128, 128)
        cos, sin = phase_block(phase_ref, start)
        parents = []
        for parent in range(3):
            halves = []
            for pair in range(2):
                d = step * 2 + pair
                block = jnp.concatenate([in_ref[d, parent], in_ref[16 + d, parent]], axis=0)
                halves.append(swap_bits(block))
            turned = jnp.concatenate([times_i(h) for h in halves], axis=1)
            parents.append((jnp.concatenate(halves, axis=1), turned))
        rows = [None] * 24
        for parent in range(3):
            plain, turned = parents[parent]
            for child in range(8):
                rows[leaf_row(child, parent) // 8] = (
                    cos[child : child + 1] * plain - sin[child : child + 1] * turned
                )
        children = split(jnp.concatenate(rows, axis=0))
        acc_ref[...] += dot3(children, radiation_block(rad_ref, start), NN)

    rows = acc_ref.shape[0]
    out_ref[pl.ds(0, rows, stride=2), :] = acc_ref[:, :128]
    out_ref[pl.ds(1, rows, stride=2), :] = acc_ref[:, 128:]


def near_kernel(own_ref, left_ref, right_ref, down_ref, up_ref, tiles_ref, out_ref, hi_ref, lo_ref, acc_ref):
    def put(ref, at_row, to_x, to_y):
        x = jnp.concatenate(
            [ref[pl.ds(at_row * 96, 48, stride=2), :], ref[pl.ds(at_row * 96 + 1, 48, stride=2), :]],
            axis=1,
        )
        hi, lo = split(x)
        hi_ref[to_x, to_y] = hi
        lo_ref[to_x, to_y] = lo

    for i in range(2):
        for j in range(2):
            put(own_ref, i * 2 + j, 1 + i, 1 + j)
        put(left_ref, i, 0, 1 + i)
        put(right_ref, i, 3, 1 + i)
    for i in range(4):
        put(down_ref, i, i, 0)
        put(up_ref, i, i, 3)
    acc_ref[...] = jnp.zeros_like(acc_ref)

    @pl.loop(0, 9)
    def _(step):
        dx = step // 3
        dy = step - dx * 3
        hi = hi_ref[pl.ds(dx, 2), pl.ds(dy, 2)].reshape(192, 256)
        lo = lo_ref[pl.ds(dx, 2), pl.ds(dy, 2)].reshape(192, 256)
        for dz in range(3):
            re = tiles_ref[step * 3 + dz, 0]
            im = tiles_ref[step * 3 + dz, 1]
            matrix = jnp.concatenate(
                [jnp.concatenate([re, -im], axis=1), jnp.concatenate([im, re], axis=1)], axis=0
            )
            y = dot3((hi, lo), split(matrix), NT).reshape(4, 48, 256)
            if dz == 0:
                acc_ref[:, 8:48] += y[:, 0:40]
            elif dz == 1:
                acc_ref[...] += y
            else:
                acc_ref[:, 0:40] += y[:, 8:48]

    out_ref[...] = acc_ref[...].reshape(192, 256)


def translate_kernel(words_ref, table_ref, src_ref, keep_ref, swap_ref, far_ref, acc_ref):
    acc_ref[...] = jnp.zeros_like(acc_ref)
    row = lax.broadcasted_iota(jnp.int32, (8, 128), 0)

    @pl.loop(0, 96)
    def _(s):
        part = src_ref[s]
        both = jnp.concatenate([part, part], axis=0)
        both = jnp.where(row < 4, both, times_i(both))
        slots, sums = [], []
        for f in range(16):
            word = words_ref[s * 16 + f]
            slot = word >> 9
            kind = word & 511
            slots.append(slot)
            sums.append(acc_ref[slot] + table_ref[kind] * both)
        for f in range(16):
            acc_ref[slots[f]] = sums[f]

    for ref, base in ((keep_ref, 0), (swap_ref, 288)):
        for block in range(3):
            part = acc_ref[pl.ds(base + block * 96, 96)]
            ref[block] = part[:, :4] + part[:, 4:]
    part = acc_ref[pl.ds(576, 96)]
    far_ref[...] = part[:, :4] + part[:, 4:]


def fold_kernel(keep_ref, got_ref, back_ref, mid_ref, ahead_ref):
    back_ref[...] = keep_ref[0] + got_ref[0]
    mid_ref[...] = keep_ref[1] + got_ref[1]
    ahead_ref[...] = keep_ref[2] + got_ref[2]


def call(kernel, out_shape, scratch=(), in_specs=None, flops=0, moved=0):
    extra = {} if in_specs is None else {"in_specs": in_specs}
    return pl.pallas_call(
        kernel,
        out_shape=out_shape,
        scratch_shapes=list(scratch),
        compiler_params=pltpu.CompilerParams(vmem_limit_bytes=VMEM_BYTES),
        cost_estimate=pl.CostEstimate(flops=flops, bytes_accessed=moved, transcendentals=0),
        **extra,
    )


def f32(*shape):
    return jax.ShapeDtypeStruct(shape, F32)


def pair_words(far_targets, far_offsets):
    slab = lax.axis_index("slab")
    ring = slab % 8
    y, core = ring // 2, ring % 2
    targets = lax.dynamic_slice_in_dim(far_targets.reshape(2, 8, 48, 16), ring, 1, 1)
    kinds = lax.dynamic_slice_in_dim(far_offsets.reshape(2, 8, 48, 16), ring, 1, 1)
    to_slab, row = targets // 48, targets % 48
    half, to_ring = to_slab // 8, to_slab % 8
    step = (to_ring // 2 - y + 4) % 4
    near_block = (step + 1) % 4 + jnp.where(to_ring % 2 == core, 0, 3)
    block = jnp.where(step == 2, 6, near_block)
    slot = block * 96 + half * 48 + row
    return (slot * 512 + kinds).reshape(-1)


def operator_table(translators):
    count = translators.shape[0]
    half = lax.axis_index("slab") // 8
    own = lax.dynamic_slice_in_dim(translators, half * 32, 32, 2)
    lanes = jnp.concatenate([own] * 4, axis=2)
    return jnp.broadcast_to(lanes[:, :, None, :], (count, 2, 4, 128)).reshape(count, 8, 128)


def moved_by(block, move):
    return lax.ppermute(block, AXES, route_of(move))


def spread(block, groups):
    return lax.all_to_all(
        block, AXES, split_axis=0, concat_axis=0, axis_index_groups=groups, tiled=True
    )


def halo(currents):
    def along_slab(block, distance):
        return lax.ppermute(
            block, "slab", [(i, i + distance) for i in range(16) if 0 <= i + distance < 16]
        )

    def along_dir(block, distance):
        return lax.ppermute(
            block, "dir", [(i, i + distance) for i in range(16) if 0 <= i + distance < 16]
        )

    left = along_slab(currents[1:2], 1)
    right = along_slab(currents[0:1], -1)
    tall = jnp.concatenate([left, currents, right], axis=0)
    down = along_dir(tall[:, 1:2], 1)
    up = along_dir(tall[:, 0:1], -1)
    return left, right, down, up


def per_device(currents, near_tiles, radiation, child_phase, translators, far_targets, far_offsets):
    groups = exchange_groups()
    rows = currents.reshape(384, 128)
    words = pair_words(far_targets, far_offsets)
    table = operator_table(translators)

    patterns = call(
        aggregate_kernel, f32(32, 3, 4, 128), flops=600_000_000, moved=2_000_000
    )(rows, radiation, child_phase)
    moved = spread(patterns, groups)

    left, right, down, up = halo(currents)
    near = call(
        near_kernel,
        f32(192, 256),
        [pltpu.VMEM((4, 4, 48, 256), BF16), pltpu.VMEM((4, 4, 48, 256), BF16), pltpu.VMEM((4, 48, 256), F32)],
        flops=2_000_000_000,
        moved=5_000_000,
    )(
        rows,
        left.reshape(192, 128),
        right.reshape(192, 128),
        down.reshape(384, 128),
        up.reshape(384, 128),
        near_tiles,
    )

    vmem = pl.BlockSpec(memory_space=pltpu.VMEM)
    keep, swap, far = call(
        translate_kernel,
        (f32(3, 96, 4, 128), f32(3, 96, 4, 128), f32(96, 4, 128)),
        [pltpu.VMEM((672, 8, 128), F32)],
        in_specs=[pl.BlockSpec(memory_space=pltpu.SMEM), vmem, vmem],
        flops=100_000_000,
        moved=3_000_000,
    )(words, table, moved.reshape(96, 4, 128))
    far_in = moved_by(far, lambda z_hi, y, core, d: (z_hi, (y + 2) % 4, 1 - core, d))
    swap_in = moved_by(swap, lambda z_hi, y, core, d: (z_hi, y, 1 - core, d))
    back, mid, ahead = call(
        fold_kernel, (f32(96, 4, 128), f32(96, 4, 128), f32(96, 4, 128)), flops=1_000_000, moved=2_000_000
    )(keep, swap_in)
    back_in = moved_by(back, lambda z_hi, y, core, d: (z_hi, (y + 3) % 4, core, d))
    ahead_in = moved_by(ahead, lambda z_hi, y, core, d: (z_hi, (y + 1) % 4, core, d))
    incoming = (mid + far_in) + (back_in + ahead_in)
    returned = spread(incoming.reshape(32, 3, 4, 128), groups)

    applied = call(
        disaggregate_kernel,
        f32(384, 128),
        [pltpu.VMEM((192, 256), F32)],
        flops=600_000_000,
        moved=2_000_000,
    )(returned, radiation, child_phase, near)
    return applied.reshape(currents.shape)


def solution(mesh):
    in_specs = (
        P("slab", "dir", None, None, None, None),
        P(),
        P(),
        P(),
        P(None, None, "dir"),
        P(),
        P(),
    )
    out_specs = P("slab", "dir", None, None, None, None)
    return jax.shard_map(
        per_device, mesh=mesh, in_specs=in_specs, out_specs=out_specs, check_vma=False
    )
```

profile of v0, /device:TPU:8, one launch (start us, length us, event | category | flops | bytes accessed | tf_op | source)
XLA Modules:
  0.0 87.2 jit_solution(650214460181080917)
XLA Ops:
  0.0 0.0 copy-start
  0.0 0.0 copy-start.1
  0.0 1.0 %copy-done.1 = f32[2,2,6,8,2,128]{5,4,3,2,1,0:T(2,128)S(1)} copy-done((f32[2,2,6,8,2,128]{5,4,3,2,1,0:T(2,128)S(1)}, f32[2,2,6,8,2,128]{5,4,3,2,1,0:T(2,128)}, u32[]{:S(2)}) %copy-start.1) | copy-done | bytes 196632
  1.0 0.0 copy-start.4
  1.0 1.2 %copy-done.4 = f32[2,1024,128]{2,1,0:T(8,128)S(1)} copy-done((f32[2,1024,128]{2,1,0:T(8,128)S(1)}, f32[2,1024,128]{2,1,0:T(8,128)}, u32[]{:S(2)}) %copy-start.4) | copy-done | bytes 1048600
  2.2 0.8 copy-done.6
  3.0 4.4 %shard_map.73 = f32[32,3,4,128]{3,2,1,0:T(4,128)} custom-call(f32[384,128]{1,0:T(8,128)S(1)} %bitcast.23, f32[2,1024,128]{2,1,0:T(8,128)S(1)} %copy-done.4, f32[8,1024]{1,0:T(8,128)S(1)} %copy-done.6), custom_call_target="tpu_custom_call" | custom-call | flops 600000000 | bytes 2000000 | tf_op jit(solution)/shard_map/pallas_call | solution.py:303
  7.4 11.3 %all-to-all-start = ((f32[32,3,4,128]{3,2,1,0:T(4,128)}), f32[32,3,4,128]{3,2,1,0:T(4,128)S(1)}, u32[]{:S(2)}, u32[]{:S(2)}) async-start(f32[32,3,4,128]{3,2,1,0:T(4,128)} %shard_map.73), calls=%async_computation | async-start | bytes 393216 | tf_op jit(solution)/shard_map/all_to_all | solution.py:273
  18.7 0.0 copy-done
  18.8 0.2 copy.11
  19.0 0.0 copy-done.8
  19.1 0.1 reshape.37
  19.2 0.0 copy-done.9
  19.2 0.1 reshape.38
  19.3 0.1 copy.12
  19.4 0.1 copy.13
  19.5 0.2 fusion.10
  19.7 0.1 reshape.39.words_ref
  19.8 10.6 %all-to-all-done = f32[32,3,4,128]{3,2,1,0:T(4,128)S(1)} async-done(((f32[32,3,4,128]{3,2,1,0:T(4,128)}), f32[32,3,4,128]{3,2,1,0:T(4,128)S(1)}, u32[]{:S(2)}, u32[]{:S(2)}) %all-to-all-start) | async-done | bytes 196640 | tf_op jit(solution)/shard_map/all_to_all | solution.py:273
  30.4 0.2 broadcast_in_dim.15
  30.6 9.1 %shard_map.74 = (f32[3,96,4,128]{3,2,1,0:T(4,128)S(1)}, f32[3,96,4,128]{3,2,1,0:T(4,128)S(1)}, f32[96,4,128]{2,1,0:T(4,128)S(1)}) custom-call(s32[1536]{0:T(1024)S(1)} %reshape.39.words_ref, f32[316,8,128]{2,1,0:T(8,128)S(1)} %bitcast.22, f32[96,4,128]{2,1,0:T(4,128)S(1)} %bitcast.25), custom_call_target="tpu_custom_call" | custom-call | flops 100000000 | bytes 3000000 | tf_op jit(solution)/shard_map/pallas_call | solution.py:325
  39.7 0.1 collective-permute-start
  39.8 0.0 copy-done.2
  39.8 2.4 %collective-permute-start.4 = (f32[1,2,6,8,2,128]{5,4,3,2,1,0:T(2,128)S(1)}, f32[1,2,6,8,2,128]{5,4,3,2,1,0:T(2,128)S(1)}, u32[]{:S(2)}, u32[]{:S(2)}) collective-permute-start(f32[1,2,6,8,2,128]{5,4,3,2,1,0:T(2,128)S(1)} %get-tuple-element.20), channel_id=1, source_target_pairs={{0,16},{16,32},{32,48},{48,64},{64,80},{80,96},{96,112},{112,128},... | collective-permute-start | bytes 294920 | tf_op jit(solution)/shard_map/ppermute | solution.py:280
  42.2 3.2 %collective-permute-start.5 = (f32[1,2,6,8,2,128]{5,4,3,2,1,0:T(2,128)S(1)}, f32[1,2,6,8,2,128]{5,4,3,2,1,0:T(2,128)S(1)}, u32[]{:S(2)}, u32[]{:S(2)}) collective-permute-start(f32[1,2,6,8,2,128]{5,4,3,2,1,0:T(2,128)S(1)} %get-tuple-element.19), channel_id=1, source_target_pairs={{16,0},{32,16},{48,32},{64,48},{80,64},{96,80},{112,96},{128,112},... | collective-permute-start | bytes 294920 | tf_op jit(solution)/shard_map/ppermute | solution.py:280
  45.4 0.4 collective-permute-done.4
  45.8 1.8 %collective-permute-done.5 = f32[1,2,6,8,2,128]{5,4,3,2,1,0:T(2,128)S(1)} collective-permute-done((f32[1,2,6,8,2,128]{5,4,3,2,1,0:T(2,128)S(1)}, f32[1,2,6,8,2,128]{5,4,3,2,1,0:T(2,128)S(1)}, u32[]{:S(2)}, u32[]{:S(2)}) %collective-permute-start.5) | collective-permute-done | bytes 98336 | tf_op jit(solution)/shard_map/ppermute | solution.py:280
  47.6 9.6 %collective-permute-start.1 = (f32[96,4,128]{2,1,0:T(4,128)S(1)}, f32[96,4,128]{2,1,0:T(4,128)S(1)}, u32[]{:S(2)}, u32[]{:S(2)}) collective-permute-start(f32[96,4,128]{2,1,0:T(4,128)S(1)} %get-tuple-element.14), channel_id=1, source_target_pairs={{0,80},{1,81},{2,82},{3,83},{4,84},{5,85},{6,86},{7,87},{8,88},{9,... | collective-permute-start | bytes 589832 | tf_op jit(solution)/shard_map/ppermute | solution.py:269
  57.2 0.0 collective-permute-done.got_ref
  57.2 0.2 shard_map.75
  57.4 0.1 collective-permute-start.2
  57.4 2.0 %collective-permute-start.3 = (f32[96,4,128]{2,1,0:T(4,128)S(1)}, f32[96,4,128]{2,1,0:T(4,128)S(1)}, u32[]{:S(2)}, u32[]{:S(2)}) collective-permute-start(f32[96,4,128]{2,1,0:T(4,128)S(1)} %get-tuple-element.16), channel_id=1, source_target_pairs={{0,32},{1,33},{2,34},{3,35},{4,36},{5,37},{6,38},{7,39},{8,40},{9,... | collective-permute-start | bytes 589832 | tf_op jit(solution)/shard_map/ppermute | solution.py:269
  59.5 2.2 %collective-permute-start.6 = (f32[4,1,6,8,2,128]{5,4,3,2,1,0:T(2,128)S(1)}, f32[4,1,6,8,2,128]{5,4,3,2,1,0:T(2,128)S(1)}, u32[]{:S(2)}, u32[]{:S(2)}) collective-permute-start(f32[4,1,6,8,2,128]{5,4,3,2,1,0:T(2,128)S(1)} %get-tuple-element.18), channel_id=1, source_target_pairs={{0,1},{1,2},{2,3},{3,4},{4,5},{5,6},{6,7},{7,8},{8,9},{9,10},{10,1... | collective-permute-start | bytes 589832 | tf_op jit(solution)/shard_map/ppermute | solution.py:285
  61.6 1.3 %collective-permute-start.7 = (f32[4,1,6,8,2,128]{5,4,3,2,1,0:T(2,128)S(1)}, f32[4,1,6,8,2,128]{5,4,3,2,1,0:T(2,128)S(1)}, u32[]{:S(2)}, u32[]{:S(2)}) collective-permute-start(f32[4,1,6,8,2,128]{5,4,3,2,1,0:T(2,128)S(1)} %get-tuple-element.17), channel_id=1, source_target_pairs={{1,0},{2,1},{3,2},{4,3},{5,4},{6,5},{7,6},{8,7},{9,8},{10,9},{11,1... | collective-permute-start | bytes 589832 | tf_op jit(solution)/shard_map/ppermute | solution.py:285
  62.9 0.0 collective-permute-done.1
  63.0 0.1 collective-permute-done.2
  63.1 0.7 collective-permute-done.3
  63.8 0.7 add_add_fusion
  64.5 8.1 %all-to-all-start.1 = ((f32[32,3,4,128]{3,2,1,0:T(4,128)}), f32[32,3,4,128]{3,2,1,0:T(4,128)S(1)}, u32[]{:S(2)}, u32[]{:S(2)}) async-start(f32[32,3,4,128]{3,2,1,0:T(4,128)} %bitcast.3), calls=%async_computation.1 | async-start | bytes 393216 | tf_op jit(solution)/shard_map/all_to_all | solution.py:273
  72.6 0.0 collective-permute-done.6
  72.6 0.0 collective-permute-done.7
  72.6 0.0 copy-start.3
  72.6 2.0 %copy-done.3 = f32[27,2,128,128]{3,2,1,0:T(8,128)S(1)} copy-done((f32[27,2,128,128]{3,2,1,0:T(8,128)S(1)}, f32[27,2,128,128]{3,2,1,0:T(8,128)}, u32[]{:S(2)}) %copy-start.3) | copy-done | bytes 3538968
  74.6 5.1 %shard_map.76.near_ref = f32[192,256]{1,0:T(8,128)S(1)} custom-call(f32[384,128]{1,0:T(8,128)S(1)} %bitcast.24, f32[192,128]{1,0:T(8,128)S(1)} %bitcast.27, f32[192,128]{1,0:T(8,128)S(1)} %bitcast.28, f32[384,128]{1,0:T(8,128)S(1)} %bitcast.29, f32[384,128]{1,0:T(8,128)S(1)} %bitcast.30, f32[27,2,128,128]{3,2,1,0:T(8,128)S(1)} %copy-done.3), custom_call_target="tpu_custom_call" | custom-call | flops 2000000000 | bytes 5000000 | tf_op jit(solution)/shard_map/pallas_call | solution.py:309
  79.8 3.9 %all-to-all-done.1.in_ref = f32[32,3,4,128]{3,2,1,0:T(4,128)S(1)} async-done(((f32[32,3,4,128]{3,2,1,0:T(4,128)}), f32[32,3,4,128]{3,2,1,0:T(4,128)S(1)}, u32[]{:S(2)}, u32[]{:S(2)}) %all-to-all-start.1) | async-done | bytes 196640 | tf_op jit(solution)/shard_map/all_to_all | solution.py:273
  83.6 0.0 copy-done.5
  83.6 0.0 copy-done.7
  83.6 3.6 %shard_map.77 = f32[384,128]{1,0:T(8,128)} custom-call(f32[32,3,4,128]{3,2,1,0:T(4,128)S(1)} %all-to-all-done.1.in_ref, f32[2,1024,128]{2,1,0:T(8,128)S(1)} %copy-done.5, f32[8,1024]{1,0:T(8,128)S(1)} %copy-done.7, f32[192,256]{1,0:T(8,128)S(1)} %shard_map.76.near_ref), custom_call_target="tpu_custom_call" | custom-call | flops 600000000 | bytes 2000000 | tf_op jit(solution)/shard_map/pallas_call | solution.py:343
  (14 shorter events, 0.2 us)
Async XLA Ops:
  0.0 18.7 %copy-start = (f32[316,2,64]{0,2,1:T(8,128)S(1)}, f32[316,2,64]{0,2,1:T(8,128)}, u32[]{:S(2)}) copy-start(f32[316,2,64]{0,2,1:T(8,128)} %param.11) | copy-start | bytes 485380
  0.0 1.0 %copy-start.1 = (f32[2,2,6,8,2,128]{5,4,3,2,1,0:T(2,128)S(1)}, f32[2,2,6,8,2,128]{5,4,3,2,1,0:T(2,128)}, u32[]{:S(2)}) copy-start(f32[2,2,6,8,2,128]{5,4,3,2,1,0:T(2,128)} %param.7) | copy-start | bytes 589828
  1.0 1.2 %copy-start.4 = (f32[2,1024,128]{2,1,0:T(8,128)S(1)}, f32[2,1024,128]{2,1,0:T(8,128)}, u32[]{:S(2)}) copy-start(f32[2,1024,128]{2,1,0:T(8,128)} %rad_ref.3) | copy-start | bytes 3145732
  2.2 0.8 copy-start.6
  3.0 16.1 %copy-start.8 = (s32[768,16]{0,1:T(8,128)S(1)}, s32[768,16]{0,1:T(8,128)}, u32[]{:S(2)}) copy-start(s32[768,16]{0,1:T(8,128)} %param.12) | copy-start | bytes 147460
  3.0 16.2 %copy-start.9 = (s32[768,16]{0,1:T(8,128)S(1)}, s32[768,16]{0,1:T(8,128)}, u32[]{:S(2)}) copy-start(s32[768,16]{0,1:T(8,128)} %param.13) | copy-start | bytes 147460
  3.0 36.8 %copy-start.2 = (f32[2,2,6,8,2,128]{5,4,3,2,1,0:T(2,128)S(1)}, f32[2,2,6,8,2,128]{5,4,3,2,1,0:T(2,128)}, u32[]{:S(2)}) copy-start(f32[2,2,6,8,2,128]{5,4,3,2,1,0:T(2,128)} %param.7) | copy-start | bytes 589828
  7.4 23.0 %all-to-all-start = ((f32[32,3,4,128]{3,2,1,0:T(4,128)}), f32[32,3,4,128]{3,2,1,0:T(4,128)S(1)}, u32[]{:S(2)}, u32[]{:S(2)}) async-start(f32[32,3,4,128]{3,2,1,0:T(4,128)} %shard_map.73), calls=%async_computation | async-start | bytes 393216 | tf_op jit(solution)/shard_map/all_to_all | solution.py:273
  39.7 17.5 %collective-permute-start = (f32[3,96,4,128]{3,2,1,0:T(4,128)S(1)}, f32[3,96,4,128]{3,2,1,0:T(4,128)S(1)}, u32[]{:S(2)}, u32[]{:S(2)}) collective-permute-start(f32[3,96,4,128]{3,2,1,0:T(4,128)S(1)} %get-tuple-element.12), channel_id=1, source_target_pairs={{0,16},{1,17},{2,18},{3,19},{4,20},{5,21},{6,22},{7,23},{8,24},{9,... | collective-permute-start | bytes 1769480 | tf_op jit(solution)/shard_map/ppermute | solution.py:269
  39.8 5.9 %collective-permute-start.4 = (f32[1,2,6,8,2,128]{5,4,3,2,1,0:T(2,128)S(1)}, f32[1,2,6,8,2,128]{5,4,3,2,1,0:T(2,128)S(1)}, u32[]{:S(2)}, u32[]{:S(2)}) collective-permute-start(f32[1,2,6,8,2,128]{5,4,3,2,1,0:T(2,128)S(1)} %get-tuple-element.20), channel_id=1, source_target_pairs={{0,16},{16,32},{32,48},{48,64},{64,80},{80,96},{96,112},{112,128},... | collective-permute-start | bytes 294920 | tf_op jit(solution)/shard_map/ppermute | solution.py:280
  42.2 5.4 %collective-permute-start.5 = (f32[1,2,6,8,2,128]{5,4,3,2,1,0:T(2,128)S(1)}, f32[1,2,6,8,2,128]{5,4,3,2,1,0:T(2,128)S(1)}, u32[]{:S(2)}, u32[]{:S(2)}) collective-permute-start(f32[1,2,6,8,2,128]{5,4,3,2,1,0:T(2,128)S(1)} %get-tuple-element.19), channel_id=1, source_target_pairs={{16,0},{32,16},{48,32},{64,48},{80,64},{96,80},{112,96},{128,112},... | collective-permute-start | bytes 294920 | tf_op jit(solution)/shard_map/ppermute | solution.py:280
  47.6 15.3 %collective-permute-start.1 = (f32[96,4,128]{2,1,0:T(4,128)S(1)}, f32[96,4,128]{2,1,0:T(4,128)S(1)}, u32[]{:S(2)}, u32[]{:S(2)}) collective-permute-start(f32[96,4,128]{2,1,0:T(4,128)S(1)} %get-tuple-element.14), channel_id=1, source_target_pairs={{0,80},{1,81},{2,82},{3,83},{4,84},{5,85},{6,86},{7,87},{8,88},{9,... | collective-permute-start | bytes 589832 | tf_op jit(solution)/shard_map/ppermute | solution.py:269
  57.4 5.7 %collective-permute-start.2 = (f32[96,4,128]{2,1,0:T(4,128)S(1)}, f32[96,4,128]{2,1,0:T(4,128)S(1)}, u32[]{:S(2)}, u32[]{:S(2)}) collective-permute-start(f32[96,4,128]{2,1,0:T(4,128)S(1)} %get-tuple-element.15), channel_id=1, source_target_pairs={{0,96},{1,97},{2,98},{3,99},{4,100},{5,101},{6,102},{7,103},{8,104... | collective-permute-start | bytes 589832 | tf_op jit(solution)/shard_map/ppermute | solution.py:269
  57.4 6.4 %collective-permute-start.3 = (f32[96,4,128]{2,1,0:T(4,128)S(1)}, f32[96,4,128]{2,1,0:T(4,128)S(1)}, u32[]{:S(2)}, u32[]{:S(2)}) collective-permute-start(f32[96,4,128]{2,1,0:T(4,128)S(1)} %get-tuple-element.16), channel_id=1, source_target_pairs={{0,32},{1,33},{2,34},{3,35},{4,36},{5,37},{6,38},{7,39},{8,40},{9,... | collective-permute-start | bytes 589832 | tf_op jit(solution)/shard_map/ppermute | solution.py:269
  59.5 13.1 %collective-permute-start.6 = (f32[4,1,6,8,2,128]{5,4,3,2,1,0:T(2,128)S(1)}, f32[4,1,6,8,2,128]{5,4,3,2,1,0:T(2,128)S(1)}, u32[]{:S(2)}, u32[]{:S(2)}) collective-permute-start(f32[4,1,6,8,2,128]{5,4,3,2,1,0:T(2,128)S(1)} %get-tuple-element.18), channel_id=1, source_target_pairs={{0,1},{1,2},{2,3},{3,4},{4,5},{5,6},{6,7},{7,8},{8,9},{9,10},{10,1... | collective-permute-start | bytes 589832 | tf_op jit(solution)/shard_map/ppermute | solution.py:285
  61.6 11.0 %collective-permute-start.7 = (f32[4,1,6,8,2,128]{5,4,3,2,1,0:T(2,128)S(1)}, f32[4,1,6,8,2,128]{5,4,3,2,1,0:T(2,128)S(1)}, u32[]{:S(2)}, u32[]{:S(2)}) collective-permute-start(f32[4,1,6,8,2,128]{5,4,3,2,1,0:T(2,128)S(1)} %get-tuple-element.17), channel_id=1, source_target_pairs={{1,0},{2,1},{3,2},{4,3},{5,4},{6,5},{7,6},{8,7},{9,8},{10,9},{11,1... | collective-permute-start | bytes 589832 | tf_op jit(solution)/shard_map/ppermute | solution.py:285
  64.5 19.1 %all-to-all-start.1 = ((f32[32,3,4,128]{3,2,1,0:T(4,128)}), f32[32,3,4,128]{3,2,1,0:T(4,128)S(1)}, u32[]{:S(2)}, u32[]{:S(2)}) async-start(f32[32,3,4,128]{3,2,1,0:T(4,128)} %bitcast.3), calls=%async_computation.1 | async-start | bytes 393216 | tf_op jit(solution)/shard_map/all_to_all | solution.py:273
  72.6 2.0 %copy-start.3 = (f32[27,2,128,128]{3,2,1,0:T(8,128)S(1)}, f32[27,2,128,128]{3,2,1,0:T(8,128)}, u32[]{:S(2)}) copy-start(f32[27,2,128,128]{3,2,1,0:T(8,128)} %tiles_ref.1) | copy-start | bytes 10616836
  74.6 9.0 %copy-start.5 = (f32[2,1024,128]{2,1,0:T(8,128)S(1)}, f32[2,1024,128]{2,1,0:T(8,128)}, u32[]{:S(2)}) copy-start(f32[2,1024,128]{2,1,0:T(8,128)} %rad_ref.3) | copy-start | bytes 3145732
  74.6 9.0 %copy-start.7 = (f32[8,1024]{1,0:T(8,128)S(1)}, f32[8,1024]{1,0:T(8,128)}, u32[]{:S(2)}) copy-start(f32[8,1024]{1,0:T(8,128)} %phase_ref.3) | copy-start | bytes 98308
where the time goes:
time: 87.7 us; the launch traced here: 87.2 us
  starting transfers between devices  40.2 us (46%)
  Pallas kernels  22.4 us (26%)
  waiting for transfers between devices  17.5 us (20%)
  local copies, waits for them, and re-layouts  5.97 us (7%)
  other arithmetic  0.95 us (1%)
    all_to_all x2, starting transfers between devices, spread(): lax.all_to_all(block, AXES, split_axis=0, concat_axis=0, axis_index_group...  19.4 us
    all_to_all x2, waiting for transfers between devices, spread(): lax.all_to_all(block, AXES, split_axis=0, concat_axis=0, axis_index_group...  14.5 us
    ppermute x4, starting transfers between devices, moved_by(): return lax.ppermute(block, AXES, route_of(move))  11.8 us
    pallas_call x1, Pallas kernels, per_device(): call(translate_kernel, (f32(3, 96, 4, 128), f32(3, 96, 4, 128), f32(96, 4...  9.09 us
    ppermute x2, starting transfers between devices, along_slab(): lax.ppermute(block, 'slab', [(i, i + distance) for i in range(16) if 0 <=...  5.56 us
    unnamed x24, local copies, waits for them, and re-layouts  5.17 us
    pallas_call x1, Pallas kernels, per_device(): call(near_kernel, f32(192, 256), [pltpu.VMEM((4, 4, 48, 256), BF16), pltp...  5.11 us
    pallas_call x1, Pallas kernels, per_device(): call(aggregate_kernel, f32(32, 3, 4, 128), flops=600000000, moved=2000000)  4.41 us
  transfers between devices with their start and end apart: 10, of which 6 were waited for; matrix products, arithmetic and copies ran while one was open for 2% of the time, Pallas kernels for 6%

commit v1 on v0

--- a/solution.py
+++ b/solution.py
@@ -65,6 +65,16 @@
     return jnp.where(row == lane, x, moved)
 
 
+def radiation_copy(rad_hbm, rad_ref, sems, i):
+    block = pl.ds(pl.multiple_of(i * 256, 256), 256)
+    return pltpu.make_async_copy(rad_hbm.at[:, block], rad_ref.at[:, block], sems.at[i])
+
+
+def tiles_copy(tiles_hbm, tiles_ref, sems, i):
+    block = pl.ds(i * 9, 9)
+    return pltpu.make_async_copy(tiles_hbm.at[block], tiles_ref.at[block], sems.at[i])
+
+
 def radiation_block(rad_ref, start):
     re = rad_ref[0, pl.ds(start, 128), :]
     im = rad_ref[1, pl.ds(start, 128), :]
@@ -91,15 +101,22 @@
     return ((i * 2 + j) * 6 + parent * 2 + l) * 8
 
 
-def aggregate_kernel(cur_ref, rad_ref, phase_ref, out_ref):
+def aggregate_kernel(
+    core_ref, cur_ref, rad_hbm, phase_ref, out_ref, beside_ref, away_ref, rad_ref, sems,
+    unroll=4, groups=(4, 4),
+):
+    core = core_ref[0]
+    beside_ref[...] = cur_ref[pl.ds(pl.multiple_of((1 - core) * 192, 8), 192), :]
+    away_ref[...] = cur_ref[pl.ds(pl.multiple_of(core * 192, 8), 192), :]
+    for i in range(4):
+        radiation_copy(rad_hbm, rad_ref, sems, i).start()
     rows = cur_ref.shape[0] // 2
     x = jnp.concatenate(
         [cur_ref[pl.ds(0, rows, stride=2), :], cur_ref[pl.ds(1, rows, stride=2), :]], axis=1
     )
     x = split(x)
 
-    @pl.loop(0, 8)
-    def _(step):
+    def directions(step, carry):
         start = pl.multiple_of(step * 128, 128)
         leaf = dot3(x, radiation_block(rad_ref, start), NT)
         cos, sin = phase_block(phase_ref, start)
@@ -117,13 +134,20 @@
                 d = step * 2 + pair
                 out_ref[d, parent] = block[:4]
                 out_ref[16 + d, parent] = block[4:]
-
-
-def disaggregate_kernel(in_ref, rad_ref, phase_ref, near_ref, out_ref, acc_ref):
+        return carry
+
+    first = 0
+    for count in groups:
+        for i in range(first // 2, (first + count) // 2):
+            radiation_copy(rad_hbm, rad_ref, sems, i).wait()
+        lax.fori_loop(first, first + count, directions, 0, unroll=unroll)
+        first += count
+
+
+def disaggregate_kernel(in_ref, rad_ref, phase_ref, near_ref, out_ref, acc_ref, unroll=4):
     acc_ref[...] = near_ref[...]
 
-    @pl.loop(0, 8)
-    def _(step):
+    def directions(step, carry):
         start = pl.multiple_of(step * 128, 128)
         cos, sin = phase_block(phase_ref, start)
         parents = []
@@ -144,13 +168,23 @@
                 )
         children = split(jnp.concatenate(rows, axis=0))
         acc_ref[...] += dot3(children, radiation_block(rad_ref, start), NN)
-
+        return carry
+
+    lax.fori_loop(0, 8, directions, 0, unroll=unroll)
     rows = acc_ref.shape[0]
     out_ref[pl.ds(0, rows, stride=2), :] = acc_ref[:, :128]
     out_ref[pl.ds(1, rows, stride=2), :] = acc_ref[:, 128:]
 
 
-def near_kernel(own_ref, left_ref, right_ref, down_ref, up_ref, tiles_ref, out_ref, hi_ref, lo_ref, acc_ref):
+def near_kernel(
+    core_ref, own_ref, beside_ref, away_ref, down_ref, up_ref, tiles_hbm,
+    out_ref, tiles_ref, hi_ref, lo_ref, acc_ref, sems,
+):
+    for i in range(3):
+        tiles_copy(tiles_hbm, tiles_ref, sems, i).start()
+    to_beside = jnp.where(core_ref[0] == 0, 3, 0)
+    to_away = 3 - to_beside
+
     def put(ref, at_row, to_x, to_y):
         x = jnp.concatenate(
             [ref[pl.ds(at_row * 96, 48, stride=2), :], ref[pl.ds(at_row * 96 + 1, 48, stride=2), :]],
@@ -163,76 +197,97 @@
     for i in range(2):
         for j in range(2):
             put(own_ref, i * 2 + j, 1 + i, 1 + j)
-        put(left_ref, i, 0, 1 + i)
-        put(right_ref, i, 3, 1 + i)
-    for i in range(4):
-        put(down_ref, i, i, 0)
-        put(up_ref, i, i, 3)
+        put(beside_ref, i, to_beside, 1 + i)
+        put(away_ref, i, to_away, 1 + i)
+    for i, to_x in enumerate((1, 2, to_beside, to_away)):
+        put(down_ref, i, to_x, 0)
+        put(up_ref, i, to_x, 3)
     acc_ref[...] = jnp.zeros_like(acc_ref)
 
-    @pl.loop(0, 9)
-    def _(step):
-        dx = step // 3
-        dy = step - dx * 3
-        hi = hi_ref[pl.ds(dx, 2), pl.ds(dy, 2)].reshape(192, 256)
-        lo = lo_ref[pl.ds(dx, 2), pl.ds(dy, 2)].reshape(192, 256)
-        for dz in range(3):
-            re = tiles_ref[step * 3 + dz, 0]
-            im = tiles_ref[step * 3 + dz, 1]
-            matrix = jnp.concatenate(
-                [jnp.concatenate([re, -im], axis=1), jnp.concatenate([im, re], axis=1)], axis=0
-            )
-            y = dot3((hi, lo), split(matrix), NT).reshape(4, 48, 256)
-            if dz == 0:
-                acc_ref[:, 8:48] += y[:, 0:40]
-            elif dz == 1:
-                acc_ref[...] += y
-            else:
-                acc_ref[:, 0:40] += y[:, 8:48]
+    @pl.loop(0, 3)
+    def _(dx):
+        tiles_copy(tiles_hbm, tiles_ref, sems, dx).wait()
+        for dy in range(3):
+            hi = hi_ref[pl.ds(dx, 2), dy : dy + 2].reshape(192, 256)
+            lo = lo_ref[pl.ds(dx, 2), dy : dy + 2].reshape(192, 256)
+            for dz in range(3):
+                re = tiles_ref[dx * 9 + dy * 3 + dz, 0]
+                im = tiles_ref[dx * 9 + dy * 3 + dz, 1]
+                matrix = jnp.concatenate(
+                    [jnp.concatenate([re, -im], axis=1), jnp.concatenate([im, re], axis=1)], axis=0
+                )
+                y = dot3((hi, lo), split(matrix), NT).reshape(4, 48, 256)
+                if dz == 0:
+                    acc_ref[:, 8:48] += y[:, 0:40]
+                elif dz == 1:
+                    acc_ref[...] += y
+                else:
+                    acc_ref[:, 0:40] += y[:, 8:48]
 
     out_ref[...] = acc_ref[...].reshape(192, 256)
 
 
-def translate_kernel(words_ref, table_ref, src_ref, keep_ref, swap_ref, far_ref, acc_ref):
+def translate_kernel(
+    slots_ref, kinds_ref, table_ref, src_ref, beside_ref, away_ref,
+    keep_ref, swap_ref, far_ref, acc_ref,
+):
     acc_ref[...] = jnp.zeros_like(acc_ref)
     row = lax.broadcasted_iota(jnp.int32, (8, 128), 0)
 
-    @pl.loop(0, 96)
-    def _(s):
+    def tile(first):
+        return pl.ds(pl.multiple_of(first, 8), 8)
+
+    def source(s, carry):
         part = src_ref[s]
         both = jnp.concatenate([part, part], axis=0)
         both = jnp.where(row < 4, both, times_i(both))
         slots, sums = [], []
         for f in range(16):
-            word = words_ref[s * 16 + f]
-            slot = word >> 9
-            kind = word & 511
+            slot = slots_ref[s * 16 + f]
             slots.append(slot)
-            sums.append(acc_ref[slot] + table_ref[kind] * both)
+            kind = kinds_ref[s * 16 + f]
+            sums.append(acc_ref[tile(slot), :] + table_ref[tile(kind), :] * both)
         for f in range(16):
-            acc_ref[slots[f]] = sums[f]
-
-    for ref, base in ((keep_ref, 0), (swap_ref, 288)):
-        for block in range(3):
-            part = acc_ref[pl.ds(base + block * 96, 96)]
-            ref[block] = part[:, :4] + part[:, 4:]
-    part = acc_ref[pl.ds(576, 96)]
-    far_ref[...] = part[:, :4] + part[:, 4:]
-
-
-def fold_kernel(keep_ref, got_ref, back_ref, mid_ref, ahead_ref):
+            acc_ref[tile(slots[f]), :] = sums[f]
+        return carry
+
+    lax.fori_loop(0, 96, source, 0, unroll=4)
+
+    def folded(block):
+        part = acc_ref[pl.ds(block * 768, 768), :].reshape(96, 8, 128)
+        return part[:, :4] + part[:, 4:]
+
+    for block in range(3):
+        keep_ref[block] = folded(block)
+        swap_ref[block] = folded(block + 3)
+    far_ref[...] = folded(6)
+
+
+def fold_kernel(
+    keep_ref, got_ref, cur_ref, beside_ref, away_ref,
+    back_ref, mid_ref, ahead_ref, down_ref, up_ref,
+):
     back_ref[...] = keep_ref[0] + got_ref[0]
     mid_ref[...] = keep_ref[1] + got_ref[1]
     ahead_ref[...] = keep_ref[2] + got_ref[2]
-
-
-def call(kernel, out_shape, scratch=(), in_specs=None, flops=0, moved=0):
+    for ref, j in ((down_ref, 1), (up_ref, 0)):
+        for i in range(2):
+            ref[pl.ds(i * 96, 96), :] = cur_ref[pl.ds(i * 192 + j * 96, 96), :]
+        ref[pl.ds(192, 96), :] = beside_ref[pl.ds(j * 96, 96), :]
+        ref[pl.ds(288, 96), :] = away_ref[pl.ds(j * 96, 96), :]
+
+
+def join_kernel(mid_ref, far_ref, back_ref, ahead_ref, down_ref, up_ref, out_ref):
+    out_ref[...] = (mid_ref[...] + far_ref[...]) + (back_ref[...] + ahead_ref[...])
+
+
+def call(kernel, out_shape, scratch=(), in_specs=None, flops=0, moved=0, vmem_bytes=VMEM_BYTES):
     extra = {} if in_specs is None else {"in_specs": in_specs}
     return pl.pallas_call(
         kernel,
         out_shape=out_shape,
         scratch_shapes=list(scratch),
-        compiler_params=pltpu.CompilerParams(vmem_limit_bytes=VMEM_BYTES),
+        compiler_params=pltpu.CompilerParams(vmem_limit_bytes=vmem_bytes),
         cost_estimate=pl.CostEstimate(flops=flops, bytes_accessed=moved, transcendentals=0),
         **extra,
     )
@@ -254,7 +309,7 @@
     near_block = (step + 1) % 4 + jnp.where(to_ring % 2 == core, 0, 3)
     block = jnp.where(step == 2, 6, near_block)
     slot = block * 96 + half * 48 + row
-    return (slot * 512 + kinds).reshape(-1)
+    return (slot * 8).reshape(-1), (kinds * 8).reshape(-1)
 
 
 def operator_table(translators):
@@ -262,7 +317,7 @@
     half = lax.axis_index("slab") // 8
     own = lax.dynamic_slice_in_dim(translators, half * 32, 32, 2)
     lanes = jnp.concatenate([own] * 4, axis=2)
-    return jnp.broadcast_to(lanes[:, :, None, :], (count, 2, 4, 128)).reshape(count, 8, 128)
+    return jnp.broadcast_to(lanes[:, :, None, :], (count, 2, 4, 128)).reshape(count * 8, 128)
 
 
 def moved_by(block, move):
@@ -275,70 +330,75 @@
     )
 
 
-def halo(currents):
-    def along_slab(block, distance):
-        return lax.ppermute(
-            block, "slab", [(i, i + distance) for i in range(16) if 0 <= i + distance < 16]
-        )
-
-    def along_dir(block, distance):
-        return lax.ppermute(
-            block, "dir", [(i, i + distance) for i in range(16) if 0 <= i + distance < 16]
-        )
-
-    left = along_slab(currents[1:2], 1)
-    right = along_slab(currents[0:1], -1)
-    tall = jnp.concatenate([left, currents, right], axis=0)
-    down = along_dir(tall[:, 1:2], 1)
-    up = along_dir(tall[:, 0:1], -1)
-    return left, right, down, up
-
-
 def per_device(currents, near_tiles, radiation, child_phase, translators, far_targets, far_offsets):
     groups = exchange_groups()
     rows = currents.reshape(384, 128)
-    words = pair_words(far_targets, far_offsets)
+    core = (lax.axis_index("slab") % 2).astype(jnp.int32).reshape(1)
+    slots, kinds = pair_words(far_targets, far_offsets)
     table = operator_table(translators)
-
-    patterns = call(
-        aggregate_kernel, f32(32, 3, 4, 128), flops=600_000_000, moved=2_000_000
-    )(rows, radiation, child_phase)
+    vmem = pl.BlockSpec(memory_space=pltpu.VMEM)
+    smem = pl.BlockSpec(memory_space=pltpu.SMEM)
+    hbm = pl.BlockSpec(memory_space=pl.ANY)
+
+    patterns, beside, away = call(
+        aggregate_kernel,
+        (f32(32, 3, 4, 128), f32(192, 128), f32(192, 128)),
+        [pltpu.VMEM((2, 1024, 128), F32), pltpu.SemaphoreType.DMA((4,))],
+        in_specs=[smem, vmem, hbm, vmem],
+        flops=600_000_000,
+        moved=2_000_000,
+        vmem_bytes=62 * 1024 * 1024,
+    )(core, rows, radiation, child_phase)
     moved = spread(patterns, groups)
-
-    left, right, down, up = halo(currents)
+    beside = moved_by(beside, lambda z_hi, y, core, d: (z_hi, y, 1 - core, d))
+    away = lax.ppermute(
+        away, "slab", [(s, s + 2 * (s % 2) - 1) for s in range(16) if 0 <= s + 2 * (s % 2) - 1 < 16]
+    )
+
+    keep, swap, far = call(
+        translate_kernel,
+        (f32(3, 96, 4, 128), f32(3, 96, 4, 128), f32(96, 4, 128)),
+        [pltpu.VMEM((5376, 128), F32)],
+        in_specs=[smem, smem, vmem, vmem, hbm, hbm],
+        flops=100_000_000,
+        moved=3_000_000,
+    )(slots, kinds, table, moved.reshape(96, 4, 128), beside, away)
+    far_in = moved_by(far, lambda z_hi, y, core, d: (z_hi, (y + 2) % 4, 1 - core, d))
+    swap_in = moved_by(swap, lambda z_hi, y, core, d: (z_hi, y, 1 - core, d))
+    back, mid, ahead, down, up = call(
+        fold_kernel,
+        (f32(96, 4, 128),) * 3 + (f32(384, 128),) * 2,
+        flops=1_000_000,
+        moved=2_000_000,
+    )(keep, swap_in, rows, beside, away)
+    back_in = moved_by(back, lambda z_hi, y, core, d: (z_hi, (y + 3) % 4, core, d))
+    ahead_in = moved_by(ahead, lambda z_hi, y, core, d: (z_hi, (y + 1) % 4, core, d))
+    down = lax.ppermute(down, "dir", [(d, d + 1) for d in range(15)])
+    up = lax.ppermute(up, "dir", [(d + 1, d) for d in range(15)])
+    incoming = call(
+        join_kernel,
+        f32(96, 4, 128),
+        in_specs=[vmem] * 4 + [hbm] * 2,
+        flops=1_000_000,
+        moved=1_000_000,
+    )(mid, far_in, back_in, ahead_in, down, up)
+    returned = spread(incoming.reshape(32, 3, 4, 128), groups)
+
     near = call(
         near_kernel,
         f32(192, 256),
-        [pltpu.VMEM((4, 4, 48, 256), BF16), pltpu.VMEM((4, 4, 48, 256), BF16), pltpu.VMEM((4, 48, 256), F32)],
+        [
+            pltpu.VMEM((27, 2, 128, 128), F32),
+            pltpu.VMEM((4, 4, 48, 256), BF16),
+            pltpu.VMEM((4, 4, 48, 256), BF16),
+            pltpu.VMEM((4, 48, 256), F32),
+            pltpu.SemaphoreType.DMA((3,)),
+        ],
+        in_specs=[smem] + [vmem] * 5 + [hbm],
         flops=2_000_000_000,
         moved=5_000_000,
-    )(
-        rows,
-        left.reshape(192, 128),
-        right.reshape(192, 128),
-        down.reshape(384, 128),
-        up.reshape(384, 128),
-        near_tiles,
-    )
-
-    vmem = pl.BlockSpec(memory_space=pltpu.VMEM)
-    keep, swap, far = call(
-        translate_kernel,
-        (f32(3, 96, 4, 128), f32(3, 96, 4, 128), f32(96, 4, 128)),
-        [pltpu.VMEM((672, 8, 128), F32)],
-        in_specs=[pl.BlockSpec(memory_space=pltpu.SMEM), vmem, vmem],
-        flops=100_000_000,
-        moved=3_000_000,
-    )(words, table, moved.reshape(96, 4, 128))
-    far_in = moved_by(far, lambda z_hi, y, core, d: (z_hi, (y + 2) % 4, 1 - core, d))
-    swap_in = moved_by(swap, lambda z_hi, y, core, d: (z_hi, y, 1 - core, d))
-    back, mid, ahead = call(
-        fold_kernel, (f32(96, 4, 128), f32(96, 4, 128), f32(96, 4, 128)), flops=1_000_000, moved=2_000_000
-    )(keep, swap_in)
-    back_in = moved_by(back, lambda z_hi, y, core, d: (z_hi, (y + 3) % 4, core, d))
-    ahead_in = moved_by(ahead, lambda z_hi, y, core, d: (z_hi, (y + 1) % 4, core, d))
-    incoming = (mid + far_in) + (back_in + ahead_in)
-    returned = spread(incoming.reshape(32, 3, 4, 128), groups)
+        vmem_bytes=50 * 1024 * 1024,
+    )(core, rows, beside, away, down, up, near_tiles)
 
     applied = call(
         disaggregate_kernel,

time: 87.7 us -> 74.7 us (0.85)
  starting transfers between devices: 40.2 us -> 33.6 us
  Pallas kernels: 22.4 us -> 18.1 us
  local copies, waits for them, and re-layouts: 5.97 us -> 2.62 us
  waiting for transfers between devices: 17.5 us -> 19.3 us
    ppermute x4 -> x5, starting transfers between devices: 11.8 us -> 5.41 us  [moved_by(): return lax.ppermute(block, AXES, route_of(move))]
    unnamed x24 -> x10, local copies, waits for them, and re-layouts: 5.17 us -> 0.19 us
    pallas_call x1, Pallas kernels: 9.09 us -> 5.62 us  [per_device(): call(translate_kernel, (f32(3, 96, 4, 128), f32(3, 96, 4, 128), f32(96, 4...]
    all_to_all x2, waiting for transfers between devices: 14.5 us -> 11.3 us  [spread(): lax.all_to_all(block, AXES, split_axis=0, concat_axis=0, axis_index_group...]
    ppermute x4 -> x3, waiting for transfers between devices: 2.15 us -> 5.24 us  [the longest x1 4.12 us: per_device(): up = lax.ppermute(up, 'dir', [(d + 1, d) for d in range(15)])]
    ppermute x4 -> x5, waiting for transfers between devices: 0.85 us -> 2.71 us  [moved_by(): return lax.ppermute(block, AXES, route_of(move))]
    pallas_call x1, Pallas kernels: 3.6 us -> 1.9 us  [per_device(): call(disaggregate_kernel, f32(384, 128), [pltpu.VMEM((192, 256), F32)], f...]
    ppermute x4 -> x3, starting transfers between devices: 9.01 us -> 7.45 us  [the longest x1 3.71 us: per_device(): down = lax.ppermute(down, 'dir', [(d, d + 1) for d in range(15)])]
  transfers between devices with their start and end apart: 10 -> 10, of which waited for: 6 -> 7; matrix products, arithmetic and copies ran while one was open for 2% -> 4% of each run, Pallas kernels for 6% -> 7%
where the time goes in v1:
time: 74.7 us; the launch traced here: 74.1 us
  starting transfers between devices  33.6 us (45%)
  waiting for transfers between devices  19.3 us (26%)
  Pallas kernels  18.1 us (24%)
  local copies, waits for them, and re-layouts  2.62 us (4%)
    all_to_all x2, starting transfers between devices, spread(): lax.all_to_all(block, AXES, split_axis=0, concat_axis=0, axis_index_group...  20.7 us
    all_to_all x2, waiting for transfers between devices, spread(): lax.all_to_all(block, AXES, split_axis=0, concat_axis=0, axis_index_group...  11.3 us
    pallas_call x1, Pallas kernels, per_device(): call(translate_kernel, (f32(3, 96, 4, 128), f32(3, 96, 4, 128), f32(96, 4...  5.62 us
    ppermute x5, starting transfers between devices, moved_by(): return lax.ppermute(block, AXES, route_of(move))  5.41 us
    pallas_call x1, Pallas kernels, per_device(): call(near_kernel, f32(192, 256), [pltpu.VMEM((27, 2, 128, 128), F32), plt...  5.31 us
    pallas_call x1, Pallas kernels, per_device(): call(aggregate_kernel, (f32(32, 3, 4, 128), f32(192, 128), f32(192, 128))...  4.38 us
    ppermute x1, waiting for transfers between devices, per_device(): up = lax.ppermute(up, 'dir', [(d + 1, d) for d in range(15)])  4.12 us
    ppermute x1, starting transfers between devices, per_device(): down = lax.ppermute(down, 'dir', [(d, d + 1) for d in range(15)])  3.71 us
  transfers between devices with their start and end apart: 10, of which 7 were waited for; matrix products, arithmetic and copies ran while one was open for 4% of the time, Pallas kernels for 7%

profile of v1, /device:TPU:8, one launch (start us, length us, event | category | flops | bytes accessed | tf_op | source)
XLA Modules:
  0.0 74.1 jit_solution(16268916843691246518)
XLA Ops:
  0.0 0.0 copy-start
  0.0 4.4 %shard_map.73 = (f32[32,3,4,128]{3,2,1,0:T(4,128)}, f32[192,128]{1,0:T(8,128)}, f32[192,128]{1,0:T(8,128)}) custom-call(s32[1]{0:T(128)} %bitcast.1.core_ref, f32[384,128]{1,0:T(8,128)} %bitcast.20, f32[2,1024,128]{2,1,0:T(8,128)} %rad_ref.1, f32[8,1024]{1,0:T(8,128)} %phase_ref.3), custom_call_target="tpu_custom_call" | custom-call | flops 600000000 | bytes 2000000 | tf_op jit(solution)/shard_map/pallas_call | solution.py:343
  4.4 0.0 copy-start.1
  4.4 11.5 %all-to-all-start = ((f32[32,3,4,128]{3,2,1,0:T(4,128)}), f32[32,3,4,128]{3,2,1,0:T(4,128)S(1)}, u32[]{:S(2)}, u32[]{:S(2)}) async-start(f32[32,3,4,128]{3,2,1,0:T(4,128)} %get-tuple-element.16), calls=%async_computation | async-start | bytes 393216 | tf_op jit(solution)/shard_map/all_to_all | solution.py:328
  15.9 0.1 collective-permute-start
  16.0 2.4 %collective-permute-start.1 = (f32[192,128]{1,0:T(8,128)}, f32[192,128]{1,0:T(8,128)S(1)}, u32[]{:S(2)}, u32[]{:S(2)}) collective-permute-start(f32[192,128]{1,0:T(8,128)} %get-tuple-element.18), channel_id=1, source_target_pairs={{16,32},{32,16},{48,64},{64,48},{80,96},{96,80},{112,128},{128,112... | collective-permute-start | bytes 294920 | tf_op jit(solution)/shard_map/ppermute | solution.py:354
  18.5 0.9 %reshape.31 = s32[2,8,48,16]{2,1,0,3:T(8,128)S(1)} reshape(s32[768,16]{0,1:T(8,128)} %param.12) | data formatting | bytes 98304 | tf_op jit(solution)/shard_map/reshape | solution.py:304
  19.4 0.9 %reshape.33 = s32[2,8,48,16]{2,1,0,3:T(8,128)S(1)} reshape(s32[768,16]{0,1:T(8,128)} %param.13) | data formatting | bytes 98304 | tf_op jit(solution)/shard_map/reshape | solution.py:305
  20.3 0.1 copy.13
  20.4 0.1 reshape.34.kinds_ref
  20.5 0.1 copy.12
  20.6 0.2 fusion.9
  20.8 0.1 reshape.32.slots_ref
  20.9 0.0 copy-done
  20.9 0.2 copy.11
  21.1 0.0 collective-permute-done.beside_ref
  21.2 1.0 %collective-permute-done.1.away_ref = f32[192,128]{1,0:T(8,128)S(1)} collective-permute-done((f32[192,128]{1,0:T(8,128)}, f32[192,128]{1,0:T(8,128)S(1)}, u32[]{:S(2)}, u32[]{:S(2)}) %collective-permute-start.1) | collective-permute-done | bytes 98336 | tf_op jit(solution)/shard_map/ppermute | solution.py:354
  22.1 5.5 %all-to-all-done = f32[32,3,4,128]{3,2,1,0:T(4,128)S(1)} async-done(((f32[32,3,4,128]{3,2,1,0:T(4,128)}), f32[32,3,4,128]{3,2,1,0:T(4,128)S(1)}, u32[]{:S(2)}, u32[]{:S(2)}) %all-to-all-start) | async-done | bytes 196640 | tf_op jit(solution)/shard_map/all_to_all | solution.py:328
  27.6 0.2 broadcast_in_dim.15
  27.8 5.6 %shard_map.74 = (f32[3,96,4,128]{3,2,1,0:T(4,128)S(1)}, f32[3,96,4,128]{3,2,1,0:T(4,128)S(1)}, f32[96,4,128]{2,1,0:T(4,128)S(1)}) custom-call(s32[1536]{0:T(1024)S(1)} %reshape.32.slots_ref, s32[1536]{0:T(1024)S(1)} %reshape.34.kinds_ref, f32[2528,128]{1,0:T(8,128)S(1)} %bitcast.18, f32[96,4,128]{2,1,0:T(4,128)S(1)} %bitcast.19, ...), custom_call_target="tpu_custom_call" | custom-call | flops 100000000 | bytes 3000000 | tf_op jit(solution)/shard_map/pallas_call | solution.py:358
  33.4 0.1 collective-permute-start.2
  33.5 3.1 %collective-permute-start.3 = (f32[96,4,128]{2,1,0:T(4,128)S(1)}, f32[96,4,128]{2,1,0:T(4,128)S(1)}, u32[]{:S(2)}, u32[]{:S(2)}) collective-permute-start(f32[96,4,128]{2,1,0:T(4,128)S(1)} %get-tuple-element.22), channel_id=1, source_target_pairs={{0,80},{1,81},{2,82},{3,83},{4,84},{5,85},{6,86},{7,87},{8,88},{9,... | collective-permute-start | bytes 589832 | tf_op jit(solution)/shard_map/ppermute | solution.py:324
  36.6 0.0 collective-permute-done.2.got_ref
  36.6 0.0 copy-done.1
  36.6 0.2 shard_map.75
  36.8 0.7 collective-permute-start.4
  37.6 1.4 %collective-permute-start.5 = (f32[96,4,128]{2,1,0:T(4,128)S(1)}, f32[96,4,128]{2,1,0:T(4,128)S(1)}, u32[]{:S(2)}, u32[]{:S(2)}) collective-permute-start(f32[96,4,128]{2,1,0:T(4,128)S(1)} %get-tuple-element.24), channel_id=1, source_target_pairs={{0,32},{1,33},{2,34},{3,35},{4,36},{5,37},{6,38},{7,39},{8,40},{9,... | collective-permute-start | bytes 589832 | tf_op jit(solution)/shard_map/ppermute | solution.py:324
  38.9 3.7 %collective-permute-start.6 = (f32[384,128]{1,0:T(8,128)S(1)}, f32[384,128]{1,0:T(8,128)S(1)}, u32[]{:S(2)}, u32[]{:S(2)}) collective-permute-start(f32[384,128]{1,0:T(8,128)S(1)} %get-tuple-element.25), channel_id=1, source_target_pairs={{0,1},{1,2},{2,3},{3,4},{4,5},{5,6},{6,7},{7,8},{8,9},{9,10},{10,1... | collective-permute-start | bytes 589832 | tf_op jit(solution)/shard_map/ppermute | solution.py:376
  42.7 1.3 %collective-permute-start.7 = (f32[384,128]{1,0:T(8,128)S(1)}, f32[384,128]{1,0:T(8,128)S(1)}, u32[]{:S(2)}, u32[]{:S(2)}) collective-permute-start(f32[384,128]{1,0:T(8,128)S(1)} %get-tuple-element.26), channel_id=1, source_target_pairs={{1,0},{2,1},{3,2},{4,3},{5,4},{6,5},{7,6},{8,7},{9,8},{10,9},{11,1... | collective-permute-start | bytes 589832 | tf_op jit(solution)/shard_map/ppermute | solution.py:377
  44.0 0.0 collective-permute-done.3.far_ref
  44.0 2.6 %collective-permute-done.4.back_ref = f32[96,4,128]{2,1,0:T(4,128)S(1)} collective-permute-done((f32[96,4,128]{2,1,0:T(4,128)S(1)}, f32[96,4,128]{2,1,0:T(4,128)S(1)}, u32[]{:S(2)}, u32[]{:S(2)}) %collective-permute-start.4) | collective-permute-done | bytes 196640 | tf_op jit(solution)/shard_map/ppermute | solution.py:324
  46.5 0.1 collective-permute-done.5.ahead_ref
  46.7 0.2 collective-permute-done.6.down_ref
  46.8 4.1 %collective-permute-done.7.up_ref = f32[384,128]{1,0:T(8,128)S(1)} collective-permute-done((f32[384,128]{1,0:T(8,128)S(1)}, f32[384,128]{1,0:T(8,128)S(1)}, u32[]{:S(2)}, u32[]{:S(2)}) %collective-permute-start.7) | collective-permute-done | bytes 196640 | tf_op jit(solution)/shard_map/ppermute | solution.py:377
  50.9 0.8 %shard_map.76 = f32[96,4,128]{2,1,0:T(4,128)} custom-call(f32[96,4,128]{2,1,0:T(4,128)S(1)} %get-tuple-element.21.mid_ref, f32[96,4,128]{2,1,0:T(4,128)S(1)} %collective-permute-done.3.far_ref, f32[96,4,128]{2,1,0:T(4,128)S(1)} %collective-permute-done.4.back_ref, f32[96,4,128]{2,1,0:T(4,128)S(1)} %collective-permute-done.5.ahead_ref, ...), custom_call_target="tpu_custom_call" | custom-call | flops 1000000 | bytes 1000000 | tf_op jit(solution)/shard_map/pallas_call | solution.py:378
  51.7 9.2 %all-to-all-start.1 = ((f32[32,3,4,128]{3,2,1,0:T(4,128)}), f32[32,3,4,128]{3,2,1,0:T(4,128)S(1)}, u32[]{:S(2)}, u32[]{:S(2)}) async-start(f32[32,3,4,128]{3,2,1,0:T(4,128)} %bitcast.4), calls=%async_computation.1 | async-start | bytes 393216 | tf_op jit(solution)/shard_map/all_to_all | solution.py:328
  61.0 0.0 copy-start.2
  61.0 0.0 copy-start.3
  61.0 5.3 %shard_map.77.near_ref = f32[192,256]{1,0:T(8,128)S(1)} custom-call(s32[1]{0:T(128)} %bitcast.1.core_ref, f32[384,128]{1,0:T(8,128)S(1)} %bitcast.22, f32[192,128]{1,0:T(8,128)S(1)} %collective-permute-done.beside_ref, f32[192,128]{1,0:T(8,128)S(1)} %collective-permute-done.1.away_ref, f32[384,128]{1,0:T(8,128)S(1)} %collective-permute-done.6.down_ref, ...), custom_call_target="tpu_custom_call" | custom-call | flops 2000000000 | bytes 5000000 | tf_op jit(solution)/shard_map/pallas_call | solution.py:387
  66.3 5.9 %all-to-all-done.1.in_ref = f32[32,3,4,128]{3,2,1,0:T(4,128)S(1)} async-done(((f32[32,3,4,128]{3,2,1,0:T(4,128)}), f32[32,3,4,128]{3,2,1,0:T(4,128)S(1)}, u32[]{:S(2)}, u32[]{:S(2)}) %all-to-all-start.1) | async-done | bytes 196640 | tf_op jit(solution)/shard_map/all_to_all | solution.py:328
  72.2 0.0 copy-done.2
  72.2 0.0 copy-done.3
  72.2 1.9 %shard_map.78 = f32[384,128]{1,0:T(8,128)} custom-call(f32[32,3,4,128]{3,2,1,0:T(4,128)S(1)} %all-to-all-done.1.in_ref, f32[2,1024,128]{2,1,0:T(8,128)S(1)} %copy-done.2, f32[8,1024]{1,0:T(8,128)S(1)} %copy-done.3, f32[192,256]{1,0:T(8,128)S(1)} %shard_map.77.near_ref), custom_call_target="tpu_custom_call" | custom-call | flops 600000000 | bytes 2000000 | tf_op jit(solution)/shard_map/pallas_call | solution.py:403
  (4 shorter events, 0.1 us)
Async XLA Ops:
  0.0 20.9 %copy-start = (f32[316,2,64]{0,2,1:T(8,128)S(1)}, f32[316,2,64]{0,2,1:T(8,128)}, u32[]{:S(2)}) copy-start(f32[316,2,64]{0,2,1:T(8,128)} %param.11) | copy-start | bytes 485380
  4.4 32.3 %copy-start.1 = (f32[2,2,6,8,2,128]{5,4,3,2,1,0:T(2,128)S(1)}, f32[2,2,6,8,2,128]{5,4,3,2,1,0:T(2,128)}, u32[]{:S(2)}) copy-start(f32[2,2,6,8,2,128]{5,4,3,2,1,0:T(2,128)} %param.7) | copy-start | bytes 589828
  4.4 23.2 %all-to-all-start = ((f32[32,3,4,128]{3,2,1,0:T(4,128)}), f32[32,3,4,128]{3,2,1,0:T(4,128)S(1)}, u32[]{:S(2)}, u32[]{:S(2)}) async-start(f32[32,3,4,128]{3,2,1,0:T(4,128)} %get-tuple-element.16), calls=%async_computation | async-start | bytes 393216 | tf_op jit(solution)/shard_map/all_to_all | solution.py:328
  15.9 5.3 %collective-permute-start = (f32[192,128]{1,0:T(8,128)}, f32[192,128]{1,0:T(8,128)S(1)}, u32[]{:S(2)}, u32[]{:S(2)}) collective-permute-start(f32[192,128]{1,0:T(8,128)} %get-tuple-element.17), channel_id=1, source_target_pairs={{0,16},{1,17},{2,18},{3,19},{4,20},{5,21},{6,22},{7,23},{8,24},{9,... | collective-permute-start | bytes 294920 | tf_op jit(solution)/shard_map/ppermute | solution.py:324
  16.0 6.1 %collective-permute-start.1 = (f32[192,128]{1,0:T(8,128)}, f32[192,128]{1,0:T(8,128)S(1)}, u32[]{:S(2)}, u32[]{:S(2)}) collective-permute-start(f32[192,128]{1,0:T(8,128)} %get-tuple-element.18), channel_id=1, source_target_pairs={{16,32},{32,16},{48,64},{64,48},{80,96},{96,80},{112,128},{128,112... | collective-permute-start | bytes 294920 | tf_op jit(solution)/shard_map/ppermute | solution.py:354
  33.4 3.2 %collective-permute-start.2 = (f32[3,96,4,128]{3,2,1,0:T(4,128)S(1)}, f32[3,96,4,128]{3,2,1,0:T(4,128)S(1)}, u32[]{:S(2)}, u32[]{:S(2)}) collective-permute-start(f32[3,96,4,128]{3,2,1,0:T(4,128)S(1)} %get-tuple-element.20), channel_id=1, source_target_pairs={{0,16},{1,17},{2,18},{3,19},{4,20},{5,21},{6,22},{7,23},{8,24},{9,... | collective-permute-start | bytes 1769480 | tf_op jit(solution)/shard_map/ppermute | solution.py:324
  33.5 10.4 %collective-permute-start.3 = (f32[96,4,128]{2,1,0:T(4,128)S(1)}, f32[96,4,128]{2,1,0:T(4,128)S(1)}, u32[]{:S(2)}, u32[]{:S(2)}) collective-permute-start(f32[96,4,128]{2,1,0:T(4,128)S(1)} %get-tuple-element.22), channel_id=1, source_target_pairs={{0,80},{1,81},{2,82},{3,83},{4,84},{5,85},{6,86},{7,87},{8,88},{9,... | collective-permute-start | bytes 589832 | tf_op jit(solution)/shard_map/ppermute | solution.py:324
  36.8 9.7 %collective-permute-start.4 = (f32[96,4,128]{2,1,0:T(4,128)S(1)}, f32[96,4,128]{2,1,0:T(4,128)S(1)}, u32[]{:S(2)}, u32[]{:S(2)}) collective-permute-start(f32[96,4,128]{2,1,0:T(4,128)S(1)} %get-tuple-element.23), channel_id=1, source_target_pairs={{0,96},{1,97},{2,98},{3,99},{4,100},{5,101},{6,102},{7,103},{8,104... | collective-permute-start | bytes 589832 | tf_op jit(solution)/shard_map/ppermute | solution.py:324
  37.6 9.1 %collective-permute-start.5 = (f32[96,4,128]{2,1,0:T(4,128)S(1)}, f32[96,4,128]{2,1,0:T(4,128)S(1)}, u32[]{:S(2)}, u32[]{:S(2)}) collective-permute-start(f32[96,4,128]{2,1,0:T(4,128)S(1)} %get-tuple-element.24), channel_id=1, source_target_pairs={{0,32},{1,33},{2,34},{3,35},{4,36},{5,37},{6,38},{7,39},{8,40},{9,... | collective-permute-start | bytes 589832 | tf_op jit(solution)/shard_map/ppermute | solution.py:324
  38.9 7.9 %collective-permute-start.6 = (f32[384,128]{1,0:T(8,128)S(1)}, f32[384,128]{1,0:T(8,128)S(1)}, u32[]{:S(2)}, u32[]{:S(2)}) collective-permute-start(f32[384,128]{1,0:T(8,128)S(1)} %get-tuple-element.25), channel_id=1, source_target_pairs={{0,1},{1,2},{2,3},{3,4},{4,5},{5,6},{6,7},{7,8},{8,9},{9,10},{10,1... | collective-permute-start | bytes 589832 | tf_op jit(solution)/shard_map/ppermute | solution.py:376
  42.7 8.3 %collective-permute-start.7 = (f32[384,128]{1,0:T(8,128)S(1)}, f32[384,128]{1,0:T(8,128)S(1)}, u32[]{:S(2)}, u32[]{:S(2)}) collective-permute-start(f32[384,128]{1,0:T(8,128)S(1)} %get-tuple-element.26), channel_id=1, source_target_pairs={{1,0},{2,1},{3,2},{4,3},{5,4},{6,5},{7,6},{8,7},{9,8},{10,9},{11,1... | collective-permute-start | bytes 589832 | tf_op jit(solution)/shard_map/ppermute | solution.py:377
  51.7 20.5 %all-to-all-start.1 = ((f32[32,3,4,128]{3,2,1,0:T(4,128)}), f32[32,3,4,128]{3,2,1,0:T(4,128)S(1)}, u32[]{:S(2)}, u32[]{:S(2)}) async-start(f32[32,3,4,128]{3,2,1,0:T(4,128)} %bitcast.4), calls=%async_computation.1 | async-start | bytes 393216 | tf_op jit(solution)/shard_map/all_to_all | solution.py:328
  61.0 11.2 %copy-start.2 = (f32[2,1024,128]{2,1,0:T(8,128)S(1)}, f32[2,1024,128]{2,1,0:T(8,128)}, u32[]{:S(2)}) copy-start(f32[2,1024,128]{2,1,0:T(8,128)} %rad_ref.1) | copy-start | bytes 3145732
  61.0 11.2 %copy-start.3 = (f32[8,1024]{1,0:T(8,128)S(1)}, f32[8,1024]{1,0:T(8,128)}, u32[]{:S(2)}) copy-start(f32[8,1024]{1,0:T(8,128)} %phase_ref.3) | copy-start | bytes 98308

commit v2 on v1

--- a/solution.py
+++ b/solution.py
@@ -102,14 +102,13 @@
 
 
 def aggregate_kernel(
-    core_ref, cur_ref, rad_hbm, phase_ref, out_ref, beside_ref, away_ref, rad_ref, sems,
-    unroll=4, groups=(4, 4),
+    cur_ref, rad_hbm, phase_ref, out_ref, down_ref, up_ref, rad_ref, sems, unroll=4, groups=(4, 4)
 ):
-    core = core_ref[0]
-    beside_ref[...] = cur_ref[pl.ds(pl.multiple_of((1 - core) * 192, 8), 192), :]
-    away_ref[...] = cur_ref[pl.ds(pl.multiple_of(core * 192, 8), 192), :]
     for i in range(4):
         radiation_copy(rad_hbm, rad_ref, sems, i).start()
+    for i in range(2):
+        down_ref[pl.ds(i * 96, 96), :] = cur_ref[pl.ds(i * 192 + 96, 96), :]
+        up_ref[pl.ds(i * 96, 96), :] = cur_ref[pl.ds(i * 192, 96), :]
     rows = cur_ref.shape[0] // 2
     x = jnp.concatenate(
         [cur_ref[pl.ds(0, rows, stride=2), :], cur_ref[pl.ds(1, rows, stride=2), :]], axis=1
@@ -197,11 +196,11 @@
     for i in range(2):
         for j in range(2):
             put(own_ref, i * 2 + j, 1 + i, 1 + j)
-        put(beside_ref, i, to_beside, 1 + i)
-        put(away_ref, i, to_away, 1 + i)
-    for i, to_x in enumerate((1, 2, to_beside, to_away)):
-        put(down_ref, i, to_x, 0)
-        put(up_ref, i, to_x, 3)
+        put(down_ref, i, 1 + i, 0)
+        put(up_ref, i, 1 + i, 3)
+    for i, to_y in enumerate((1, 2, 0, 3)):
+        put(beside_ref, i, to_beside, to_y)
+        put(away_ref, i, to_away, to_y)
     acc_ref[...] = jnp.zeros_like(acc_ref)
 
     @pl.loop(0, 3)
@@ -228,7 +227,7 @@
 
 
 def translate_kernel(
-    slots_ref, kinds_ref, table_ref, src_ref, beside_ref, away_ref,
+    slots_ref, kinds_ref, table_ref, src_ref, down_ref, up_ref,
     keep_ref, swap_ref, far_ref, acc_ref,
 ):
     acc_ref[...] = jnp.zeros_like(acc_ref)
@@ -264,20 +263,20 @@
 
 
 def fold_kernel(
-    keep_ref, got_ref, cur_ref, beside_ref, away_ref,
-    back_ref, mid_ref, ahead_ref, down_ref, up_ref,
+    core_ref, keep_ref, got_ref, cur_ref, down_ref, up_ref,
+    back_ref, mid_ref, ahead_ref, beside_ref, away_ref,
 ):
     back_ref[...] = keep_ref[0] + got_ref[0]
     mid_ref[...] = keep_ref[1] + got_ref[1]
     ahead_ref[...] = keep_ref[2] + got_ref[2]
-    for ref, j in ((down_ref, 1), (up_ref, 0)):
-        for i in range(2):
-            ref[pl.ds(i * 96, 96), :] = cur_ref[pl.ds(i * 192 + j * 96, 96), :]
-        ref[pl.ds(192, 96), :] = beside_ref[pl.ds(j * 96, 96), :]
-        ref[pl.ds(288, 96), :] = away_ref[pl.ds(j * 96, 96), :]
-
-
-def join_kernel(mid_ref, far_ref, back_ref, ahead_ref, down_ref, up_ref, out_ref):
+    core = core_ref[0]
+    for ref, row in ((beside_ref, 1 - core), (away_ref, core)):
+        ref[pl.ds(0, 192), :] = cur_ref[pl.ds(pl.multiple_of(row * 192, 8), 192), :]
+        ref[pl.ds(192, 96), :] = down_ref[pl.ds(pl.multiple_of(row * 96, 8), 96), :]
+        ref[pl.ds(288, 96), :] = up_ref[pl.ds(pl.multiple_of(row * 96, 8), 96), :]
+
+
+def join_kernel(mid_ref, far_ref, back_ref, ahead_ref, beside_ref, away_ref, out_ref):
     out_ref[...] = (mid_ref[...] + far_ref[...]) + (back_ref[...] + ahead_ref[...])
 
 
@@ -301,8 +300,13 @@
     slab = lax.axis_index("slab")
     ring = slab % 8
     y, core = ring // 2, ring % 2
-    targets = lax.dynamic_slice_in_dim(far_targets.reshape(2, 8, 48, 16), ring, 1, 1)
-    kinds = lax.dynamic_slice_in_dim(far_offsets.reshape(2, 8, 48, 16), ring, 1, 1)
+
+    def own(table):
+        return jnp.concatenate(
+            [lax.dynamic_slice_in_dim(table, (ring + z_hi * 8) * 48, 48, 0) for z_hi in range(2)]
+        )
+
+    targets, kinds = own(far_targets), own(far_offsets)
     to_slab, row = targets // 48, targets % 48
     half, to_ring = to_slab // 8, to_slab % 8
     step = (to_ring // 2 - y + 4) % 4
@@ -340,20 +344,18 @@
     smem = pl.BlockSpec(memory_space=pltpu.SMEM)
     hbm = pl.BlockSpec(memory_space=pl.ANY)
 
-    patterns, beside, away = call(
+    patterns, down, up = call(
         aggregate_kernel,
         (f32(32, 3, 4, 128), f32(192, 128), f32(192, 128)),
         [pltpu.VMEM((2, 1024, 128), F32), pltpu.SemaphoreType.DMA((4,))],
-        in_specs=[smem, vmem, hbm, vmem],
+        in_specs=[vmem, hbm, vmem],
         flops=600_000_000,
         moved=2_000_000,
         vmem_bytes=62 * 1024 * 1024,
-    )(core, rows, radiation, child_phase)
+    )(rows, radiation, child_phase)
     moved = spread(patterns, groups)
-    beside = moved_by(beside, lambda z_hi, y, core, d: (z_hi, y, 1 - core, d))
-    away = lax.ppermute(
-        away, "slab", [(s, s + 2 * (s % 2) - 1) for s in range(16) if 0 <= s + 2 * (s % 2) - 1 < 16]
-    )
+    down = lax.ppermute(down, "dir", [(d, d + 1) for d in range(15)])
+    up = lax.ppermute(up, "dir", [(d + 1, d) for d in range(15)])
 
     keep, swap, far = call(
         translate_kernel,
@@ -362,26 +364,29 @@
         in_specs=[smem, smem, vmem, vmem, hbm, hbm],
         flops=100_000_000,
         moved=3_000_000,
-    )(slots, kinds, table, moved.reshape(96, 4, 128), beside, away)
+    )(slots, kinds, table, moved.reshape(96, 4, 128), down, up)
     far_in = moved_by(far, lambda z_hi, y, core, d: (z_hi, (y + 2) % 4, 1 - core, d))
     swap_in = moved_by(swap, lambda z_hi, y, core, d: (z_hi, y, 1 - core, d))
-    back, mid, ahead, down, up = call(
+    back, mid, ahead, beside, away = call(
         fold_kernel,
         (f32(96, 4, 128),) * 3 + (f32(384, 128),) * 2,
+        in_specs=[smem] + [vmem] * 5,
         flops=1_000_000,
         moved=2_000_000,
-    )(keep, swap_in, rows, beside, away)
+    )(core, keep, swap_in, rows, down, up)
     back_in = moved_by(back, lambda z_hi, y, core, d: (z_hi, (y + 3) % 4, core, d))
     ahead_in = moved_by(ahead, lambda z_hi, y, core, d: (z_hi, (y + 1) % 4, core, d))
-    down = lax.ppermute(down, "dir", [(d, d + 1) for d in range(15)])
-    up = lax.ppermute(up, "dir", [(d + 1, d) for d in range(15)])
+    beside = moved_by(beside, lambda z_hi, y, core, d: (z_hi, y, 1 - core, d))
+    away = lax.ppermute(
+        away, "slab", [(s, s + 2 * (s % 2) - 1) for s in range(16) if 0 <= s + 2 * (s % 2) - 1 < 16]
+    )
     incoming = call(
         join_kernel,
         f32(96, 4, 128),
         in_specs=[vmem] * 4 + [hbm] * 2,
         flops=1_000_000,
         moved=1_000_000,
-    )(mid, far_in, back_in, ahead_in, down, up)
+    )(mid, far_in, back_in, ahead_in, beside, away)
     returned = spread(incoming.reshape(32, 3, 4, 128), groups)
 
     near = call(

time: 74.7 us -> 74.6 us (level)
  the two profiles are of different devices: /device:TPU:8 before, /device:TPU:32 now
where the time goes in v2:
time: 74.6 us; the launch traced here: 74.2 us
  starting transfers between devices  40.8 us (55%)
  Pallas kernels  18.2 us (24%)
  waiting for transfers between devices  12.6 us (17%)
  local copies, waits for them, and re-layouts  2.04 us (3%)
    all_to_all x2, starting transfers between devices, spread(): lax.all_to_all(block, AXES, split_axis=0, concat_axis=0, axis_index_group...  26.7 us
    ppermute x5, waiting for transfers between devices, moved_by(): return lax.ppermute(block, AXES, route_of(move))  7.12 us
    pallas_call x1, Pallas kernels, per_device(): call(translate_kernel, (f32(3, 96, 4, 128), f32(3, 96, 4, 128), f32(96, 4...  5.62 us
    ppermute x5, starting transfers between devices, moved_by(): return lax.ppermute(block, AXES, route_of(move))  5.52 us
    pallas_call x1, Pallas kernels, per_device(): call(near_kernel, f32(192, 256), [pltpu.VMEM((27, 2, 128, 128), F32), plt...  5.31 us
    all_to_all x2, waiting for transfers between devices, spread(): lax.all_to_all(block, AXES, split_axis=0, concat_axis=0, axis_index_group...  5.22 us
    ppermute x1, starting transfers between devices, per_device(): up = lax.ppermute(up, 'dir', [(d + 1, d) for d in range(15)])  4.58 us
    pallas_call x1, Pallas kernels, per_device(): call(aggregate_kernel, (f32(32, 3, 4, 128), f32(192, 128), f32(192, 128))...  4.41 us
  transfers between devices with their start and end apart: 10, of which 5 were waited for; matrix products, arithmetic and copies ran while one was open for 3% of the time, Pallas kernels for 7%

profile of v2, /device:TPU:32, one launch (start us, length us, event | category | flops | bytes accessed | tf_op | source)
XLA Modules:
  0.0 74.2 jit_solution(12444881783885034017)
XLA Ops:
  0.0 0.0 copy-start
  0.0 4.4 %shard_map.73 = (f32[32,3,4,128]{3,2,1,0:T(4,128)}, f32[192,128]{1,0:T(8,128)}, f32[192,128]{1,0:T(8,128)}) custom-call(f32[384,128]{1,0:T(8,128)} %bitcast.8, f32[2,1024,128]{2,1,0:T(8,128)} %rad_ref.1, f32[8,1024]{1,0:T(8,128)} %phase_ref.3), custom_call_target="tpu_custom_call" | custom-call | flops 600000000 | bytes 2000000 | tf_op jit(solution)/shard_map/pallas_call | solution.py:347
  4.4 11.2 %all-to-all-start = ((f32[32,3,4,128]{3,2,1,0:T(4,128)}), f32[32,3,4,128]{3,2,1,0:T(4,128)S(1)}, u32[]{:S(2)}, u32[]{:S(2)}) async-start(f32[32,3,4,128]{3,2,1,0:T(4,128)} %get-tuple-element.16), calls=%async_computation | async-start | bytes 393216 | tf_op jit(solution)/shard_map/all_to_all | solution.py:332
  15.6 3.4 %collective-permute-start = (f32[192,128]{1,0:T(8,128)}, f32[192,128]{1,0:T(8,128)S(1)}, u32[]{:S(2)}, u32[]{:S(2)}) collective-permute-start(f32[192,128]{1,0:T(8,128)} %get-tuple-element.17), channel_id=1, source_target_pairs={{0,1},{1,2},{2,3},{3,4},{4,5},{5,6},{6,7},{7,8},{8,9},{9,10},{10,1... | collective-permute-start | bytes 294920 | tf_op jit(solution)/shard_map/ppermute | solution.py:357
  19.0 4.6 %collective-permute-start.1 = (f32[192,128]{1,0:T(8,128)}, f32[192,128]{1,0:T(8,128)S(1)}, u32[]{:S(2)}, u32[]{:S(2)}) collective-permute-start(f32[192,128]{1,0:T(8,128)} %get-tuple-element.18), channel_id=1, source_target_pairs={{1,0},{2,1},{3,2},{4,3},{5,4},{6,5},{7,6},{8,7},{9,8},{10,9},{11,1... | collective-permute-start | bytes 294920 | tf_op jit(solution)/shard_map/ppermute | solution.py:358
  23.6 0.9 %constant_dynamic-slice_fusion.2 = (s32[48,16]{0,1:T(8,128)S(1)}, s32[48,16]{0,1:T(8,128)S(1)}, s32[48,16]{0,1:T(8,128)S(1)}, s32[48,16]{0,1:T(8,128)S(1)}) fusion(s32[768,16]{0,1:T(8,128)} %param.13, s32[]{:T(128)S(6)} %select_n.86, s32[]{:T(128)S(6)} %select_n.87, s32[768,16]{0,1:T(8,128)} %param.12), kind=kLoop, calls=%fused_computation.43 | loop fusion | bytes 24584 | tf_op jit(solution)/shard_map/dynamic_slice | solution.py:306
  24.5 0.1 add_multiply_fusion
  24.6 0.1 broadcast_divide_fusion
  24.6 0.0 copy-done
  24.7 0.1 sign_compare_fusion.2
  24.8 0.1 copy.9
  24.9 0.1 ne.103
  25.0 0.1 copy.11
  25.1 0.1 div.42
  25.2 0.1 copy.12
  25.3 0.1 mul.41.kinds_ref
  25.3 0.1 copy.10
  25.4 0.1 rem.141
  25.5 0.1 fusion.9.slots_ref
  25.6 0.2 copy.13
  25.8 0.0 collective-permute-done.down_ref
  25.8 0.3 collective-permute-done.1.up_ref
  26.1 0.4 all-to-all-done
  26.5 0.2 broadcast_in_dim.15
  26.7 5.6 %shard_map.74 = (f32[3,96,4,128]{3,2,1,0:T(4,128)S(1)}, f32[3,96,4,128]{3,2,1,0:T(4,128)S(1)}, f32[96,4,128]{2,1,0:T(4,128)S(1)}) custom-call(s32[1536]{0:T(1024)S(1)} %fusion.9.slots_ref, s32[1536]{0:T(1024)S(1)} %mul.41.kinds_ref, f32[2528,128]{1,0:T(8,128)S(1)} %bitcast.6, f32[96,4,128]{2,1,0:T(4,128)S(1)} %bitcast.7, ...), custom_call_target="tpu_custom_call" | custom-call | flops 100000000 | bytes 3000000 | tf_op jit(solution)/shard_map/pallas_call | solution.py:360
  32.3 0.1 collective-permute-start.2
  32.5 3.3 %collective-permute-start.3 = (f32[96,4,128]{2,1,0:T(4,128)S(1)}, f32[96,4,128]{2,1,0:T(4,128)S(1)}, u32[]{:S(2)}, u32[]{:S(2)}) collective-permute-start(f32[96,4,128]{2,1,0:T(4,128)S(1)} %get-tuple-element.22), channel_id=1, source_target_pairs={{0,80},{1,81},{2,82},{3,83},{4,84},{5,85},{6,86},{7,87},{8,88},{9,... | collective-permute-start | bytes 589832 | tf_op jit(solution)/shard_map/ppermute | solution.py:328
  35.8 0.0 collective-permute-done.2.got_ref
  35.8 0.0 copy-done.1
  35.8 0.2 shard_map.75
  36.0 1.8 %collective-permute-start.4 = (f32[96,4,128]{2,1,0:T(4,128)S(1)}, f32[96,4,128]{2,1,0:T(4,128)S(1)}, u32[]{:S(2)}, u32[]{:S(2)}) collective-permute-start(f32[96,4,128]{2,1,0:T(4,128)S(1)} %get-tuple-element.23), channel_id=1, source_target_pairs={{0,96},{1,97},{2,98},{3,99},{4,100},{5,101},{6,102},{7,103},{8,104... | collective-permute-start | bytes 589832 | tf_op jit(solution)/shard_map/ppermute | solution.py:328
  37.7 0.4 collective-permute-start.5
  38.1 0.0 collective-permute-start.6
  38.1 0.7 collective-permute-start.7
  38.7 2.3 %collective-permute-done.3.far_ref = f32[96,4,128]{2,1,0:T(4,128)S(1)} collective-permute-done((f32[96,4,128]{2,1,0:T(4,128)S(1)}, f32[96,4,128]{2,1,0:T(4,128)S(1)}, u32[]{:S(2)}, u32[]{:S(2)}) %collective-permute-start.3) | collective-permute-done | bytes 196640 | tf_op jit(solution)/shard_map/ppermute | solution.py:328
  41.1 4.8 %collective-permute-done.4.back_ref = f32[96,4,128]{2,1,0:T(4,128)S(1)} collective-permute-done((f32[96,4,128]{2,1,0:T(4,128)S(1)}, f32[96,4,128]{2,1,0:T(4,128)S(1)}, u32[]{:S(2)}, u32[]{:S(2)}) %collective-permute-start.4) | collective-permute-done | bytes 196640 | tf_op jit(solution)/shard_map/ppermute | solution.py:328
  45.9 0.0 collective-permute-done.5.ahead_ref
  45.9 0.0 collective-permute-done.6.beside_ref
  45.9 0.0 collective-permute-done.7.away_ref
  45.9 0.8 %shard_map.76 = f32[96,4,128]{2,1,0:T(4,128)} custom-call(f32[96,4,128]{2,1,0:T(4,128)S(1)} %get-tuple-element.21.mid_ref, f32[96,4,128]{2,1,0:T(4,128)S(1)} %collective-permute-done.3.far_ref, f32[96,4,128]{2,1,0:T(4,128)S(1)} %collective-permute-done.4.back_ref, f32[96,4,128]{2,1,0:T(4,128)S(1)} %collective-permute-done.5.ahead_ref, ...), custom_call_target="tpu_custom_call" | custom-call | flops 1000000 | bytes 1000000 | tf_op jit(solution)/shard_map/pallas_call | solution.py:383
  46.6 15.5 %all-to-all-start.1 = ((f32[32,3,4,128]{3,2,1,0:T(4,128)}), f32[32,3,4,128]{3,2,1,0:T(4,128)S(1)}, u32[]{:S(2)}, u32[]{:S(2)}) async-start(f32[32,3,4,128]{3,2,1,0:T(4,128)} %bitcast.4), calls=%async_computation.1 | async-start | bytes 393216 | tf_op jit(solution)/shard_map/all_to_all | solution.py:332
  62.1 0.0 copy-start.2
  62.2 0.0 copy-start.3
  62.2 5.3 %shard_map.77.near_ref = f32[192,256]{1,0:T(8,128)S(1)} custom-call(s32[1]{0:T(128)} %bitcast.core_ref, f32[384,128]{1,0:T(8,128)S(1)} %bitcast.10, f32[384,128]{1,0:T(8,128)S(1)} %collective-permute-done.6.beside_ref, f32[384,128]{1,0:T(8,128)S(1)} %collective-permute-done.7.away_ref, f32[192,128]{1,0:T(8,128)S(1)} %collective-permute-done.down_ref, ...), custom_call_target="tpu_custom_call" | custom-call | flops 2000000000 | bytes 5000000 | tf_op jit(solution)/shard_map/pallas_call | solution.py:392
  67.5 4.8 %all-to-all-done.1.in_ref = f32[32,3,4,128]{3,2,1,0:T(4,128)S(1)} async-done(((f32[32,3,4,128]{3,2,1,0:T(4,128)}), f32[32,3,4,128]{3,2,1,0:T(4,128)S(1)}, u32[]{:S(2)}, u32[]{:S(2)}) %all-to-all-start.1) | async-done | bytes 196640 | tf_op jit(solution)/shard_map/all_to_all | solution.py:332
  72.3 0.0 copy-done.2
  72.3 0.0 copy-done.3
  72.3 1.9 %shard_map.78 = f32[384,128]{1,0:T(8,128)} custom-call(f32[32,3,4,128]{3,2,1,0:T(4,128)S(1)} %all-to-all-done.1.in_ref, f32[2,1024,128]{2,1,0:T(8,128)S(1)} %copy-done.2, f32[8,1024]{1,0:T(8,128)S(1)} %copy-done.3, f32[192,256]{1,0:T(8,128)S(1)} %shard_map.77.near_ref), custom_call_target="tpu_custom_call" | custom-call | flops 600000000 | bytes 2000000 | tf_op jit(solution)/shard_map/pallas_call | solution.py:408
  (3 shorter events, 0.0 us)
Async XLA Ops:
  0.0 24.6 %copy-start = (f32[316,2,64]{0,2,1:T(8,128)S(1)}, f32[316,2,64]{0,2,1:T(8,128)}, u32[]{:S(2)}) copy-start(f32[316,2,64]{0,2,1:T(8,128)} %param.11) | copy-start | bytes 485380
  0.0 35.8 %copy-start.1 = (f32[2,2,6,8,2,128]{5,4,3,2,1,0:T(2,128)S(1)}, f32[2,2,6,8,2,128]{5,4,3,2,1,0:T(2,128)}, u32[]{:S(2)}) copy-start(f32[2,2,6,8,2,128]{5,4,3,2,1,0:T(2,128)} %param.7) | copy-start | bytes 589828
  4.4 22.1 %all-to-all-start = ((f32[32,3,4,128]{3,2,1,0:T(4,128)}), f32[32,3,4,128]{3,2,1,0:T(4,128)S(1)}, u32[]{:S(2)}, u32[]{:S(2)}) async-start(f32[32,3,4,128]{3,2,1,0:T(4,128)} %get-tuple-element.16), calls=%async_computation | async-start | bytes 393216 | tf_op jit(solution)/shard_map/all_to_all | solution.py:332
  15.6 10.2 %collective-permute-start = (f32[192,128]{1,0:T(8,128)}, f32[192,128]{1,0:T(8,128)S(1)}, u32[]{:S(2)}, u32[]{:S(2)}) collective-permute-start(f32[192,128]{1,0:T(8,128)} %get-tuple-element.17), channel_id=1, source_target_pairs={{0,1},{1,2},{2,3},{3,4},{4,5},{5,6},{6,7},{7,8},{8,9},{9,10},{10,1... | collective-permute-start | bytes 294920 | tf_op jit(solution)/shard_map/ppermute | solution.py:357
  19.0 7.1 %collective-permute-start.1 = (f32[192,128]{1,0:T(8,128)}, f32[192,128]{1,0:T(8,128)S(1)}, u32[]{:S(2)}, u32[]{:S(2)}) collective-permute-start(f32[192,128]{1,0:T(8,128)} %get-tuple-element.18), channel_id=1, source_target_pairs={{1,0},{2,1},{3,2},{4,3},{5,4},{6,5},{7,6},{8,7},{9,8},{10,9},{11,1... | collective-permute-start | bytes 294920 | tf_op jit(solution)/shard_map/ppermute | solution.py:358
  32.3 3.4 %collective-permute-start.2 = (f32[3,96,4,128]{3,2,1,0:T(4,128)S(1)}, f32[3,96,4,128]{3,2,1,0:T(4,128)S(1)}, u32[]{:S(2)}, u32[]{:S(2)}) collective-permute-start(f32[3,96,4,128]{3,2,1,0:T(4,128)S(1)} %get-tuple-element.20), channel_id=1, source_target_pairs={{0,16},{1,17},{2,18},{3,19},{4,20},{5,21},{6,22},{7,23},{8,24},{9,... | collective-permute-start | bytes 1769480 | tf_op jit(solution)/shard_map/ppermute | solution.py:328
  32.5 8.6 %collective-permute-start.3 = (f32[96,4,128]{2,1,0:T(4,128)S(1)}, f32[96,4,128]{2,1,0:T(4,128)S(1)}, u32[]{:S(2)}, u32[]{:S(2)}) collective-permute-start(f32[96,4,128]{2,1,0:T(4,128)S(1)} %get-tuple-element.22), channel_id=1, source_target_pairs={{0,80},{1,81},{2,82},{3,83},{4,84},{5,85},{6,86},{7,87},{8,88},{9,... | collective-permute-start | bytes 589832 | tf_op jit(solution)/shard_map/ppermute | solution.py:328
  36.0 9.9 %collective-permute-start.4 = (f32[96,4,128]{2,1,0:T(4,128)S(1)}, f32[96,4,128]{2,1,0:T(4,128)S(1)}, u32[]{:S(2)}, u32[]{:S(2)}) collective-permute-start(f32[96,4,128]{2,1,0:T(4,128)S(1)} %get-tuple-element.23), channel_id=1, source_target_pairs={{0,96},{1,97},{2,98},{3,99},{4,100},{5,101},{6,102},{7,103},{8,104... | collective-permute-start | bytes 589832 | tf_op jit(solution)/shard_map/ppermute | solution.py:328
  37.7 8.1 %collective-permute-start.5 = (f32[96,4,128]{2,1,0:T(4,128)S(1)}, f32[96,4,128]{2,1,0:T(4,128)S(1)}, u32[]{:S(2)}, u32[]{:S(2)}) collective-permute-start(f32[96,4,128]{2,1,0:T(4,128)S(1)} %get-tuple-element.24), channel_id=1, source_target_pairs={{0,32},{1,33},{2,34},{3,35},{4,36},{5,37},{6,38},{7,39},{8,40},{9,... | collective-permute-start | bytes 589832 | tf_op jit(solution)/shard_map/ppermute | solution.py:328
  38.1 7.8 %collective-permute-start.6 = (f32[384,128]{1,0:T(8,128)S(1)}, f32[384,128]{1,0:T(8,128)S(1)}, u32[]{:S(2)}, u32[]{:S(2)}) collective-permute-start(f32[384,128]{1,0:T(8,128)S(1)} %get-tuple-element.25), channel_id=1, source_target_pairs={{0,16},{1,17},{2,18},{3,19},{4,20},{5,21},{6,22},{7,23},{8,24},{9,... | collective-permute-start | bytes 589832 | tf_op jit(solution)/shard_map/ppermute | solution.py:328
  38.1 7.8 %collective-permute-start.7 = (f32[384,128]{1,0:T(8,128)S(1)}, f32[384,128]{1,0:T(8,128)S(1)}, u32[]{:S(2)}, u32[]{:S(2)}) collective-permute-start(f32[384,128]{1,0:T(8,128)S(1)} %get-tuple-element.26), channel_id=1, source_target_pairs={{16,32},{32,16},{48,64},{64,48},{80,96},{96,80},{112,128},{128,112... | collective-permute-start | bytes 589832 | tf_op jit(solution)/shard_map/ppermute | solution.py:380
  46.6 25.7 %all-to-all-start.1 = ((f32[32,3,4,128]{3,2,1,0:T(4,128)}), f32[32,3,4,128]{3,2,1,0:T(4,128)S(1)}, u32[]{:S(2)}, u32[]{:S(2)}) async-start(f32[32,3,4,128]{3,2,1,0:T(4,128)} %bitcast.4), calls=%async_computation.1 | async-start | bytes 393216 | tf_op jit(solution)/shard_map/all_to_all | solution.py:332
  62.1 10.2 %copy-start.2 = (f32[2,1024,128]{2,1,0:T(8,128)S(1)}, f32[2,1024,128]{2,1,0:T(8,128)}, u32[]{:S(2)}) copy-start(f32[2,1024,128]{2,1,0:T(8,128)} %rad_ref.1) | copy-start | bytes 3145732
  62.2 10.2 %copy-start.3 = (f32[8,1024]{1,0:T(8,128)S(1)}, f32[8,1024]{1,0:T(8,128)}, u32[]{:S(2)}) copy-start(f32[8,1024]{1,0:T(8,128)} %phase_ref.3) | copy-start | bytes 98308

commit v3 on v2

--- a/solution.py
+++ b/solution.py
@@ -263,21 +263,23 @@
 
 
 def fold_kernel(
-    core_ref, keep_ref, got_ref, cur_ref, down_ref, up_ref,
+    core_ref, keep_ref, got_ref, far_ref, cur_ref, down_ref, up_ref,
     back_ref, mid_ref, ahead_ref, beside_ref, away_ref,
 ):
-    back_ref[...] = keep_ref[0] + got_ref[0]
+    core = core_ref[0]
+    far = far_ref[...]
+    zero = jnp.zeros_like(far)
+    back_ref[...] = keep_ref[0] + got_ref[0] + jnp.where(core == 1, far, zero)
     mid_ref[...] = keep_ref[1] + got_ref[1]
-    ahead_ref[...] = keep_ref[2] + got_ref[2]
-    core = core_ref[0]
+    ahead_ref[...] = keep_ref[2] + got_ref[2] + jnp.where(core == 0, far, zero)
     for ref, row in ((beside_ref, 1 - core), (away_ref, core)):
         ref[pl.ds(0, 192), :] = cur_ref[pl.ds(pl.multiple_of(row * 192, 8), 192), :]
         ref[pl.ds(192, 96), :] = down_ref[pl.ds(pl.multiple_of(row * 96, 8), 96), :]
         ref[pl.ds(288, 96), :] = up_ref[pl.ds(pl.multiple_of(row * 96, 8), 96), :]
 
 
-def join_kernel(mid_ref, far_ref, back_ref, ahead_ref, beside_ref, away_ref, out_ref):
-    out_ref[...] = (mid_ref[...] + far_ref[...]) + (back_ref[...] + ahead_ref[...])
+def join_kernel(mid_ref, back_ref, ahead_ref, out_ref):
+    out_ref[...] = mid_ref[...] + (back_ref[...] + ahead_ref[...])
 
 
 def call(kernel, out_shape, scratch=(), in_specs=None, flops=0, moved=0, vmem_bytes=VMEM_BYTES):
@@ -365,15 +367,15 @@
         flops=100_000_000,
         moved=3_000_000,
     )(slots, kinds, table, moved.reshape(96, 4, 128), down, up)
-    far_in = moved_by(far, lambda z_hi, y, core, d: (z_hi, (y + 2) % 4, 1 - core, d))
+    far_in = moved_by(far, lambda z_hi, y, core, d: (z_hi, (y + 2 * core - 1) % 4, 1 - core, d))
     swap_in = moved_by(swap, lambda z_hi, y, core, d: (z_hi, y, 1 - core, d))
     back, mid, ahead, beside, away = call(
         fold_kernel,
         (f32(96, 4, 128),) * 3 + (f32(384, 128),) * 2,
-        in_specs=[smem] + [vmem] * 5,
+        in_specs=[smem] + [vmem] * 6,
         flops=1_000_000,
         moved=2_000_000,
-    )(core, keep, swap_in, rows, down, up)
+    )(core, keep, swap_in, far_in, rows, down, up)
     back_in = moved_by(back, lambda z_hi, y, core, d: (z_hi, (y + 3) % 4, core, d))
     ahead_in = moved_by(ahead, lambda z_hi, y, core, d: (z_hi, (y + 1) % 4, core, d))
     beside = moved_by(beside, lambda z_hi, y, core, d: (z_hi, y, 1 - core, d))
@@ -383,10 +385,9 @@
     incoming = call(
         join_kernel,
         f32(96, 4, 128),
-        in_specs=[vmem] * 4 + [hbm] * 2,
         flops=1_000_000,
         moved=1_000_000,
-    )(mid, far_in, back_in, ahead_in, beside, away)
+    )(mid, back_in, ahead_in)
     returned = spread(incoming.reshape(32, 3, 4, 128), groups)
 
     near = call(

time: 74.6 us -> 74.2 us (level)
  the two profiles are of different devices: /device:TPU:32 before, /device:TPU:1 now
where the time goes in v3:
time: 74.2 us; the launch traced here: 73.8 us
  starting transfers between devices  34.9 us (47%)
  Pallas kernels  18.2 us (25%)
  waiting for transfers between devices  18.2 us (25%)
  local copies, waits for them, and re-layouts  2.04 us (3%)
    all_to_all x2, starting transfers between devices, spread(): lax.all_to_all(block, AXES, split_axis=0, concat_axis=0, axis_index_group...  19.8 us
    ppermute x5, waiting for transfers between devices, moved_by(): return lax.ppermute(block, AXES, route_of(move))  9.66 us
    ppermute x5, starting transfers between devices, moved_by(): return lax.ppermute(block, AXES, route_of(move))  8.74 us
    all_to_all x2, waiting for transfers between devices, spread(): lax.all_to_all(block, AXES, split_axis=0, concat_axis=0, axis_index_group...  5.77 us
    pallas_call x1, Pallas kernels, per_device(): call(translate_kernel, (f32(3, 96, 4, 128), f32(3, 96, 4, 128), f32(96, 4...  5.62 us
    pallas_call x1, Pallas kernels, per_device(): call(near_kernel, f32(192, 256), [pltpu.VMEM((27, 2, 128, 128), F32), plt...  5.29 us
    pallas_call x1, Pallas kernels, per_device(): call(aggregate_kernel, (f32(32, 3, 4, 128), f32(192, 128), f32(192, 128))...  4.41 us
    ppermute x1, starting transfers between devices, per_device(): down = lax.ppermute(down, 'dir', [(d, d + 1) for d in range(15)])  3.14 us
  transfers between devices with their start and end apart: 10, of which 6 were waited for; matrix products, arithmetic and copies ran while one was open for 3% of the time, Pallas kernels for 8%

profile of v3, /device:TPU:1, one launch (start us, length us, event | category | flops | bytes accessed | tf_op | source)
XLA Modules:
  0.0 73.8 jit_solution(645917618931382678)
XLA Ops:
  0.0 0.0 copy-start
  0.0 4.4 %shard_map.73 = (f32[32,3,4,128]{3,2,1,0:T(4,128)}, f32[192,128]{1,0:T(8,128)}, f32[192,128]{1,0:T(8,128)}) custom-call(f32[384,128]{1,0:T(8,128)} %bitcast.8, f32[2,1024,128]{2,1,0:T(8,128)} %rad_ref.1, f32[8,1024]{1,0:T(8,128)} %phase_ref.3), custom_call_target="tpu_custom_call" | custom-call | flops 600000000 | bytes 2000000 | tf_op jit(solution)/shard_map/pallas_call | solution.py:349
  4.4 11.9 %all-to-all-start = ((f32[32,3,4,128]{3,2,1,0:T(4,128)}), f32[32,3,4,128]{3,2,1,0:T(4,128)S(1)}, u32[]{:S(2)}, u32[]{:S(2)}) async-start(f32[32,3,4,128]{3,2,1,0:T(4,128)} %get-tuple-element.16), calls=%async_computation | async-start | bytes 393216 | tf_op jit(solution)/shard_map/all_to_all | solution.py:334
  16.3 3.1 %collective-permute-start = (f32[192,128]{1,0:T(8,128)}, f32[192,128]{1,0:T(8,128)S(1)}, u32[]{:S(2)}, u32[]{:S(2)}) collective-permute-start(f32[192,128]{1,0:T(8,128)} %get-tuple-element.17), channel_id=1, source_target_pairs={{0,1},{1,2},{2,3},{3,4},{4,5},{5,6},{6,7},{7,8},{8,9},{9,10},{10,1... | collective-permute-start | bytes 294920 | tf_op jit(solution)/shard_map/ppermute | solution.py:359
  19.5 1.3 %collective-permute-start.1 = (f32[192,128]{1,0:T(8,128)}, f32[192,128]{1,0:T(8,128)S(1)}, u32[]{:S(2)}, u32[]{:S(2)}) collective-permute-start(f32[192,128]{1,0:T(8,128)} %get-tuple-element.18), channel_id=1, source_target_pairs={{1,0},{2,1},{3,2},{4,3},{5,4},{6,5},{7,6},{8,7},{9,8},{10,9},{11,1... | collective-permute-start | bytes 294920 | tf_op jit(solution)/shard_map/ppermute | solution.py:360
  20.8 0.9 %constant_dynamic-slice_fusion.2 = (s32[48,16]{0,1:T(8,128)S(1)}, s32[48,16]{0,1:T(8,128)S(1)}, s32[48,16]{0,1:T(8,128)S(1)}, s32[48,16]{0,1:T(8,128)S(1)}) fusion(s32[768,16]{0,1:T(8,128)} %param.13, s32[]{:T(128)S(6)} %select_n.86, s32[]{:T(128)S(6)} %select_n.87, s32[768,16]{0,1:T(8,128)} %param.12), kind=kLoop, calls=%fused_computation.43 | loop fusion | bytes 24584 | tf_op jit(solution)/shard_map/dynamic_slice | solution.py:308
  21.6 0.1 add_multiply_fusion
  21.7 0.1 broadcast_divide_fusion
  21.8 0.0 copy-done
  21.8 0.1 sign_compare_fusion.2
  21.9 0.1 copy.9
  22.0 0.1 ne.103
  22.1 0.1 copy.11
  22.2 0.1 div.42
  22.3 0.1 copy.12
  22.4 0.1 mul.41.kinds_ref
  22.5 0.1 copy.10
  22.6 0.1 rem.141
  22.7 0.1 fusion.9.slots_ref
  22.8 0.2 copy.13
  23.0 0.0 collective-permute-done.down_ref
  23.0 2.7 %collective-permute-done.1.up_ref = f32[192,128]{1,0:T(8,128)S(1)} collective-permute-done((f32[192,128]{1,0:T(8,128)}, f32[192,128]{1,0:T(8,128)S(1)}, u32[]{:S(2)}, u32[]{:S(2)}) %collective-permute-start.1) | collective-permute-done | bytes 98336 | tf_op jit(solution)/shard_map/ppermute | solution.py:360
  25.7 0.5 all-to-all-done
  26.2 0.2 broadcast_in_dim.15
  26.5 5.6 %shard_map.74 = (f32[3,96,4,128]{3,2,1,0:T(4,128)S(1)}, f32[3,96,4,128]{3,2,1,0:T(4,128)S(1)}, f32[96,4,128]{2,1,0:T(4,128)S(1)}) custom-call(s32[1536]{0:T(1024)S(1)} %fusion.9.slots_ref, s32[1536]{0:T(1024)S(1)} %mul.41.kinds_ref, f32[2528,128]{1,0:T(8,128)S(1)} %bitcast.6, f32[96,4,128]{2,1,0:T(4,128)S(1)} %bitcast.7, ...), custom_call_target="tpu_custom_call" | custom-call | flops 100000000 | bytes 3000000 | tf_op jit(solution)/shard_map/pallas_call | solution.py:362
  32.1 3.7 %collective-permute-start.2 = (f32[3,96,4,128]{3,2,1,0:T(4,128)S(1)}, f32[3,96,4,128]{3,2,1,0:T(4,128)S(1)}, u32[]{:S(2)}, u32[]{:S(2)}) collective-permute-start(f32[3,96,4,128]{3,2,1,0:T(4,128)S(1)} %get-tuple-element.20), channel_id=1, source_target_pairs={{0,16},{1,17},{2,18},{3,19},{4,20},{5,21},{6,22},{7,23},{8,24},{9,... | collective-permute-start | bytes 1769480 | tf_op jit(solution)/shard_map/ppermute | solution.py:330
  35.8 1.3 %collective-permute-start.3 = (f32[96,4,128]{2,1,0:T(4,128)S(1)}, f32[96,4,128]{2,1,0:T(4,128)S(1)}, u32[]{:S(2)}, u32[]{:S(2)}) collective-permute-start(f32[96,4,128]{2,1,0:T(4,128)S(1)} %get-tuple-element.21), channel_id=1, source_target_pairs={{0,112},{1,113},{2,114},{3,115},{4,116},{5,117},{6,118},{7,119},{8... | collective-permute-start | bytes 589832 | tf_op jit(solution)/shard_map/ppermute | solution.py:330
  37.1 4.1 %collective-permute-done.3.far_ref = f32[96,4,128]{2,1,0:T(4,128)S(1)} collective-permute-done((f32[96,4,128]{2,1,0:T(4,128)S(1)}, f32[96,4,128]{2,1,0:T(4,128)S(1)}, u32[]{:S(2)}, u32[]{:S(2)}) %collective-permute-start.3) | collective-permute-done | bytes 196640 | tf_op jit(solution)/shard_map/ppermute | solution.py:330
  41.2 0.0 collective-permute-done.2.got_ref
  41.2 0.0 copy-done.1
  41.2 0.2 shard_map.75
  41.4 3.7 %collective-permute-start.4 = (f32[96,4,128]{2,1,0:T(4,128)S(1)}, f32[96,4,128]{2,1,0:T(4,128)S(1)}, u32[]{:S(2)}, u32[]{:S(2)}) collective-permute-start(f32[96,4,128]{2,1,0:T(4,128)S(1)} %get-tuple-element.23), channel_id=1, source_target_pairs={{0,96},{1,97},{2,98},{3,99},{4,100},{5,101},{6,102},{7,103},{8,104... | collective-permute-start | bytes 589832 | tf_op jit(solution)/shard_map/ppermute | solution.py:330
  45.2 0.0 collective-permute-start.5
  45.2 0.0 collective-permute-start.6
  45.2 1.9 %collective-permute-start.7 = (f32[384,128]{1,0:T(8,128)S(1)}, f32[384,128]{1,0:T(8,128)S(1)}, u32[]{:S(2)}, u32[]{:S(2)}) collective-permute-start(f32[384,128]{1,0:T(8,128)S(1)} %get-tuple-element.26), channel_id=1, source_target_pairs={{16,32},{32,16},{48,64},{64,48},{80,96},{96,80},{112,128},{128,112... | collective-permute-start | bytes 589832 | tf_op jit(solution)/shard_map/ppermute | solution.py:382
  47.1 2.1 %collective-permute-done.4.back_ref = f32[96,4,128]{2,1,0:T(4,128)S(1)} collective-permute-done((f32[96,4,128]{2,1,0:T(4,128)S(1)}, f32[96,4,128]{2,1,0:T(4,128)S(1)}, u32[]{:S(2)}, u32[]{:S(2)}) %collective-permute-start.4) | collective-permute-done | bytes 196640 | tf_op jit(solution)/shard_map/ppermute | solution.py:330
  49.2 3.4 %collective-permute-done.5.ahead_ref = f32[96,4,128]{2,1,0:T(4,128)S(1)} collective-permute-done((f32[96,4,128]{2,1,0:T(4,128)S(1)}, f32[96,4,128]{2,1,0:T(4,128)S(1)}, u32[]{:S(2)}, u32[]{:S(2)}) %collective-permute-start.5) | collective-permute-done | bytes 196640 | tf_op jit(solution)/shard_map/ppermute | solution.py:330
  52.6 0.7 %shard_map.76 = f32[96,4,128]{2,1,0:T(4,128)} custom-call(f32[96,4,128]{2,1,0:T(4,128)S(1)} %get-tuple-element.22.mid_ref, f32[96,4,128]{2,1,0:T(4,128)S(1)} %collective-permute-done.4.back_ref, f32[96,4,128]{2,1,0:T(4,128)S(1)} %collective-permute-done.5.ahead_ref), custom_call_target="tpu_custom_call" | custom-call | flops 1000000 | bytes 1000000 | tf_op jit(solution)/shard_map/pallas_call | solution.py:385
  53.4 7.9 %all-to-all-start.1 = ((f32[32,3,4,128]{3,2,1,0:T(4,128)}), f32[32,3,4,128]{3,2,1,0:T(4,128)S(1)}, u32[]{:S(2)}, u32[]{:S(2)}) async-start(f32[32,3,4,128]{3,2,1,0:T(4,128)} %bitcast.4), calls=%async_computation.1 | async-start | bytes 393216 | tf_op jit(solution)/shard_map/all_to_all | solution.py:334
  61.3 0.0 copy-start.2
  61.3 0.0 copy-start.3
  61.3 0.0 collective-permute-done.6.beside_ref
  61.4 0.0 collective-permute-done.7.away_ref
  61.4 5.3 %shard_map.77.near_ref = f32[192,256]{1,0:T(8,128)S(1)} custom-call(s32[1]{0:T(128)} %bitcast.core_ref, f32[384,128]{1,0:T(8,128)S(1)} %bitcast.10, f32[384,128]{1,0:T(8,128)S(1)} %collective-permute-done.6.beside_ref, f32[384,128]{1,0:T(8,128)S(1)} %collective-permute-done.7.away_ref, f32[192,128]{1,0:T(8,128)S(1)} %collective-permute-done.down_ref, ...), custom_call_target="tpu_custom_call" | custom-call | flops 2000000000 | bytes 5000000 | tf_op jit(solution)/shard_map/pallas_call | solution.py:393
  66.7 5.2 %all-to-all-done.1.in_ref = f32[32,3,4,128]{3,2,1,0:T(4,128)S(1)} async-done(((f32[32,3,4,128]{3,2,1,0:T(4,128)}), f32[32,3,4,128]{3,2,1,0:T(4,128)S(1)}, u32[]{:S(2)}, u32[]{:S(2)}) %all-to-all-start.1) | async-done | bytes 196640 | tf_op jit(solution)/shard_map/all_to_all | solution.py:334
  71.9 0.0 copy-done.2
  71.9 0.0 copy-done.3
  71.9 1.9 %shard_map.78 = f32[384,128]{1,0:T(8,128)} custom-call(f32[32,3,4,128]{3,2,1,0:T(4,128)S(1)} %all-to-all-done.1.in_ref, f32[2,1024,128]{2,1,0:T(8,128)S(1)} %copy-done.2, f32[8,1024]{1,0:T(8,128)S(1)} %copy-done.3, f32[192,256]{1,0:T(8,128)S(1)} %shard_map.77.near_ref), custom_call_target="tpu_custom_call" | custom-call | flops 600000000 | bytes 2000000 | tf_op jit(solution)/shard_map/pallas_call | solution.py:409
  (3 shorter events, 0.0 us)
Async XLA Ops:
  0.0 21.8 %copy-start = (f32[316,2,64]{0,2,1:T(8,128)S(1)}, f32[316,2,64]{0,2,1:T(8,128)}, u32[]{:S(2)}) copy-start(f32[316,2,64]{0,2,1:T(8,128)} %param.11) | copy-start | bytes 485380
  0.0 41.2 %copy-start.1 = (f32[2,2,6,8,2,128]{5,4,3,2,1,0:T(2,128)S(1)}, f32[2,2,6,8,2,128]{5,4,3,2,1,0:T(2,128)}, u32[]{:S(2)}) copy-start(f32[2,2,6,8,2,128]{5,4,3,2,1,0:T(2,128)} %param.7) | copy-start | bytes 589828
  4.4 21.8 %all-to-all-start = ((f32[32,3,4,128]{3,2,1,0:T(4,128)}), f32[32,3,4,128]{3,2,1,0:T(4,128)S(1)}, u32[]{:S(2)}, u32[]{:S(2)}) async-start(f32[32,3,4,128]{3,2,1,0:T(4,128)} %get-tuple-element.16), calls=%async_computation | async-start | bytes 393216 | tf_op jit(solution)/shard_map/all_to_all | solution.py:334
  16.3 6.7 %collective-permute-start = (f32[192,128]{1,0:T(8,128)}, f32[192,128]{1,0:T(8,128)S(1)}, u32[]{:S(2)}, u32[]{:S(2)}) collective-permute-start(f32[192,128]{1,0:T(8,128)} %get-tuple-element.17), channel_id=1, source_target_pairs={{0,1},{1,2},{2,3},{3,4},{4,5},{5,6},{6,7},{7,8},{8,9},{9,10},{10,1... | collective-permute-start | bytes 294920 | tf_op jit(solution)/shard_map/ppermute | solution.py:359
  19.5 6.2 %collective-permute-start.1 = (f32[192,128]{1,0:T(8,128)}, f32[192,128]{1,0:T(8,128)S(1)}, u32[]{:S(2)}, u32[]{:S(2)}) collective-permute-start(f32[192,128]{1,0:T(8,128)} %get-tuple-element.18), channel_id=1, source_target_pairs={{1,0},{2,1},{3,2},{4,3},{5,4},{6,5},{7,6},{8,7},{9,8},{10,9},{11,1... | collective-permute-start | bytes 294920 | tf_op jit(solution)/shard_map/ppermute | solution.py:360
  32.1 9.1 %collective-permute-start.2 = (f32[3,96,4,128]{3,2,1,0:T(4,128)S(1)}, f32[3,96,4,128]{3,2,1,0:T(4,128)S(1)}, u32[]{:S(2)}, u32[]{:S(2)}) collective-permute-start(f32[3,96,4,128]{3,2,1,0:T(4,128)S(1)} %get-tuple-element.20), channel_id=1, source_target_pairs={{0,16},{1,17},{2,18},{3,19},{4,20},{5,21},{6,22},{7,23},{8,24},{9,... | collective-permute-start | bytes 1769480 | tf_op jit(solution)/shard_map/ppermute | solution.py:330
  35.8 5.4 %collective-permute-start.3 = (f32[96,4,128]{2,1,0:T(4,128)S(1)}, f32[96,4,128]{2,1,0:T(4,128)S(1)}, u32[]{:S(2)}, u32[]{:S(2)}) collective-permute-start(f32[96,4,128]{2,1,0:T(4,128)S(1)} %get-tuple-element.21), channel_id=1, source_target_pairs={{0,112},{1,113},{2,114},{3,115},{4,116},{5,117},{6,118},{7,119},{8... | collective-permute-start | bytes 589832 | tf_op jit(solution)/shard_map/ppermute | solution.py:330
  41.4 7.8 %collective-permute-start.4 = (f32[96,4,128]{2,1,0:T(4,128)S(1)}, f32[96,4,128]{2,1,0:T(4,128)S(1)}, u32[]{:S(2)}, u32[]{:S(2)}) collective-permute-start(f32[96,4,128]{2,1,0:T(4,128)S(1)} %get-tuple-element.23), channel_id=1, source_target_pairs={{0,96},{1,97},{2,98},{3,99},{4,100},{5,101},{6,102},{7,103},{8,104... | collective-permute-start | bytes 589832 | tf_op jit(solution)/shard_map/ppermute | solution.py:330
  45.2 7.5 %collective-permute-start.5 = (f32[96,4,128]{2,1,0:T(4,128)S(1)}, f32[96,4,128]{2,1,0:T(4,128)S(1)}, u32[]{:S(2)}, u32[]{:S(2)}) collective-permute-start(f32[96,4,128]{2,1,0:T(4,128)S(1)} %get-tuple-element.24), channel_id=1, source_target_pairs={{0,32},{1,33},{2,34},{3,35},{4,36},{5,37},{6,38},{7,39},{8,40},{9,... | collective-permute-start | bytes 589832 | tf_op jit(solution)/shard_map/ppermute | solution.py:330
  45.2 16.2 %collective-permute-start.6 = (f32[384,128]{1,0:T(8,128)S(1)}, f32[384,128]{1,0:T(8,128)S(1)}, u32[]{:S(2)}, u32[]{:S(2)}) collective-permute-start(f32[384,128]{1,0:T(8,128)S(1)} %get-tuple-element.25), channel_id=1, source_target_pairs={{0,16},{1,17},{2,18},{3,19},{4,20},{5,21},{6,22},{7,23},{8,24},{9,... | collective-permute-start | bytes 589832 | tf_op jit(solution)/shard_map/ppermute | solution.py:330
  45.2 16.2 %collective-permute-start.7 = (f32[384,128]{1,0:T(8,128)S(1)}, f32[384,128]{1,0:T(8,128)S(1)}, u32[]{:S(2)}, u32[]{:S(2)}) collective-permute-start(f32[384,128]{1,0:T(8,128)S(1)} %get-tuple-element.26), channel_id=1, source_target_pairs={{16,32},{32,16},{48,64},{64,48},{80,96},{96,80},{112,128},{128,112... | collective-permute-start | bytes 589832 | tf_op jit(solution)/shard_map/ppermute | solution.py:382
  53.4 18.5 %all-to-all-start.1 = ((f32[32,3,4,128]{3,2,1,0:T(4,128)}), f32[32,3,4,128]{3,2,1,0:T(4,128)S(1)}, u32[]{:S(2)}, u32[]{:S(2)}) async-start(f32[32,3,4,128]{3,2,1,0:T(4,128)} %bitcast.4), calls=%async_computation.1 | async-start | bytes 393216 | tf_op jit(solution)/shard_map/all_to_all | solution.py:334
  61.3 10.6 %copy-start.2 = (f32[2,1024,128]{2,1,0:T(8,128)S(1)}, f32[2,1024,128]{2,1,0:T(8,128)}, u32[]{:S(2)}) copy-start(f32[2,1024,128]{2,1,0:T(8,128)} %rad_ref.1) | copy-start | bytes 3145732
  61.3 10.6 %copy-start.3 = (f32[8,1024]{1,0:T(8,128)S(1)}, f32[8,1024]{1,0:T(8,128)}, u32[]{:S(2)}) copy-start(f32[8,1024]{1,0:T(8,128)} %phase_ref.3) | copy-start | bytes 98308

commit v4 on v2

--- a/solution.py
+++ b/solution.py
@@ -102,10 +102,17 @@
 
 
 def aggregate_kernel(
-    cur_ref, rad_hbm, phase_ref, out_ref, down_ref, up_ref, rad_ref, sems, unroll=4, groups=(4, 4)
+    cur_hbm, rad_hbm, phase_hbm, out_ref, down_ref, up_ref, cur_ref, rad_ref, phase_ref, sems,
+    unroll=4, groups=(4, 4),
 ):
+    cur_copy = pltpu.make_async_copy(cur_hbm, cur_ref, sems.at[4])
+    phase_copy = pltpu.make_async_copy(phase_hbm, phase_ref, sems.at[5])
+    cur_copy.start()
     for i in range(4):
         radiation_copy(rad_hbm, rad_ref, sems, i).start()
+        if i == 1:
+            phase_copy.start()
+    cur_copy.wait()
     for i in range(2):
         down_ref[pl.ds(i * 96, 96), :] = cur_ref[pl.ds(i * 192 + 96, 96), :]
         up_ref[pl.ds(i * 96, 96), :] = cur_ref[pl.ds(i * 192, 96), :]
@@ -135,6 +142,7 @@
                 out_ref[16 + d, parent] = block[4:]
         return carry
 
+    phase_copy.wait()
     first = 0
     for count in groups:
         for i in range(first // 2, (first + count) // 2):
@@ -276,7 +284,7 @@
         ref[pl.ds(288, 96), :] = up_ref[pl.ds(pl.multiple_of(row * 96, 8), 96), :]
 
 
-def join_kernel(mid_ref, far_ref, back_ref, ahead_ref, beside_ref, away_ref, out_ref):
+def join_kernel(mid_ref, far_ref, back_ref, ahead_ref, out_ref):
     out_ref[...] = (mid_ref[...] + far_ref[...]) + (back_ref[...] + ahead_ref[...])
 
 
@@ -347,8 +355,13 @@
     patterns, down, up = call(
         aggregate_kernel,
         (f32(32, 3, 4, 128), f32(192, 128), f32(192, 128)),
-        [pltpu.VMEM((2, 1024, 128), F32), pltpu.SemaphoreType.DMA((4,))],
-        in_specs=[vmem, hbm, vmem],
+        [
+            pltpu.VMEM((384, 128), F32),
+            pltpu.VMEM((2, 1024, 128), F32),
+            pltpu.VMEM((8, 1024), F32),
+            pltpu.SemaphoreType.DMA((6,)),
+        ],
+        in_specs=[hbm] * 3,
         flops=600_000_000,
         moved=2_000_000,
         vmem_bytes=62 * 1024 * 1024,
@@ -381,12 +394,8 @@
         away, "slab", [(s, s + 2 * (s % 2) - 1) for s in range(16) if 0 <= s + 2 * (s % 2) - 1 < 16]
     )
     incoming = call(
-        join_kernel,
-        f32(96, 4, 128),
-        in_specs=[vmem] * 4 + [hbm] * 2,
-        flops=1_000_000,
-        moved=1_000_000,
-    )(mid, far_in, back_in, ahead_in, beside, away)
+        join_kernel, f32(96, 4, 128), flops=1_000_000, moved=1_000_000
+    )(mid, far_in, back_in, ahead_in)
     returned = spread(incoming.reshape(32, 3, 4, 128), groups)
 
     near = call(

time: 74.6 us -> 69.9 us (0.937)
  the two profiles are of different devices: /device:TPU:32 before, /device:TPU:8 now
where the time goes in v4:
time: 69.9 us; the launch traced here: 69.5 us
  starting transfers between devices  32.5 us (46%)
  Pallas kernels  17.3 us (25%)
  waiting for transfers between devices  17.1 us (24%)
  local copies, waits for them, and re-layouts  2.04 us (3%)
    all_to_all x2, starting transfers between devices, spread(): lax.all_to_all(block, AXES, split_axis=0, concat_axis=0, axis_index_group...  19.5 us
    all_to_all x2, waiting for transfers between devices, spread(): lax.all_to_all(block, AXES, split_axis=0, concat_axis=0, axis_index_group...  8.09 us
    ppermute x5, waiting for transfers between devices, moved_by(): return lax.ppermute(block, AXES, route_of(move))  5.64 us
    pallas_call x1, Pallas kernels, per_device(): call(translate_kernel, (f32(3, 96, 4, 128), f32(3, 96, 4, 128), f32(96, 4...  5.62 us
    pallas_call x1, Pallas kernels, per_device(): call(near_kernel, f32(192, 256), [pltpu.VMEM((27, 2, 128, 128), F32), plt...  5.3 us
    ppermute x5, starting transfers between devices, moved_by(): return lax.ppermute(block, AXES, route_of(move))  4.62 us
    ppermute x1, starting transfers between devices, per_device(): down = lax.ppermute(down, 'dir', [(d, d + 1) for d in range(15)])  3.7 us
    pallas_call x1, Pallas kernels, per_device(): call(aggregate_kernel, (f32(32, 3, 4, 128), f32(192, 128), f32(192, 128))...  3.58 us
  transfers between devices with their start and end apart: 10, of which 6 were waited for; matrix products, arithmetic and copies ran while one was open for 3% of the time, Pallas kernels for 9%

profile of v4, /device:TPU:8, one launch (start us, length us, event | category | flops | bytes accessed | tf_op | source)
XLA Modules:
  0.0 69.5 jit_solution(1113405250208726601)
XLA Ops:
  0.0 0.0 copy-start
  0.0 3.6 %shard_map.73 = (f32[32,3,4,128]{3,2,1,0:T(4,128)}, f32[192,128]{1,0:T(8,128)}, f32[192,128]{1,0:T(8,128)}) custom-call(f32[384,128]{1,0:T(8,128)} %bitcast.8, f32[2,1024,128]{2,1,0:T(8,128)} %rad_ref.1, f32[8,1024]{1,0:T(8,128)} %phase_ref.1), custom_call_target="tpu_custom_call" | custom-call | flops 600000000 | bytes 2000000 | tf_op jit(solution)/shard_map/pallas_call | solution.py:355
  3.6 11.3 %all-to-all-start = ((f32[32,3,4,128]{3,2,1,0:T(4,128)}), f32[32,3,4,128]{3,2,1,0:T(4,128)S(1)}, u32[]{:S(2)}, u32[]{:S(2)}) async-start(f32[32,3,4,128]{3,2,1,0:T(4,128)} %get-tuple-element.16), calls=%async_computation | async-start | bytes 393216 | tf_op jit(solution)/shard_map/all_to_all | solution.py:340
  14.9 3.7 %collective-permute-start = (f32[192,128]{1,0:T(8,128)}, f32[192,128]{1,0:T(8,128)S(1)}, u32[]{:S(2)}, u32[]{:S(2)}) collective-permute-start(f32[192,128]{1,0:T(8,128)} %get-tuple-element.17), channel_id=1, source_target_pairs={{0,1},{1,2},{2,3},{3,4},{4,5},{5,6},{6,7},{7,8},{8,9},{9,10},{10,1... | collective-permute-start | bytes 294920 | tf_op jit(solution)/shard_map/ppermute | solution.py:370
  18.6 1.3 %collective-permute-start.1 = (f32[192,128]{1,0:T(8,128)}, f32[192,128]{1,0:T(8,128)S(1)}, u32[]{:S(2)}, u32[]{:S(2)}) collective-permute-start(f32[192,128]{1,0:T(8,128)} %get-tuple-element.18), channel_id=1, source_target_pairs={{1,0},{2,1},{3,2},{4,3},{5,4},{6,5},{7,6},{8,7},{9,8},{10,9},{11,1... | collective-permute-start | bytes 294920 | tf_op jit(solution)/shard_map/ppermute | solution.py:371
  20.0 0.9 %constant_dynamic-slice_fusion.2 = (s32[48,16]{0,1:T(8,128)S(1)}, s32[48,16]{0,1:T(8,128)S(1)}, s32[48,16]{0,1:T(8,128)S(1)}, s32[48,16]{0,1:T(8,128)S(1)}) fusion(s32[768,16]{0,1:T(8,128)} %param.13, s32[]{:T(128)S(6)} %select_n.86, s32[]{:T(128)S(6)} %select_n.87, s32[768,16]{0,1:T(8,128)} %param.12), kind=kLoop, calls=%fused_computation.43 | loop fusion | bytes 24584 | tf_op jit(solution)/shard_map/dynamic_slice | solution.py:314
  20.8 0.1 add_multiply_fusion
  20.9 0.1 broadcast_divide_fusion
  21.0 0.0 copy-done
  21.0 0.1 sign_compare_fusion.2
  21.1 0.1 copy.9
  21.2 0.1 ne.103
  21.3 0.1 copy.11
  21.4 0.1 div.42
  21.5 0.1 copy.12
  21.6 0.1 mul.41.kinds_ref
  21.7 0.1 copy.10
  21.8 0.1 rem.141
  21.8 0.1 fusion.9.slots_ref
  21.9 0.2 copy.13
  22.1 0.0 collective-permute-done.down_ref
  22.1 3.3 %collective-permute-done.1.up_ref = f32[192,128]{1,0:T(8,128)S(1)} collective-permute-done((f32[192,128]{1,0:T(8,128)}, f32[192,128]{1,0:T(8,128)S(1)}, u32[]{:S(2)}, u32[]{:S(2)}) %collective-permute-start.1) | collective-permute-done | bytes 98336 | tf_op jit(solution)/shard_map/ppermute | solution.py:371
  25.5 2.0 %all-to-all-done = f32[32,3,4,128]{3,2,1,0:T(4,128)S(1)} async-done(((f32[32,3,4,128]{3,2,1,0:T(4,128)}), f32[32,3,4,128]{3,2,1,0:T(4,128)S(1)}, u32[]{:S(2)}, u32[]{:S(2)}) %all-to-all-start) | async-done | bytes 196640 | tf_op jit(solution)/shard_map/all_to_all | solution.py:340
  27.5 0.2 broadcast_in_dim.15
  27.8 5.6 %shard_map.74 = (f32[3,96,4,128]{3,2,1,0:T(4,128)S(1)}, f32[3,96,4,128]{3,2,1,0:T(4,128)S(1)}, f32[96,4,128]{2,1,0:T(4,128)S(1)}) custom-call(s32[1536]{0:T(1024)S(1)} %fusion.9.slots_ref, s32[1536]{0:T(1024)S(1)} %mul.41.kinds_ref, f32[2528,128]{1,0:T(8,128)S(1)} %bitcast.6, f32[96,4,128]{2,1,0:T(4,128)S(1)} %bitcast.7, ...), custom_call_target="tpu_custom_call" | custom-call | flops 100000000 | bytes 3000000 | tf_op jit(solution)/shard_map/pallas_call | solution.py:373
  33.4 0.1 collective-permute-start.2
  33.5 2.4 %collective-permute-start.3 = (f32[96,4,128]{2,1,0:T(4,128)S(1)}, f32[96,4,128]{2,1,0:T(4,128)S(1)}, u32[]{:S(2)}, u32[]{:S(2)}) collective-permute-start(f32[96,4,128]{2,1,0:T(4,128)S(1)} %get-tuple-element.22), channel_id=1, source_target_pairs={{0,80},{1,81},{2,82},{3,83},{4,84},{5,85},{6,86},{7,87},{8,88},{9,... | collective-permute-start | bytes 589832 | tf_op jit(solution)/shard_map/ppermute | solution.py:336
  35.9 0.0 collective-permute-done.2.got_ref
  35.9 0.0 copy-done.1
  35.9 0.2 shard_map.75
  36.1 1.4 %collective-permute-start.4 = (f32[96,4,128]{2,1,0:T(4,128)S(1)}, f32[96,4,128]{2,1,0:T(4,128)S(1)}, u32[]{:S(2)}, u32[]{:S(2)}) collective-permute-start(f32[96,4,128]{2,1,0:T(4,128)S(1)} %get-tuple-element.23), channel_id=1, source_target_pairs={{0,96},{1,97},{2,98},{3,99},{4,100},{5,101},{6,102},{7,103},{8,104... | collective-permute-start | bytes 589832 | tf_op jit(solution)/shard_map/ppermute | solution.py:336
  37.5 0.7 collective-permute-start.5
  38.2 0.0 collective-permute-start.6
  38.2 3.4 %collective-permute-start.7 = (f32[384,128]{1,0:T(8,128)S(1)}, f32[384,128]{1,0:T(8,128)S(1)}, u32[]{:S(2)}, u32[]{:S(2)}) collective-permute-start(f32[384,128]{1,0:T(8,128)S(1)} %get-tuple-element.26), channel_id=1, source_target_pairs={{16,32},{32,16},{48,64},{64,48},{80,96},{96,80},{112,128},{128,112... | collective-permute-start | bytes 589832 | tf_op jit(solution)/shard_map/ppermute | solution.py:393
  41.6 0.3 collective-permute-done.3.far_ref
  41.8 4.7 %collective-permute-done.4.back_ref = f32[96,4,128]{2,1,0:T(4,128)S(1)} collective-permute-done((f32[96,4,128]{2,1,0:T(4,128)S(1)}, f32[96,4,128]{2,1,0:T(4,128)S(1)}, u32[]{:S(2)}, u32[]{:S(2)}) %collective-permute-start.4) | collective-permute-done | bytes 196640 | tf_op jit(solution)/shard_map/ppermute | solution.py:336
  46.5 0.7 %collective-permute-done.5.ahead_ref = f32[96,4,128]{2,1,0:T(4,128)S(1)} collective-permute-done((f32[96,4,128]{2,1,0:T(4,128)S(1)}, f32[96,4,128]{2,1,0:T(4,128)S(1)}, u32[]{:S(2)}, u32[]{:S(2)}) %collective-permute-start.5) | collective-permute-done | bytes 196640 | tf_op jit(solution)/shard_map/ppermute | solution.py:336
  47.2 0.8 %shard_map.76 = f32[96,4,128]{2,1,0:T(4,128)} custom-call(f32[96,4,128]{2,1,0:T(4,128)S(1)} %get-tuple-element.21.mid_ref, f32[96,4,128]{2,1,0:T(4,128)S(1)} %collective-permute-done.3.far_ref, f32[96,4,128]{2,1,0:T(4,128)S(1)} %collective-permute-done.4.back_ref, f32[96,4,128]{2,1,0:T(4,128)S(1)} %collective-permute-done.5.ahead_ref), custom_call_target="tpu_custom_call" | custom-call | flops 1000000 | bytes 1000000 | tf_op jit(solution)/shard_map/pallas_call | solution.py:396
  48.0 8.2 %all-to-all-start.1 = ((f32[32,3,4,128]{3,2,1,0:T(4,128)}), f32[32,3,4,128]{3,2,1,0:T(4,128)S(1)}, u32[]{:S(2)}, u32[]{:S(2)}) async-start(f32[32,3,4,128]{3,2,1,0:T(4,128)} %bitcast.4), calls=%async_computation.1 | async-start | bytes 393216 | tf_op jit(solution)/shard_map/all_to_all | solution.py:340
  56.2 0.0 copy-start.2
  56.2 0.0 copy-start.3
  56.2 0.0 collective-permute-done.6.beside_ref
  56.2 0.0 collective-permute-done.7.away_ref
  56.2 5.3 %shard_map.77.near_ref = f32[192,256]{1,0:T(8,128)S(1)} custom-call(s32[1]{0:T(128)} %bitcast.core_ref, f32[384,128]{1,0:T(8,128)S(1)} %bitcast.10, f32[384,128]{1,0:T(8,128)S(1)} %collective-permute-done.6.beside_ref, f32[384,128]{1,0:T(8,128)S(1)} %collective-permute-done.7.away_ref, f32[192,128]{1,0:T(8,128)S(1)} %collective-permute-done.down_ref, ...), custom_call_target="tpu_custom_call" | custom-call | flops 2000000000 | bytes 5000000 | tf_op jit(solution)/shard_map/pallas_call | solution.py:401
  61.5 6.0 %all-to-all-done.1.in_ref = f32[32,3,4,128]{3,2,1,0:T(4,128)S(1)} async-done(((f32[32,3,4,128]{3,2,1,0:T(4,128)}), f32[32,3,4,128]{3,2,1,0:T(4,128)S(1)}, u32[]{:S(2)}, u32[]{:S(2)}) %all-to-all-start.1) | async-done | bytes 196640 | tf_op jit(solution)/shard_map/all_to_all | solution.py:340
  67.6 0.0 copy-done.2
  67.6 0.0 copy-done.3
  67.6 1.9 %shard_map.78 = f32[384,128]{1,0:T(8,128)} custom-call(f32[32,3,4,128]{3,2,1,0:T(4,128)S(1)} %all-to-all-done.1.in_ref, f32[2,1024,128]{2,1,0:T(8,128)S(1)} %copy-done.2, f32[8,1024]{1,0:T(8,128)S(1)} %copy-done.3, f32[192,256]{1,0:T(8,128)S(1)} %shard_map.77.near_ref), custom_call_target="tpu_custom_call" | custom-call | flops 600000000 | bytes 2000000 | tf_op jit(solution)/shard_map/pallas_call | solution.py:417
  (3 shorter events, 0.0 us)
Async XLA Ops:
  0.0 21.0 %copy-start = (f32[316,2,64]{0,2,1:T(8,128)S(1)}, f32[316,2,64]{0,2,1:T(8,128)}, u32[]{:S(2)}) copy-start(f32[316,2,64]{0,2,1:T(8,128)} %param.11) | copy-start | bytes 485380
  0.0 35.9 %copy-start.1 = (f32[2,2,6,8,2,128]{5,4,3,2,1,0:T(2,128)S(1)}, f32[2,2,6,8,2,128]{5,4,3,2,1,0:T(2,128)}, u32[]{:S(2)}) copy-start(f32[2,2,6,8,2,128]{5,4,3,2,1,0:T(2,128)} %param.7) | copy-start | bytes 589828
  3.6 23.9 %all-to-all-start = ((f32[32,3,4,128]{3,2,1,0:T(4,128)}), f32[32,3,4,128]{3,2,1,0:T(4,128)S(1)}, u32[]{:S(2)}, u32[]{:S(2)}) async-start(f32[32,3,4,128]{3,2,1,0:T(4,128)} %get-tuple-element.16), calls=%async_computation | async-start | bytes 393216 | tf_op jit(solution)/shard_map/all_to_all | solution.py:340
  14.9 7.2 %collective-permute-start = (f32[192,128]{1,0:T(8,128)}, f32[192,128]{1,0:T(8,128)S(1)}, u32[]{:S(2)}, u32[]{:S(2)}) collective-permute-start(f32[192,128]{1,0:T(8,128)} %get-tuple-element.17), channel_id=1, source_target_pairs={{0,1},{1,2},{2,3},{3,4},{4,5},{5,6},{6,7},{7,8},{8,9},{9,10},{10,1... | collective-permute-start | bytes 294920 | tf_op jit(solution)/shard_map/ppermute | solution.py:370
  18.6 6.9 %collective-permute-start.1 = (f32[192,128]{1,0:T(8,128)}, f32[192,128]{1,0:T(8,128)S(1)}, u32[]{:S(2)}, u32[]{:S(2)}) collective-permute-start(f32[192,128]{1,0:T(8,128)} %get-tuple-element.18), channel_id=1, source_target_pairs={{1,0},{2,1},{3,2},{4,3},{5,4},{6,5},{7,6},{8,7},{9,8},{10,9},{11,1... | collective-permute-start | bytes 294920 | tf_op jit(solution)/shard_map/ppermute | solution.py:371
  33.4 2.5 %collective-permute-start.2 = (f32[3,96,4,128]{3,2,1,0:T(4,128)S(1)}, f32[3,96,4,128]{3,2,1,0:T(4,128)S(1)}, u32[]{:S(2)}, u32[]{:S(2)}) collective-permute-start(f32[3,96,4,128]{3,2,1,0:T(4,128)S(1)} %get-tuple-element.20), channel_id=1, source_target_pairs={{0,16},{1,17},{2,18},{3,19},{4,20},{5,21},{6,22},{7,23},{8,24},{9,... | collective-permute-start | bytes 1769480 | tf_op jit(solution)/shard_map/ppermute | solution.py:336
  33.5 8.3 %collective-permute-start.3 = (f32[96,4,128]{2,1,0:T(4,128)S(1)}, f32[96,4,128]{2,1,0:T(4,128)S(1)}, u32[]{:S(2)}, u32[]{:S(2)}) collective-permute-start(f32[96,4,128]{2,1,0:T(4,128)S(1)} %get-tuple-element.22), channel_id=1, source_target_pairs={{0,80},{1,81},{2,82},{3,83},{4,84},{5,85},{6,86},{7,87},{8,88},{9,... | collective-permute-start | bytes 589832 | tf_op jit(solution)/shard_map/ppermute | solution.py:336
  36.1 10.4 %collective-permute-start.4 = (f32[96,4,128]{2,1,0:T(4,128)S(1)}, f32[96,4,128]{2,1,0:T(4,128)S(1)}, u32[]{:S(2)}, u32[]{:S(2)}) collective-permute-start(f32[96,4,128]{2,1,0:T(4,128)S(1)} %get-tuple-element.23), channel_id=1, source_target_pairs={{0,96},{1,97},{2,98},{3,99},{4,100},{5,101},{6,102},{7,103},{8,104... | collective-permute-start | bytes 589832 | tf_op jit(solution)/shard_map/ppermute | solution.py:336
  37.5 9.7 %collective-permute-start.5 = (f32[96,4,128]{2,1,0:T(4,128)S(1)}, f32[96,4,128]{2,1,0:T(4,128)S(1)}, u32[]{:S(2)}, u32[]{:S(2)}) collective-permute-start(f32[96,4,128]{2,1,0:T(4,128)S(1)} %get-tuple-element.24), channel_id=1, source_target_pairs={{0,32},{1,33},{2,34},{3,35},{4,36},{5,37},{6,38},{7,39},{8,40},{9,... | collective-permute-start | bytes 589832 | tf_op jit(solution)/shard_map/ppermute | solution.py:336
  38.2 18.0 %collective-permute-start.6 = (f32[384,128]{1,0:T(8,128)S(1)}, f32[384,128]{1,0:T(8,128)S(1)}, u32[]{:S(2)}, u32[]{:S(2)}) collective-permute-start(f32[384,128]{1,0:T(8,128)S(1)} %get-tuple-element.25), channel_id=1, source_target_pairs={{0,16},{1,17},{2,18},{3,19},{4,20},{5,21},{6,22},{7,23},{8,24},{9,... | collective-permute-start | bytes 589832 | tf_op jit(solution)/shard_map/ppermute | solution.py:336
  38.2 18.0 %collective-permute-start.7 = (f32[384,128]{1,0:T(8,128)S(1)}, f32[384,128]{1,0:T(8,128)S(1)}, u32[]{:S(2)}, u32[]{:S(2)}) collective-permute-start(f32[384,128]{1,0:T(8,128)S(1)} %get-tuple-element.26), channel_id=1, source_target_pairs={{16,32},{32,16},{48,64},{64,48},{80,96},{96,80},{112,128},{128,112... | collective-permute-start | bytes 589832 | tf_op jit(solution)/shard_map/ppermute | solution.py:393
  48.0 19.6 %all-to-all-start.1 = ((f32[32,3,4,128]{3,2,1,0:T(4,128)}), f32[32,3,4,128]{3,2,1,0:T(4,128)S(1)}, u32[]{:S(2)}, u32[]{:S(2)}) async-start(f32[32,3,4,128]{3,2,1,0:T(4,128)} %bitcast.4), calls=%async_computation.1 | async-start | bytes 393216 | tf_op jit(solution)/shard_map/all_to_all | solution.py:340
  56.2 11.4 %copy-start.2 = (f32[2,1024,128]{2,1,0:T(8,128)S(1)}, f32[2,1024,128]{2,1,0:T(8,128)}, u32[]{:S(2)}) copy-start(f32[2,1024,128]{2,1,0:T(8,128)} %rad_ref.1) | copy-start | bytes 3145732
  56.2 11.4 %copy-start.3 = (f32[8,1024]{1,0:T(8,128)S(1)}, f32[8,1024]{1,0:T(8,128)}, u32[]{:S(2)}) copy-start(f32[8,1024]{1,0:T(8,128)} %phase_ref.1) | copy-start | bytes 98308

commit v5 on v4

--- a/solution.py
+++ b/solution.py
@@ -102,7 +102,7 @@
 
 
 def aggregate_kernel(
-    cur_hbm, rad_hbm, phase_hbm, out_ref, down_ref, up_ref, cur_ref, rad_ref, phase_ref, sems,
+    core_ref, cur_hbm, rad_hbm, phase_hbm, out_ref, lent_ref, cur_ref, rad_ref, phase_ref, sems,
     unroll=4, groups=(4, 4),
 ):
     cur_copy = pltpu.make_async_copy(cur_hbm, cur_ref, sems.at[4])
@@ -114,8 +114,8 @@
             phase_copy.start()
     cur_copy.wait()
     for i in range(2):
-        down_ref[pl.ds(i * 96, 96), :] = cur_ref[pl.ds(i * 192 + 96, 96), :]
-        up_ref[pl.ds(i * 96, 96), :] = cur_ref[pl.ds(i * 192, 96), :]
+        first = pl.multiple_of(i * 192 + core_ref[0] * 96, 8)
+        lent_ref[pl.ds(i * 96, 96), :] = cur_ref[pl.ds(first, 96), :]
     rows = cur_ref.shape[0] // 2
     x = jnp.concatenate(
         [cur_ref[pl.ds(0, rows, stride=2), :], cur_ref[pl.ds(1, rows, stride=2), :]], axis=1
@@ -184,18 +184,21 @@
 
 
 def near_kernel(
-    core_ref, own_ref, beside_ref, away_ref, down_ref, up_ref, tiles_hbm,
+    core_ref, own_ref, side_ref, cross_ref, away_ref, tiles_hbm,
     out_ref, tiles_ref, hi_ref, lo_ref, acc_ref, sems,
 ):
     for i in range(3):
         tiles_copy(tiles_hbm, tiles_ref, sems, i).start()
-    to_beside = jnp.where(core_ref[0] == 0, 3, 0)
-    to_away = 3 - to_beside
-
-    def put(ref, at_row, to_x, to_y):
+    core = core_ref[0]
+    to_beside = 3 - 3 * core
+    to_away = 3 * core
+    side_y = 3 * core
+    cross_y = 3 - 3 * core
+
+    def put(ref, first, to_x, to_y):
+        first = pl.multiple_of(first, 8)
         x = jnp.concatenate(
-            [ref[pl.ds(at_row * 96, 48, stride=2), :], ref[pl.ds(at_row * 96 + 1, 48, stride=2), :]],
-            axis=1,
+            [ref[pl.ds(first, 48, stride=2), :], ref[pl.ds(first + 1, 48, stride=2), :]], axis=1
         )
         hi, lo = split(x)
         hi_ref[to_x, to_y] = hi
@@ -203,12 +206,14 @@
 
     for i in range(2):
         for j in range(2):
-            put(own_ref, i * 2 + j, 1 + i, 1 + j)
-        put(down_ref, i, 1 + i, 0)
-        put(up_ref, i, 1 + i, 3)
+            put(own_ref, (i * 2 + j) * 96, 1 + i, 1 + j)
+        put(side_ref, i * 96, 1 + i, side_y)
+        put(cross_ref, i * 96, 1 + i, cross_y)
+        put(cross_ref, 288 + i * 96, to_beside, 1 + i)
+    put(side_ref, 192 + core * 96, to_beside, side_y)
+    put(cross_ref, 192, to_beside, cross_y)
     for i, to_y in enumerate((1, 2, 0, 3)):
-        put(beside_ref, i, to_beside, to_y)
-        put(away_ref, i, to_away, to_y)
+        put(away_ref, i * 96, to_away, to_y)
     acc_ref[...] = jnp.zeros_like(acc_ref)
 
     @pl.loop(0, 3)
@@ -235,7 +240,7 @@
 
 
 def translate_kernel(
-    slots_ref, kinds_ref, table_ref, src_ref, down_ref, up_ref,
+    slots_ref, kinds_ref, table_ref, src_ref, side_ref,
     keep_ref, swap_ref, far_ref, acc_ref,
 ):
     acc_ref[...] = jnp.zeros_like(acc_ref)
@@ -250,9 +255,9 @@
         both = jnp.where(row < 4, both, times_i(both))
         slots, sums = [], []
         for f in range(16):
-            slot = slots_ref[s * 16 + f]
+            slot = slots_ref[f, s]
             slots.append(slot)
-            kind = kinds_ref[s * 16 + f]
+            kind = kinds_ref[f, s]
             sums.append(acc_ref[tile(slot), :] + table_ref[tile(kind), :] * both)
         for f in range(16):
             acc_ref[tile(slots[f]), :] = sums[f]
@@ -270,18 +275,60 @@
     far_ref[...] = folded(6)
 
 
+def pair_kernel(core_ref, cur_ref, got_ref, out_ref):
+    j = 1 - core_ref[0]
+    for i in range(2):
+        first = pl.multiple_of(i * 192 + j * 96, 8)
+        out_ref[pl.ds(i * 96, 96), :] = cur_ref[pl.ds(first, 96), :]
+    out_ref[pl.ds(192, 192), :] = got_ref[...]
+
+
+def lists_kernel(slab_ref, targets_ref, kinds_ref, tr_ref, order_ref, slots_ref, rows_ref, table_ref):
+    slab = slab_ref[0]
+    ring, z_hi = slab & 7, slab >> 3
+    y, core = ring >> 1, ring & 1
+    lane = lax.broadcasted_iota(jnp.int32, (16, 128), 1)
+
+    def own(ref):
+        low = pltpu.roll(ref[...], (16 - ring) * 48, 1)
+        high = pltpu.roll(ref[...], (9 - ring) * 48, 1)
+        return jnp.where(lane < 48, low[:, :128], high[:, :128])
+
+    target = own(targets_ref)
+    to_slab = (target * 683) >> 15
+    to_ring = to_slab & 7
+    step = ((to_ring >> 1) - y + 4) & 3
+    near_block = ((step + 1) & 3) + jnp.where((to_ring & 1) == core, 0, 3)
+    block = jnp.where(step == 2, 6, near_block)
+    slots_ref[...] = (block * 96 + (to_slab >> 3) * 48 + (target - to_slab * 48)) * 8
+    rows_ref[...] = own(kinds_ref) * 8
+
+    def part(c):
+        half = tr_ref[c, pl.ds(pl.multiple_of(z_hi * 32, 32), 32), :]
+        lanes = jnp.concatenate([half] * 4, axis=0).T
+        return jnp.broadcast_to(lanes[:, None, :], (lanes.shape[0], 4, 128))
+
+    table_ref[...] = jnp.concatenate([part(0), part(1)], axis=1)
+
+
 def fold_kernel(
-    core_ref, keep_ref, got_ref, cur_ref, down_ref, up_ref,
-    back_ref, mid_ref, ahead_ref, beside_ref, away_ref,
+    core_ref, keep_ref, got_ref, cur_ref, side_ref, back_ref, mid_ref, ahead_ref, cross_ref
 ):
     back_ref[...] = keep_ref[0] + got_ref[0]
     mid_ref[...] = keep_ref[1] + got_ref[1]
     ahead_ref[...] = keep_ref[2] + got_ref[2]
+    row = 1 - core_ref[0]
+    cross_ref[pl.ds(0, 192), :] = side_ref[pl.ds(192, 192), :]
+    cross_ref[pl.ds(192, 96), :] = side_ref[pl.ds(pl.multiple_of(row * 96, 8), 96), :]
+    cross_ref[pl.ds(288, 192), :] = cur_ref[pl.ds(pl.multiple_of(row * 192, 8), 192), :]
+
+
+def away_kernel(core_ref, cur_ref, side_ref, cross_ref, far_ref, out_ref):
     core = core_ref[0]
-    for ref, row in ((beside_ref, 1 - core), (away_ref, core)):
-        ref[pl.ds(0, 192), :] = cur_ref[pl.ds(pl.multiple_of(row * 192, 8), 192), :]
-        ref[pl.ds(192, 96), :] = down_ref[pl.ds(pl.multiple_of(row * 96, 8), 96), :]
-        ref[pl.ds(288, 96), :] = up_ref[pl.ds(pl.multiple_of(row * 96, 8), 96), :]
+    first = pl.multiple_of(core * 96, 8)
+    out_ref[pl.ds(0, 192), :] = cur_ref[pl.ds(pl.multiple_of(core * 192, 8), 192), :]
+    out_ref[pl.ds(pl.multiple_of(192 + core * 96, 8), 96), :] = side_ref[pl.ds(first, 96), :]
+    out_ref[pl.ds(pl.multiple_of(288 - core * 96, 8), 96), :] = cross_ref[pl.ds(first, 96), :]
 
 
 def join_kernel(mid_ref, far_ref, back_ref, ahead_ref, out_ref):
@@ -304,34 +351,6 @@
     return jax.ShapeDtypeStruct(shape, F32)
 
 
-def pair_words(far_targets, far_offsets):
-    slab = lax.axis_index("slab")
-    ring = slab % 8
-    y, core = ring // 2, ring % 2
-
-    def own(table):
-        return jnp.concatenate(
-            [lax.dynamic_slice_in_dim(table, (ring + z_hi * 8) * 48, 48, 0) for z_hi in range(2)]
-        )
-
-    targets, kinds = own(far_targets), own(far_offsets)
-    to_slab, row = targets // 48, targets % 48
-    half, to_ring = to_slab // 8, to_slab % 8
-    step = (to_ring // 2 - y + 4) % 4
-    near_block = (step + 1) % 4 + jnp.where(to_ring % 2 == core, 0, 3)
-    block = jnp.where(step == 2, 6, near_block)
-    slot = block * 96 + half * 48 + row
-    return (slot * 8).reshape(-1), (kinds * 8).reshape(-1)
-
-
-def operator_table(translators):
-    count = translators.shape[0]
-    half = lax.axis_index("slab") // 8
-    own = lax.dynamic_slice_in_dim(translators, half * 32, 32, 2)
-    lanes = jnp.concatenate([own] * 4, axis=2)
-    return jnp.broadcast_to(lanes[:, :, None, :], (count, 2, 4, 128)).reshape(count * 8, 128)
-
-
 def moved_by(block, move):
     return lax.ppermute(block, AXES, route_of(move))
 
@@ -345,56 +364,79 @@
 def per_device(currents, near_tiles, radiation, child_phase, translators, far_targets, far_offsets):
     groups = exchange_groups()
     rows = currents.reshape(384, 128)
-    core = (lax.axis_index("slab") % 2).astype(jnp.int32).reshape(1)
-    slots, kinds = pair_words(far_targets, far_offsets)
-    table = operator_table(translators)
+    slab = lax.axis_index("slab").astype(jnp.int32).reshape(1)
+    core = slab & 1
     vmem = pl.BlockSpec(memory_space=pltpu.VMEM)
     smem = pl.BlockSpec(memory_space=pltpu.SMEM)
     hbm = pl.BlockSpec(memory_space=pl.ANY)
 
-    patterns, down, up = call(
+    patterns, lent = call(
         aggregate_kernel,
-        (f32(32, 3, 4, 128), f32(192, 128), f32(192, 128)),
+        (f32(32, 3, 4, 128), f32(192, 128)),
         [
             pltpu.VMEM((384, 128), F32),
             pltpu.VMEM((2, 1024, 128), F32),
             pltpu.VMEM((8, 1024), F32),
             pltpu.SemaphoreType.DMA((6,)),
         ],
-        in_specs=[hbm] * 3,
+        in_specs=[smem] + [hbm] * 3,
         flops=600_000_000,
         moved=2_000_000,
         vmem_bytes=62 * 1024 * 1024,
-    )(rows, radiation, child_phase)
+    )(core, rows, radiation, child_phase)
     moved = spread(patterns, groups)
-    down = lax.ppermute(down, "dir", [(d, d + 1) for d in range(15)])
-    up = lax.ppermute(up, "dir", [(d + 1, d) for d in range(15)])
+    got = moved_by(lent, lambda z_hi, y, core, d: (z_hi, y, 1 - core, d))
+    side = call(
+        pair_kernel, f32(384, 128), in_specs=[smem, vmem, vmem], flops=1000, moved=400_000
+    )(core, rows, got)
+    count = translators.shape[0]
+    lists = jax.ShapeDtypeStruct((16, 128), jnp.int32)
+    slots, kinds, table = call(
+        lists_kernel,
+        (lists, lists, f32(count, 8, 128)),
+        in_specs=[smem] + [vmem] * 3 + [hbm],
+        flops=1_000_000,
+        moved=2_000_000,
+    )(slab, far_targets.T, far_offsets.T, translators.transpose(1, 2, 0), side)
+    table = table.reshape(count * 8, 128)
+    side = moved_by(
+        side,
+        lambda z_hi, y, core, d: (z_hi, y, core, d + 1 - 2 * core)
+        if 0 <= d + 1 - 2 * core < 16
+        else None,
+    )
 
     keep, swap, far = call(
         translate_kernel,
         (f32(3, 96, 4, 128), f32(3, 96, 4, 128), f32(96, 4, 128)),
         [pltpu.VMEM((5376, 128), F32)],
-        in_specs=[smem, smem, vmem, vmem, hbm, hbm],
+        in_specs=[smem, smem, vmem, vmem, hbm],
         flops=100_000_000,
         moved=3_000_000,
-    )(slots, kinds, table, moved.reshape(96, 4, 128), down, up)
+    )(slots, kinds, table, moved.reshape(96, 4, 128), side)
     far_in = moved_by(far, lambda z_hi, y, core, d: (z_hi, (y + 2) % 4, 1 - core, d))
     swap_in = moved_by(swap, lambda z_hi, y, core, d: (z_hi, y, 1 - core, d))
-    back, mid, ahead, beside, away = call(
+    back, mid, ahead, cross = call(
         fold_kernel,
-        (f32(96, 4, 128),) * 3 + (f32(384, 128),) * 2,
-        in_specs=[smem] + [vmem] * 5,
+        (f32(96, 4, 128),) * 3 + (f32(480, 128),),
+        in_specs=[smem] + [vmem] * 4,
         flops=1_000_000,
         moved=2_000_000,
-    )(core, keep, swap_in, rows, down, up)
+    )(core, keep, swap_in, rows, side)
     back_in = moved_by(back, lambda z_hi, y, core, d: (z_hi, (y + 3) % 4, core, d))
     ahead_in = moved_by(ahead, lambda z_hi, y, core, d: (z_hi, (y + 1) % 4, core, d))
-    beside = moved_by(beside, lambda z_hi, y, core, d: (z_hi, y, 1 - core, d))
+    cross = moved_by(cross, lambda z_hi, y, core, d: (z_hi, y, 1 - core, d))
+    payload = call(
+        away_kernel, f32(384, 128), in_specs=[smem] + [vmem] * 3 + [hbm], flops=1000, moved=400_000
+    )(core, rows, side, cross, far_in)
     away = lax.ppermute(
-        away, "slab", [(s, s + 2 * (s % 2) - 1) for s in range(16) if 0 <= s + 2 * (s % 2) - 1 < 16]
+        payload, "slab", [(s, s + 2 * (s % 2) - 1) for s in range(16) if 0 <= s + 2 * (s % 2) - 1 < 16]
     )
     incoming = call(
-        join_kernel, f32(96, 4, 128), flops=1_000_000, moved=1_000_000
+        join_kernel,
+        f32(96, 4, 128),
+        flops=1_000_000,
+        moved=1_000_000,
     )(mid, far_in, back_in, ahead_in)
     returned = spread(incoming.reshape(32, 3, 4, 128), groups)
 
@@ -408,11 +450,11 @@
             pltpu.VMEM((4, 48, 256), F32),
             pltpu.SemaphoreType.DMA((3,)),
         ],
-        in_specs=[smem] + [vmem] * 5 + [hbm],
+        in_specs=[smem] + [vmem] * 4 + [hbm],
         flops=2_000_000_000,
         moved=5_000_000,
         vmem_bytes=50 * 1024 * 1024,
-    )(core, rows, beside, away, down, up, near_tiles)
+    )(core, rows, side, cross, away, near_tiles)
 
     applied = call(
         disaggregate_kernel,

time: 69.9 us -> 72.1 us (1.031)
  local copies, waits for them, and re-layouts: 2.04 us -> 3.46 us
  waiting for transfers between devices: 17.1 us -> 18.5 us
  starting transfers between devices: 32.5 us -> 31.2 us
  Pallas kernels: 17.3 us -> 18.3 us
    ppermute x3 -> x1, starting transfers between devices: 8.35 us -> 2.63 us  [per_device(): lax.ppermute(payload, 'slab', [(s, s + 2 * (s % 2) - 1) for s in range(16...]
    ppermute x5 -> x7, waiting for transfers between devices: 5.64 us -> 9.96 us  [moved_by(): return lax.ppermute(block, AXES, route_of(move))]
    ppermute x5 -> x7, starting transfers between devices: 4.62 us -> 8.41 us  [moved_by(): return lax.ppermute(block, AXES, route_of(move))]
    unnamed x8 -> x14, local copies, waits for them, and re-layouts: 0.02 us -> 3.46 us
    ppermute x3 -> x1, waiting for transfers between devices: 3.34 us -> 0.01 us  [per_device(): lax.ppermute(payload, 'slab', [(s, s + 2 * (s % 2) - 1) for s in range(16...]
    dynamic_slice x2 -> x0, local copies, waits for them, and re-layouts: 0.87 us -> none  [the longest x1 0.85 us: own(): lax.dynamic_slice_in_dim(table, (ring + z_hi * 8) * 48, 48, 0)]
    pallas_call x2 -> x5, Pallas kernels: 3.76 us -> 4.17 us  [the longest x1 3.56 us: per_device(): call(aggregate_kernel, (f32(32, 3, 4, 128), f32(192, 128)), [pltpu.VMEM((...]
  transfers between devices with their start and end apart: 10 -> 10, of which waited for: 6 -> 8; matrix products, arithmetic and copies ran while one was open for 3% -> 0% of each run, Pallas kernels for 9% -> 9%
where the time goes in v5:
time: 72.1 us; the launch traced here: 71.6 us
  starting transfers between devices  31.2 us (43%)
  waiting for transfers between devices  18.5 us (26%)
  Pallas kernels  18.3 us (25%)
  local copies, waits for them, and re-layouts  3.46 us (5%)
    all_to_all x2, starting transfers between devices, spread(): lax.all_to_all(block, AXES, split_axis=0, concat_axis=0, axis_index_group...  20.2 us
    ppermute x7, waiting for transfers between devices, moved_by(): return lax.ppermute(block, AXES, route_of(move))  9.96 us
    all_to_all x2, waiting for transfers between devices, spread(): lax.all_to_all(block, AXES, split_axis=0, concat_axis=0, axis_index_group...  8.57 us
    ppermute x7, starting transfers between devices, moved_by(): return lax.ppermute(block, AXES, route_of(move))  8.41 us
    pallas_call x1, Pallas kernels, per_device(): call(translate_kernel, (f32(3, 96, 4, 128), f32(3, 96, 4, 128), f32(96, 4...  6.13 us
    pallas_call x1, Pallas kernels, per_device(): call(near_kernel, f32(192, 256), [pltpu.VMEM((27, 2, 128, 128), F32), plt...  5.29 us
    pallas_call x1, Pallas kernels, per_device(): call(aggregate_kernel, (f32(32, 3, 4, 128), f32(192, 128)), [pltpu.VMEM((...  3.56 us
    unnamed x14, local copies, waits for them, and re-layouts  3.46 us
  transfers between devices with their start and end apart: 10, of which 8 were waited for; matrix products, arithmetic and copies ran while one was open for 0% of the time, Pallas kernels for 9%

profile of v5, /device:TPU:8, one launch (start us, length us, event | category | flops | bytes accessed | tf_op | source)
XLA Modules:
  0.0 71.6 jit_solution(17766382519910455115)
XLA Ops:
  0.0 0.0 copy-start.1
  0.0 3.6 %shard_map.73 = (f32[32,3,4,128]{3,2,1,0:T(4,128)}, f32[192,128]{1,0:T(8,128)}) custom-call(s32[1]{0:T(128)S(6)} %and.4.core_ref, f32[384,128]{1,0:T(8,128)} %bitcast.9, f32[2,1024,128]{2,1,0:T(8,128)} %rad_ref.1, f32[8,1024]{1,0:T(8,128)} %phase_ref.1), custom_call_target="tpu_custom_call" | custom-call | flops 600000000 | bytes 2000000 | tf_op jit(solution)/shard_map/pallas_call | solution.py:373
  3.6 11.3 %all-to-all-start = ((f32[32,3,4,128]{3,2,1,0:T(4,128)}), f32[32,3,4,128]{3,2,1,0:T(4,128)S(1)}, u32[]{:S(2)}, u32[]{:S(2)}) async-start(f32[32,3,4,128]{3,2,1,0:T(4,128)} %get-tuple-element.21), calls=%async_computation | async-start | bytes 393216 | tf_op jit(solution)/shard_map/all_to_all | solution.py:359
  14.9 0.1 collective-permute-start
  15.0 1.5 %collective-permute-done.got_ref = f32[192,128]{1,0:T(8,128)S(1)} collective-permute-done((f32[192,128]{1,0:T(8,128)}, f32[192,128]{1,0:T(8,128)S(1)}, u32[]{:S(2)}, u32[]{:S(2)}) %collective-permute-start) | collective-permute-done | bytes 98336 | tf_op jit(solution)/shard_map/ppermute | solution.py:355
  16.5 0.0 copy-start
  16.5 0.9 %copy-done = f32[2,2,6,8,2,128]{5,4,3,2,1,0:T(2,128)S(1)} copy-done((f32[2,2,6,8,2,128]{5,4,3,2,1,0:T(2,128)S(1)}, f32[2,2,6,8,2,128]{5,4,3,2,1,0:T(2,128)}, u32[]{:S(2)}) %copy-start) | copy-done | bytes 196632
  17.5 3.7 %collective-permute-start.1 = (f32[384,128]{1,0:T(8,128)S(1)}, f32[384,128]{1,0:T(8,128)S(1)}, u32[]{:S(2)}, u32[]{:S(2)}) collective-permute-start(f32[384,128]{1,0:T(8,128)S(1)} %shard_map.74.order_ref), channel_id=1, source_target_pairs={{0,1},{1,2},{2,3},{3,4},{4,5},{5,6},{6,7},{7,8},{8,9},{9,10},{10,1... | collective-permute-start | bytes 589832 | tf_op jit(solution)/shard_map/ppermute | solution.py:355
  21.2 0.0 copy-start.2
  21.2 0.9 %copy-done.2 = f32[316,2,64]{0,2,1:T(8,128)S(1)} copy-done((f32[316,2,64]{0,2,1:T(8,128)S(1)}, f32[316,2,64]{0,2,1:T(8,128)}, u32[]{:S(2)}) %copy-start.2) | copy-done | bytes 161816
  22.1 0.0 copy-start.3
  22.1 0.8 %copy-done.3 = s32[768,16]{0,1:T(8,128)S(1)} copy-done((s32[768,16]{0,1:T(8,128)S(1)}, s32[768,16]{0,1:T(8,128)}, u32[]{:S(2)}) %copy-start.3) | copy-done | bytes 49176
  22.9 0.0 copy-start.4
  22.9 0.8 %copy-done.4 = s32[768,16]{0,1:T(8,128)S(1)} copy-done((s32[768,16]{0,1:T(8,128)S(1)}, s32[768,16]{0,1:T(8,128)}, u32[]{:S(2)}) %copy-start.4) | copy-done | bytes 49176
  23.7 0.4 shard_map.75
  24.1 0.3 collective-permute-done.1.side_ref
  24.5 2.1 %all-to-all-done = f32[32,3,4,128]{3,2,1,0:T(4,128)S(1)} async-done(((f32[32,3,4,128]{3,2,1,0:T(4,128)}), f32[32,3,4,128]{3,2,1,0:T(4,128)S(1)}, u32[]{:S(2)}, u32[]{:S(2)}) %all-to-all-start) | async-done | bytes 196640 | tf_op jit(solution)/shard_map/all_to_all | solution.py:359
  26.6 6.1 %shard_map.76 = (f32[3,96,4,128]{3,2,1,0:T(4,128)S(1)}, f32[3,96,4,128]{3,2,1,0:T(4,128)S(1)}, f32[96,4,128]{2,1,0:T(4,128)S(1)}) custom-call(s32[16,128]{1,0:T(8,128)S(1)} %get-tuple-element.18.slots_ref, s32[16,128]{1,0:T(8,128)S(1)} %get-tuple-element.19.kinds_ref, f32[2528,128]{1,0:T(8,128)S(1)} %bitcast.14, f32[96,4,128]{2,1,0:T(4,128)S(1)} %bitcast.15, ...), custom_call_target="tpu_custom_call" | custom-call | flops 100000000 | bytes 3000000 | tf_op jit(solution)/shard_map/pallas_call | solution.py:409
  32.8 0.1 collective-permute-start.2
  32.9 2.0 %collective-permute-done.2.got_ref = f32[3,96,4,128]{3,2,1,0:T(4,128)S(1)} collective-permute-done((f32[3,96,4,128]{3,2,1,0:T(4,128)S(1)}, f32[3,96,4,128]{3,2,1,0:T(4,128)S(1)}, u32[]{:S(2)}, u32[]{:S(2)}) %collective-permute-start.2) | collective-permute-done | bytes 589856 | tf_op jit(solution)/shard_map/ppermute | solution.py:355
  34.8 0.0 copy-done.1
  34.8 0.2 shard_map.77
  35.0 0.2 collective-permute-start.6
  35.2 2.3 %collective-permute-start.3 = (f32[96,4,128]{2,1,0:T(4,128)S(1)}, f32[96,4,128]{2,1,0:T(4,128)S(1)}, u32[]{:S(2)}, u32[]{:S(2)}) collective-permute-start(f32[96,4,128]{2,1,0:T(4,128)S(1)} %get-tuple-element.25), channel_id=1, source_target_pairs={{0,80},{1,81},{2,82},{3,83},{4,84},{5,85},{6,86},{7,87},{8,88},{9,... | collective-permute-start | bytes 589832 | tf_op jit(solution)/shard_map/ppermute | solution.py:355
  37.5 1.3 %collective-permute-start.4 = (f32[96,4,128]{2,1,0:T(4,128)S(1)}, f32[96,4,128]{2,1,0:T(4,128)S(1)}, u32[]{:S(2)}, u32[]{:S(2)}) collective-permute-start(f32[96,4,128]{2,1,0:T(4,128)S(1)} %get-tuple-element.26), channel_id=1, source_target_pairs={{0,96},{1,97},{2,98},{3,99},{4,100},{5,101},{6,102},{7,103},{8,104... | collective-permute-start | bytes 589832 | tf_op jit(solution)/shard_map/ppermute | solution.py:355
  38.9 0.7 collective-permute-start.5
  39.5 4.0 %collective-permute-done.3.far_ref = f32[96,4,128]{2,1,0:T(4,128)S(1)} collective-permute-done((f32[96,4,128]{2,1,0:T(4,128)S(1)}, f32[96,4,128]{2,1,0:T(4,128)S(1)}, u32[]{:S(2)}, u32[]{:S(2)}) %collective-permute-start.3) | collective-permute-done | bytes 196640 | tf_op jit(solution)/shard_map/ppermute | solution.py:355
  43.6 0.0 collective-permute-done.6.cross_ref
  43.6 2.6 %collective-permute-start.7 = (f32[384,128]{1,0:T(8,128)S(1)}, f32[384,128]{1,0:T(8,128)S(1)}, u32[]{:S(2)}, u32[]{:S(2)}) collective-permute-start(f32[384,128]{1,0:T(8,128)S(1)} %shard_map.79), channel_id=1, source_target_pairs={{16,32},{32,16},{48,64},{64,48},{80,96},{96,80},{112,128},{128,112... | collective-permute-start | bytes 589832 | tf_op jit(solution)/shard_map/ppermute | solution.py:432
  46.2 1.9 %collective-permute-done.4.back_ref = f32[96,4,128]{2,1,0:T(4,128)S(1)} collective-permute-done((f32[96,4,128]{2,1,0:T(4,128)S(1)}, f32[96,4,128]{2,1,0:T(4,128)S(1)}, u32[]{:S(2)}, u32[]{:S(2)}) %collective-permute-start.4) | collective-permute-done | bytes 196640 | tf_op jit(solution)/shard_map/ppermute | solution.py:355
  48.2 0.2 collective-permute-done.5.ahead_ref
  48.3 0.8 %shard_map.78 = f32[96,4,128]{2,1,0:T(4,128)} custom-call(f32[96,4,128]{2,1,0:T(4,128)S(1)} %get-tuple-element.24.mid_ref, f32[96,4,128]{2,1,0:T(4,128)S(1)} %collective-permute-done.3.far_ref, f32[96,4,128]{2,1,0:T(4,128)S(1)} %collective-permute-done.4.back_ref, f32[96,4,128]{2,1,0:T(4,128)S(1)} %collective-permute-done.5.ahead_ref), custom_call_target="tpu_custom_call" | custom-call | flops 1000000 | bytes 1000000 | tf_op jit(solution)/shard_map/pallas_call | solution.py:435
  49.1 8.9 %all-to-all-start.1 = ((f32[32,3,4,128]{3,2,1,0:T(4,128)}), f32[32,3,4,128]{3,2,1,0:T(4,128)S(1)}, u32[]{:S(2)}, u32[]{:S(2)}) async-start(f32[32,3,4,128]{3,2,1,0:T(4,128)} %bitcast.7), calls=%async_computation.1 | async-start | bytes 393216 | tf_op jit(solution)/shard_map/all_to_all | solution.py:359
  58.0 0.0 copy-start.5
  58.0 0.0 copy-start.6
  58.0 0.0 collective-permute-done.7.away_ref
  58.0 5.3 %shard_map.80.near_ref = f32[192,256]{1,0:T(8,128)S(1)} custom-call(s32[1]{0:T(128)S(6)} %and.4.core_ref, f32[384,128]{1,0:T(8,128)S(1)} %bitcast.13, f32[384,128]{1,0:T(8,128)S(1)} %collective-permute-done.1.side_ref, f32[480,128]{1,0:T(8,128)S(1)} %collective-permute-done.6.cross_ref, f32[384,128]{1,0:T(8,128)S(1)} %collective-permute-done.7.away_ref, ...), custom_call_target="tpu_custom_call" | custom-call | flops 2000000000 | bytes 5000000 | tf_op jit(solution)/shard_map/pallas_call | solution.py:443
  63.3 6.4 %all-to-all-done.1.in_ref = f32[32,3,4,128]{3,2,1,0:T(4,128)S(1)} async-done(((f32[32,3,4,128]{3,2,1,0:T(4,128)}), f32[32,3,4,128]{3,2,1,0:T(4,128)S(1)}, u32[]{:S(2)}, u32[]{:S(2)}) %all-to-all-start.1) | async-done | bytes 196640 | tf_op jit(solution)/shard_map/all_to_all | solution.py:359
  69.7 0.0 copy-done.5
  69.7 0.0 copy-done.6
  69.7 1.9 %shard_map.81 = f32[384,128]{1,0:T(8,128)} custom-call(f32[32,3,4,128]{3,2,1,0:T(4,128)S(1)} %all-to-all-done.1.in_ref, f32[2,1024,128]{2,1,0:T(8,128)S(1)} %copy-done.5, f32[8,1024]{1,0:T(8,128)S(1)} %copy-done.6, f32[192,256]{1,0:T(8,128)S(1)} %shard_map.80.near_ref), custom_call_target="tpu_custom_call" | custom-call | flops 600000000 | bytes 2000000 | tf_op jit(solution)/shard_map/pallas_call | solution.py:459
  (2 shorter events, 0.0 us)
Async XLA Ops:
  0.0 34.8 %copy-start.1 = (f32[2,2,6,8,2,128]{5,4,3,2,1,0:T(2,128)S(1)}, f32[2,2,6,8,2,128]{5,4,3,2,1,0:T(2,128)}, u32[]{:S(2)}) copy-start(f32[2,2,6,8,2,128]{5,4,3,2,1,0:T(2,128)} %param.7) | copy-start | bytes 589828
  3.6 23.0 %all-to-all-start = ((f32[32,3,4,128]{3,2,1,0:T(4,128)}), f32[32,3,4,128]{3,2,1,0:T(4,128)S(1)}, u32[]{:S(2)}, u32[]{:S(2)}) async-start(f32[32,3,4,128]{3,2,1,0:T(4,128)} %get-tuple-element.21), calls=%async_computation | async-start | bytes 393216 | tf_op jit(solution)/shard_map/all_to_all | solution.py:359
  14.9 1.6 %collective-permute-start = (f32[192,128]{1,0:T(8,128)}, f32[192,128]{1,0:T(8,128)S(1)}, u32[]{:S(2)}, u32[]{:S(2)}) collective-permute-start(f32[192,128]{1,0:T(8,128)} %get-tuple-element.17), channel_id=1, source_target_pairs={{0,16},{1,17},{2,18},{3,19},{4,20},{5,21},{6,22},{7,23},{8,24},{9,... | collective-permute-start | bytes 294920 | tf_op jit(solution)/shard_map/ppermute | solution.py:355
  16.5 0.9 %copy-start = (f32[2,2,6,8,2,128]{5,4,3,2,1,0:T(2,128)S(1)}, f32[2,2,6,8,2,128]{5,4,3,2,1,0:T(2,128)}, u32[]{:S(2)}) copy-start(f32[2,2,6,8,2,128]{5,4,3,2,1,0:T(2,128)} %param.7) | copy-start | bytes 589828
  17.5 7.0 %collective-permute-start.1 = (f32[384,128]{1,0:T(8,128)S(1)}, f32[384,128]{1,0:T(8,128)S(1)}, u32[]{:S(2)}, u32[]{:S(2)}) collective-permute-start(f32[384,128]{1,0:T(8,128)S(1)} %shard_map.74.order_ref), channel_id=1, source_target_pairs={{0,1},{1,2},{2,3},{3,4},{4,5},{5,6},{6,7},{7,8},{8,9},{9,10},{10,1... | collective-permute-start | bytes 589832 | tf_op jit(solution)/shard_map/ppermute | solution.py:355
  21.2 0.9 %copy-start.2 = (f32[316,2,64]{0,2,1:T(8,128)S(1)}, f32[316,2,64]{0,2,1:T(8,128)}, u32[]{:S(2)}) copy-start(f32[316,2,64]{0,2,1:T(8,128)} %param.11) | copy-start | bytes 485380
  22.1 0.8 %copy-start.3 = (s32[768,16]{0,1:T(8,128)S(1)}, s32[768,16]{0,1:T(8,128)}, u32[]{:S(2)}) copy-start(s32[768,16]{0,1:T(8,128)} %param.12) | copy-start | bytes 147460
  22.9 0.8 %copy-start.4 = (s32[768,16]{0,1:T(8,128)S(1)}, s32[768,16]{0,1:T(8,128)}, u32[]{:S(2)}) copy-start(s32[768,16]{0,1:T(8,128)} %param.13) | copy-start | bytes 147460
  32.8 2.1 %collective-permute-start.2 = (f32[3,96,4,128]{3,2,1,0:T(4,128)S(1)}, f32[3,96,4,128]{3,2,1,0:T(4,128)S(1)}, u32[]{:S(2)}, u32[]{:S(2)}) collective-permute-start(f32[3,96,4,128]{3,2,1,0:T(4,128)S(1)} %get-tuple-element.23), channel_id=1, source_target_pairs={{0,16},{1,17},{2,18},{3,19},{4,20},{5,21},{6,22},{7,23},{8,24},{9,... | collective-permute-start | bytes 1769480 | tf_op jit(solution)/shard_map/ppermute | solution.py:355
  35.0 8.6 %collective-permute-start.6 = (f32[480,128]{1,0:T(8,128)S(1)}, f32[480,128]{1,0:T(8,128)S(1)}, u32[]{:S(2)}, u32[]{:S(2)}) collective-permute-start(f32[480,128]{1,0:T(8,128)S(1)} %get-tuple-element.28), channel_id=1, source_target_pairs={{0,16},{1,17},{2,18},{3,19},{4,20},{5,21},{6,22},{7,23},{8,24},{9,... | collective-permute-start | bytes 737288 | tf_op jit(solution)/shard_map/ppermute | solution.py:355
  35.2 8.3 %collective-permute-start.3 = (f32[96,4,128]{2,1,0:T(4,128)S(1)}, f32[96,4,128]{2,1,0:T(4,128)S(1)}, u32[]{:S(2)}, u32[]{:S(2)}) collective-permute-start(f32[96,4,128]{2,1,0:T(4,128)S(1)} %get-tuple-element.25), channel_id=1, source_target_pairs={{0,80},{1,81},{2,82},{3,83},{4,84},{5,85},{6,86},{7,87},{8,88},{9,... | collective-permute-start | bytes 589832 | tf_op jit(solution)/shard_map/ppermute | solution.py:355
  37.5 10.7 %collective-permute-start.4 = (f32[96,4,128]{2,1,0:T(4,128)S(1)}, f32[96,4,128]{2,1,0:T(4,128)S(1)}, u32[]{:S(2)}, u32[]{:S(2)}) collective-permute-start(f32[96,4,128]{2,1,0:T(4,128)S(1)} %get-tuple-element.26), channel_id=1, source_target_pairs={{0,96},{1,97},{2,98},{3,99},{4,100},{5,101},{6,102},{7,103},{8,104... | collective-permute-start | bytes 589832 | tf_op jit(solution)/shard_map/ppermute | solution.py:355
  38.9 9.5 %collective-permute-start.5 = (f32[96,4,128]{2,1,0:T(4,128)S(1)}, f32[96,4,128]{2,1,0:T(4,128)S(1)}, u32[]{:S(2)}, u32[]{:S(2)}) collective-permute-start(f32[96,4,128]{2,1,0:T(4,128)S(1)} %get-tuple-element.27), channel_id=1, source_target_pairs={{0,32},{1,33},{2,34},{3,35},{4,36},{5,37},{6,38},{7,39},{8,40},{9,... | collective-permute-start | bytes 589832 | tf_op jit(solution)/shard_map/ppermute | solution.py:355
  43.6 14.4 %collective-permute-start.7 = (f32[384,128]{1,0:T(8,128)S(1)}, f32[384,128]{1,0:T(8,128)S(1)}, u32[]{:S(2)}, u32[]{:S(2)}) collective-permute-start(f32[384,128]{1,0:T(8,128)S(1)} %shard_map.79), channel_id=1, source_target_pairs={{16,32},{32,16},{48,64},{64,48},{80,96},{96,80},{112,128},{128,112... | collective-permute-start | bytes 589832 | tf_op jit(solution)/shard_map/ppermute | solution.py:432
  49.1 20.6 %all-to-all-start.1 = ((f32[32,3,4,128]{3,2,1,0:T(4,128)}), f32[32,3,4,128]{3,2,1,0:T(4,128)S(1)}, u32[]{:S(2)}, u32[]{:S(2)}) async-start(f32[32,3,4,128]{3,2,1,0:T(4,128)} %bitcast.7), calls=%async_computation.1 | async-start | bytes 393216 | tf_op jit(solution)/shard_map/all_to_all | solution.py:359
  58.0 11.8 %copy-start.5 = (f32[2,1024,128]{2,1,0:T(8,128)S(1)}, f32[2,1024,128]{2,1,0:T(8,128)}, u32[]{:S(2)}) copy-start(f32[2,1024,128]{2,1,0:T(8,128)} %rad_ref.1) | copy-start | bytes 3145732
  58.0 11.7 %copy-start.6 = (f32[8,1024]{1,0:T(8,128)S(1)}, f32[8,1024]{1,0:T(8,128)}, u32[]{:S(2)}) copy-start(f32[8,1024]{1,0:T(8,128)} %phase_ref.1) | copy-start | bytes 98308

commit v6 on v1

--- a/solution.py
+++ b/solution.py
@@ -102,14 +102,20 @@
 
 
 def aggregate_kernel(
-    core_ref, cur_ref, rad_hbm, phase_ref, out_ref, beside_ref, away_ref, rad_ref, sems,
-    unroll=4, groups=(4, 4),
+    core_ref, cur_hbm, rad_hbm, phase_hbm, out_ref, beside_ref, away_ref,
+    cur_ref, rad_ref, phase_ref, sems, unroll=8, groups=(8,),
 ):
+    cur_copy = pltpu.make_async_copy(cur_hbm, cur_ref, sems.at[4])
+    phase_copy = pltpu.make_async_copy(phase_hbm, phase_ref, sems.at[5])
+    cur_copy.start()
+    for i in range(4):
+        radiation_copy(rad_hbm, rad_ref, sems, i).start()
+        if i == 1:
+            phase_copy.start()
+    cur_copy.wait()
     core = core_ref[0]
     beside_ref[...] = cur_ref[pl.ds(pl.multiple_of((1 - core) * 192, 8), 192), :]
     away_ref[...] = cur_ref[pl.ds(pl.multiple_of(core * 192, 8), 192), :]
-    for i in range(4):
-        radiation_copy(rad_hbm, rad_ref, sems, i).start()
     rows = cur_ref.shape[0] // 2
     x = jnp.concatenate(
         [cur_ref[pl.ds(0, rows, stride=2), :], cur_ref[pl.ds(1, rows, stride=2), :]], axis=1
@@ -136,6 +142,7 @@
                 out_ref[16 + d, parent] = block[4:]
         return carry
 
+    phase_copy.wait()
     first = 0
     for count in groups:
         for i in range(first // 2, (first + count) // 2):
@@ -144,7 +151,7 @@
         first += count
 
 
-def disaggregate_kernel(in_ref, rad_ref, phase_ref, near_ref, out_ref, acc_ref, unroll=4):
+def disaggregate_kernel(in_ref, rad_ref, phase_ref, near_ref, out_ref, acc_ref, unroll=8):
     acc_ref[...] = near_ref[...]
 
     def directions(step, carry):
@@ -264,8 +271,7 @@
 
 
 def fold_kernel(
-    keep_ref, got_ref, cur_ref, beside_ref, away_ref,
-    back_ref, mid_ref, ahead_ref, down_ref, up_ref,
+    keep_ref, got_ref, cur_ref, beside_ref, away_ref, back_ref, mid_ref, ahead_ref, down_ref, up_ref
 ):
     back_ref[...] = keep_ref[0] + got_ref[0]
     mid_ref[...] = keep_ref[1] + got_ref[1]
@@ -277,7 +283,7 @@
         ref[pl.ds(288, 96), :] = away_ref[pl.ds(j * 96, 96), :]
 
 
-def join_kernel(mid_ref, far_ref, back_ref, ahead_ref, down_ref, up_ref, out_ref):
+def join_kernel(mid_ref, far_ref, back_ref, ahead_ref, out_ref):
     out_ref[...] = (mid_ref[...] + far_ref[...]) + (back_ref[...] + ahead_ref[...])
 
 
@@ -301,8 +307,13 @@
     slab = lax.axis_index("slab")
     ring = slab % 8
     y, core = ring // 2, ring % 2
-    targets = lax.dynamic_slice_in_dim(far_targets.reshape(2, 8, 48, 16), ring, 1, 1)
-    kinds = lax.dynamic_slice_in_dim(far_offsets.reshape(2, 8, 48, 16), ring, 1, 1)
+
+    def own(table):
+        return jnp.concatenate(
+            [lax.dynamic_slice_in_dim(table, (ring + z_hi * 8) * 48, 48, 0) for z_hi in range(2)]
+        )
+
+    targets, kinds = own(far_targets), own(far_offsets)
     to_slab, row = targets // 48, targets % 48
     half, to_ring = to_slab // 8, to_slab % 8
     step = (to_ring // 2 - y + 4) % 4
@@ -343,8 +354,13 @@
     patterns, beside, away = call(
         aggregate_kernel,
         (f32(32, 3, 4, 128), f32(192, 128), f32(192, 128)),
-        [pltpu.VMEM((2, 1024, 128), F32), pltpu.SemaphoreType.DMA((4,))],
-        in_specs=[smem, vmem, hbm, vmem],
+        [
+            pltpu.VMEM((384, 128), F32),
+            pltpu.VMEM((2, 1024, 128), F32),
+            pltpu.VMEM((8, 1024), F32),
+            pltpu.SemaphoreType.DMA((6,)),
+        ],
+        in_specs=[smem] + [hbm] * 3,
         flops=600_000_000,
         moved=2_000_000,
         vmem_bytes=62 * 1024 * 1024,
@@ -376,12 +392,8 @@
     down = lax.ppermute(down, "dir", [(d, d + 1) for d in range(15)])
     up = lax.ppermute(up, "dir", [(d + 1, d) for d in range(15)])
     incoming = call(
-        join_kernel,
-        f32(96, 4, 128),
-        in_specs=[vmem] * 4 + [hbm] * 2,
-        flops=1_000_000,
-        moved=1_000_000,
-    )(mid, far_in, back_in, ahead_in, down, up)
+        join_kernel, f32(96, 4, 128), flops=1_000_000, moved=1_000_000
+    )(mid, far_in, back_in, ahead_in)
     returned = spread(incoming.reshape(32, 3, 4, 128), groups)
 
     near = call(

time: 74.7 us -> 69.9 us (0.936)
  the two profiles are of different devices: /device:TPU:8 before, /device:TPU:1 now
where the time goes in v6:
time: 69.9 us; the launch traced here: 69.5 us
  starting transfers between devices  38 us (54%)
  Pallas kernels  16.9 us (24%)
  waiting for transfers between devices  12.1 us (17%)
  local copies, waits for them, and re-layouts  2.04 us (3%)
    all_to_all x2, starting transfers between devices, spread(): lax.all_to_all(block, AXES, split_axis=0, concat_axis=0, axis_index_group...  20.9 us
    ppermute x5, starting transfers between devices, moved_by(): return lax.ppermute(block, AXES, route_of(move))  9.3 us
    all_to_all x2, waiting for transfers between devices, spread(): lax.all_to_all(block, AXES, split_axis=0, concat_axis=0, axis_index_group...  7.56 us
    pallas_call x1, Pallas kernels, per_device(): call(translate_kernel, (f32(3, 96, 4, 128), f32(3, 96, 4, 128), f32(96, 4...  5.62 us
    pallas_call x1, Pallas kernels, per_device(): call(near_kernel, f32(192, 256), [pltpu.VMEM((27, 2, 128, 128), F32), plt...  5.29 us
    ppermute x1, starting transfers between devices, per_device(): down = lax.ppermute(down, 'dir', [(d, d + 1) for d in range(15)])  3.44 us
    pallas_call x1, Pallas kernels, per_device(): call(aggregate_kernel, (f32(32, 3, 4, 128), f32(192, 128), f32(192, 128))...  3.41 us
    ppermute x5, waiting for transfers between devices, moved_by(): return lax.ppermute(block, AXES, route_of(move))  3.39 us
  transfers between devices with their start and end apart: 10, of which 4 were waited for; matrix products, arithmetic and copies ran while one was open for 3% of the time, Pallas kernels for 9%

profile of v6, /device:TPU:1, one launch (start us, length us, event | category | flops | bytes accessed | tf_op | source)
XLA Modules:
  0.0 69.5 jit_solution(6899088050634705201)
XLA Ops:
  0.0 0.0 copy-start
  0.0 3.4 %shard_map.73 = (f32[32,3,4,128]{3,2,1,0:T(4,128)}, f32[192,128]{1,0:T(8,128)}, f32[192,128]{1,0:T(8,128)}) custom-call(s32[1]{0:T(128)} %bitcast.1.core_ref, f32[384,128]{1,0:T(8,128)} %bitcast.8, f32[2,1024,128]{2,1,0:T(8,128)} %rad_ref.1, f32[8,1024]{1,0:T(8,128)} %phase_ref.1), custom_call_target="tpu_custom_call" | custom-call | flops 600000000 | bytes 2000000 | tf_op jit(solution)/shard_map/pallas_call | solution.py:354
  3.4 11.9 %all-to-all-start = ((f32[32,3,4,128]{3,2,1,0:T(4,128)}), f32[32,3,4,128]{3,2,1,0:T(4,128)S(1)}, u32[]{:S(2)}, u32[]{:S(2)}) async-start(f32[32,3,4,128]{3,2,1,0:T(4,128)} %get-tuple-element.16), calls=%async_computation | async-start | bytes 393216 | tf_op jit(solution)/shard_map/all_to_all | solution.py:339
  15.3 1.0 %collective-permute-start = (f32[192,128]{1,0:T(8,128)}, f32[192,128]{1,0:T(8,128)S(1)}, u32[]{:S(2)}, u32[]{:S(2)}) collective-permute-start(f32[192,128]{1,0:T(8,128)} %get-tuple-element.17), channel_id=1, source_target_pairs={{0,16},{1,17},{2,18},{3,19},{4,20},{5,21},{6,22},{7,23},{8,24},{9,... | collective-permute-start | bytes 294920 | tf_op jit(solution)/shard_map/ppermute | solution.py:335
  16.4 3.1 %collective-permute-start.1 = (f32[192,128]{1,0:T(8,128)}, f32[192,128]{1,0:T(8,128)S(1)}, u32[]{:S(2)}, u32[]{:S(2)}) collective-permute-start(f32[192,128]{1,0:T(8,128)} %get-tuple-element.18), channel_id=1, source_target_pairs={{16,32},{32,16},{48,64},{64,48},{80,96},{96,80},{112,128},{128,112... | collective-permute-start | bytes 294920 | tf_op jit(solution)/shard_map/ppermute | solution.py:370
  19.5 0.9 %constant_dynamic-slice_fusion.2 = (s32[48,16]{0,1:T(8,128)S(1)}, s32[48,16]{0,1:T(8,128)S(1)}, s32[48,16]{0,1:T(8,128)S(1)}, s32[48,16]{0,1:T(8,128)S(1)}) fusion(s32[768,16]{0,1:T(8,128)} %param.13, s32[]{:T(128)S(6)} %select_n.85, s32[]{:T(128)S(6)} %select_n.86, s32[768,16]{0,1:T(8,128)} %param.12), kind=kLoop, calls=%fused_computation.43 | loop fusion | bytes 24584 | tf_op jit(solution)/shard_map/dynamic_slice | solution.py:313
  20.3 0.1 add_multiply_fusion
  20.4 0.1 broadcast_divide_fusion
  20.5 0.0 copy-done
  20.5 0.1 sign_compare_fusion.2
  20.6 0.1 copy.9
  20.7 0.1 ne.102
  20.8 0.1 copy.11
  20.9 0.1 div.42
  21.0 0.1 copy.12
  21.1 0.1 mul.41.kinds_ref
  21.2 0.1 copy.10
  21.3 0.1 rem.138
  21.4 0.1 fusion.9.slots_ref
  21.5 0.2 copy.13
  21.7 0.0 collective-permute-done.beside_ref
  21.7 1.1 %collective-permute-done.1.away_ref = f32[192,128]{1,0:T(8,128)S(1)} collective-permute-done((f32[192,128]{1,0:T(8,128)}, f32[192,128]{1,0:T(8,128)S(1)}, u32[]{:S(2)}, u32[]{:S(2)}) %collective-permute-start.1) | collective-permute-done | bytes 98336 | tf_op jit(solution)/shard_map/ppermute | solution.py:370
  22.8 2.4 %all-to-all-done = f32[32,3,4,128]{3,2,1,0:T(4,128)S(1)} async-done(((f32[32,3,4,128]{3,2,1,0:T(4,128)}), f32[32,3,4,128]{3,2,1,0:T(4,128)S(1)}, u32[]{:S(2)}, u32[]{:S(2)}) %all-to-all-start) | async-done | bytes 196640 | tf_op jit(solution)/shard_map/all_to_all | solution.py:339
  25.2 0.2 broadcast_in_dim.15
  25.5 5.6 %shard_map.74 = (f32[3,96,4,128]{3,2,1,0:T(4,128)S(1)}, f32[3,96,4,128]{3,2,1,0:T(4,128)S(1)}, f32[96,4,128]{2,1,0:T(4,128)S(1)}) custom-call(s32[1536]{0:T(1024)S(1)} %fusion.9.slots_ref, s32[1536]{0:T(1024)S(1)} %mul.41.kinds_ref, f32[2528,128]{1,0:T(8,128)S(1)} %bitcast.6, f32[96,4,128]{2,1,0:T(4,128)S(1)} %bitcast.7, ...), custom_call_target="tpu_custom_call" | custom-call | flops 100000000 | bytes 3000000 | tf_op jit(solution)/shard_map/pallas_call | solution.py:374
  31.1 2.8 %collective-permute-start.2 = (f32[3,96,4,128]{3,2,1,0:T(4,128)S(1)}, f32[3,96,4,128]{3,2,1,0:T(4,128)S(1)}, u32[]{:S(2)}, u32[]{:S(2)}) collective-permute-start(f32[3,96,4,128]{3,2,1,0:T(4,128)S(1)} %get-tuple-element.20), channel_id=1, source_target_pairs={{0,16},{1,17},{2,18},{3,19},{4,20},{5,21},{6,22},{7,23},{8,24},{9,... | collective-permute-start | bytes 1769480 | tf_op jit(solution)/shard_map/ppermute | solution.py:335
  33.9 2.9 %collective-permute-start.3 = (f32[96,4,128]{2,1,0:T(4,128)S(1)}, f32[96,4,128]{2,1,0:T(4,128)S(1)}, u32[]{:S(2)}, u32[]{:S(2)}) collective-permute-start(f32[96,4,128]{2,1,0:T(4,128)S(1)} %get-tuple-element.22), channel_id=1, source_target_pairs={{0,80},{1,81},{2,82},{3,83},{4,84},{5,85},{6,86},{7,87},{8,88},{9,... | collective-permute-start | bytes 589832 | tf_op jit(solution)/shard_map/ppermute | solution.py:335
  36.8 0.0 collective-permute-done.2.got_ref
  36.8 0.0 copy-done.1
  36.8 0.2 shard_map.75
  37.0 2.5 %collective-permute-start.4 = (f32[96,4,128]{2,1,0:T(4,128)S(1)}, f32[96,4,128]{2,1,0:T(4,128)S(1)}, u32[]{:S(2)}, u32[]{:S(2)}) collective-permute-start(f32[96,4,128]{2,1,0:T(4,128)S(1)} %get-tuple-element.23), channel_id=1, source_target_pairs={{0,96},{1,97},{2,98},{3,99},{4,100},{5,101},{6,102},{7,103},{8,104... | collective-permute-start | bytes 589832 | tf_op jit(solution)/shard_map/ppermute | solution.py:335
  39.5 0.0 collective-permute-start.5
  39.5 3.4 %collective-permute-start.6 = (f32[384,128]{1,0:T(8,128)S(1)}, f32[384,128]{1,0:T(8,128)S(1)}, u32[]{:S(2)}, u32[]{:S(2)}) collective-permute-start(f32[384,128]{1,0:T(8,128)S(1)} %get-tuple-element.25), channel_id=1, source_target_pairs={{0,1},{1,2},{2,3},{3,4},{4,5},{5,6},{6,7},{7,8},{8,9},{9,10},{10,1... | collective-permute-start | bytes 589832 | tf_op jit(solution)/shard_map/ppermute | solution.py:392
  43.0 1.3 %collective-permute-start.7 = (f32[384,128]{1,0:T(8,128)S(1)}, f32[384,128]{1,0:T(8,128)S(1)}, u32[]{:S(2)}, u32[]{:S(2)}) collective-permute-start(f32[384,128]{1,0:T(8,128)S(1)} %get-tuple-element.26), channel_id=1, source_target_pairs={{1,0},{2,1},{3,2},{4,3},{5,4},{6,5},{7,6},{8,7},{9,8},{10,9},{11,1... | collective-permute-start | bytes 589832 | tf_op jit(solution)/shard_map/ppermute | solution.py:393
  44.3 0.0 collective-permute-done.3.far_ref
  44.3 3.4 %collective-permute-done.4.back_ref = f32[96,4,128]{2,1,0:T(4,128)S(1)} collective-permute-done((f32[96,4,128]{2,1,0:T(4,128)S(1)}, f32[96,4,128]{2,1,0:T(4,128)S(1)}, u32[]{:S(2)}, u32[]{:S(2)}) %collective-permute-start.4) | collective-permute-done | bytes 196640 | tf_op jit(solution)/shard_map/ppermute | solution.py:335
  47.7 0.0 collective-permute-done.5.ahead_ref
  47.7 0.8 %shard_map.76 = f32[96,4,128]{2,1,0:T(4,128)} custom-call(f32[96,4,128]{2,1,0:T(4,128)S(1)} %get-tuple-element.21.mid_ref, f32[96,4,128]{2,1,0:T(4,128)S(1)} %collective-permute-done.3.far_ref, f32[96,4,128]{2,1,0:T(4,128)S(1)} %collective-permute-done.4.back_ref, f32[96,4,128]{2,1,0:T(4,128)S(1)} %collective-permute-done.5.ahead_ref), custom_call_target="tpu_custom_call" | custom-call | flops 1000000 | bytes 1000000 | tf_op jit(solution)/shard_map/pallas_call | solution.py:394
  48.4 9.0 %all-to-all-start.1 = ((f32[32,3,4,128]{3,2,1,0:T(4,128)}), f32[32,3,4,128]{3,2,1,0:T(4,128)S(1)}, u32[]{:S(2)}, u32[]{:S(2)}) async-start(f32[32,3,4,128]{3,2,1,0:T(4,128)} %bitcast.4), calls=%async_computation.1 | async-start | bytes 393216 | tf_op jit(solution)/shard_map/all_to_all | solution.py:339
  57.5 0.0 copy-start.2
  57.5 0.0 copy-start.3
  57.5 0.0 collective-permute-done.6.down_ref
  57.5 0.0 collective-permute-done.7.up_ref
  57.5 5.3 %shard_map.77.near_ref = f32[192,256]{1,0:T(8,128)S(1)} custom-call(s32[1]{0:T(128)} %bitcast.1.core_ref, f32[384,128]{1,0:T(8,128)S(1)} %bitcast.10, f32[192,128]{1,0:T(8,128)S(1)} %collective-permute-done.beside_ref, f32[192,128]{1,0:T(8,128)S(1)} %collective-permute-done.1.away_ref, f32[384,128]{1,0:T(8,128)S(1)} %collective-permute-done.6.down_ref, ...), custom_call_target="tpu_custom_call" | custom-call | flops 2000000000 | bytes 5000000 | tf_op jit(solution)/shard_map/pallas_call | solution.py:399
  62.8 5.1 %all-to-all-done.1.in_ref = f32[32,3,4,128]{3,2,1,0:T(4,128)S(1)} async-done(((f32[32,3,4,128]{3,2,1,0:T(4,128)}), f32[32,3,4,128]{3,2,1,0:T(4,128)S(1)}, u32[]{:S(2)}, u32[]{:S(2)}) %all-to-all-start.1) | async-done | bytes 196640 | tf_op jit(solution)/shard_map/all_to_all | solution.py:339
  67.9 0.0 copy-done.2
  67.9 0.0 copy-done.3
  67.9 1.6 %shard_map.78 = f32[384,128]{1,0:T(8,128)} custom-call(f32[32,3,4,128]{3,2,1,0:T(4,128)S(1)} %all-to-all-done.1.in_ref, f32[2,1024,128]{2,1,0:T(8,128)S(1)} %copy-done.2, f32[8,1024]{1,0:T(8,128)S(1)} %copy-done.3, f32[192,256]{1,0:T(8,128)S(1)} %shard_map.77.near_ref), custom_call_target="tpu_custom_call" | custom-call | flops 600000000 | bytes 2000000 | tf_op jit(solution)/shard_map/pallas_call | solution.py:415
  (3 shorter events, 0.0 us)
Async XLA Ops:
  0.0 20.5 %copy-start = (f32[316,2,64]{0,2,1:T(8,128)S(1)}, f32[316,2,64]{0,2,1:T(8,128)}, u32[]{:S(2)}) copy-start(f32[316,2,64]{0,2,1:T(8,128)} %param.11) | copy-start | bytes 485380
  0.0 36.8 %copy-start.1 = (f32[2,2,6,8,2,128]{5,4,3,2,1,0:T(2,128)S(1)}, f32[2,2,6,8,2,128]{5,4,3,2,1,0:T(2,128)}, u32[]{:S(2)}) copy-start(f32[2,2,6,8,2,128]{5,4,3,2,1,0:T(2,128)} %param.7) | copy-start | bytes 589828
  3.4 21.8 %all-to-all-start = ((f32[32,3,4,128]{3,2,1,0:T(4,128)}), f32[32,3,4,128]{3,2,1,0:T(4,128)S(1)}, u32[]{:S(2)}, u32[]{:S(2)}) async-start(f32[32,3,4,128]{3,2,1,0:T(4,128)} %get-tuple-element.16), calls=%async_computation | async-start | bytes 393216 | tf_op jit(solution)/shard_map/all_to_all | solution.py:339
  15.3 6.4 %collective-permute-start = (f32[192,128]{1,0:T(8,128)}, f32[192,128]{1,0:T(8,128)S(1)}, u32[]{:S(2)}, u32[]{:S(2)}) collective-permute-start(f32[192,128]{1,0:T(8,128)} %get-tuple-element.17), channel_id=1, source_target_pairs={{0,16},{1,17},{2,18},{3,19},{4,20},{5,21},{6,22},{7,23},{8,24},{9,... | collective-permute-start | bytes 294920 | tf_op jit(solution)/shard_map/ppermute | solution.py:335
  16.4 6.4 %collective-permute-start.1 = (f32[192,128]{1,0:T(8,128)}, f32[192,128]{1,0:T(8,128)S(1)}, u32[]{:S(2)}, u32[]{:S(2)}) collective-permute-start(f32[192,128]{1,0:T(8,128)} %get-tuple-element.18), channel_id=1, source_target_pairs={{16,32},{32,16},{48,64},{64,48},{80,96},{96,80},{112,128},{128,112... | collective-permute-start | bytes 294920 | tf_op jit(solution)/shard_map/ppermute | solution.py:370
  31.1 5.7 %collective-permute-start.2 = (f32[3,96,4,128]{3,2,1,0:T(4,128)S(1)}, f32[3,96,4,128]{3,2,1,0:T(4,128)S(1)}, u32[]{:S(2)}, u32[]{:S(2)}) collective-permute-start(f32[3,96,4,128]{3,2,1,0:T(4,128)S(1)} %get-tuple-element.20), channel_id=1, source_target_pairs={{0,16},{1,17},{2,18},{3,19},{4,20},{5,21},{6,22},{7,23},{8,24},{9,... | collective-permute-start | bytes 1769480 | tf_op jit(solution)/shard_map/ppermute | solution.py:335
  33.9 10.4 %collective-permute-start.3 = (f32[96,4,128]{2,1,0:T(4,128)S(1)}, f32[96,4,128]{2,1,0:T(4,128)S(1)}, u32[]{:S(2)}, u32[]{:S(2)}) collective-permute-start(f32[96,4,128]{2,1,0:T(4,128)S(1)} %get-tuple-element.22), channel_id=1, source_target_pairs={{0,80},{1,81},{2,82},{3,83},{4,84},{5,85},{6,86},{7,87},{8,88},{9,... | collective-permute-start | bytes 589832 | tf_op jit(solution)/shard_map/ppermute | solution.py:335
  37.0 10.7 %collective-permute-start.4 = (f32[96,4,128]{2,1,0:T(4,128)S(1)}, f32[96,4,128]{2,1,0:T(4,128)S(1)}, u32[]{:S(2)}, u32[]{:S(2)}) collective-permute-start(f32[96,4,128]{2,1,0:T(4,128)S(1)} %get-tuple-element.23), channel_id=1, source_target_pairs={{0,96},{1,97},{2,98},{3,99},{4,100},{5,101},{6,102},{7,103},{8,104... | collective-permute-start | bytes 589832 | tf_op jit(solution)/shard_map/ppermute | solution.py:335
  39.5 8.1 %collective-permute-start.5 = (f32[96,4,128]{2,1,0:T(4,128)S(1)}, f32[96,4,128]{2,1,0:T(4,128)S(1)}, u32[]{:S(2)}, u32[]{:S(2)}) collective-permute-start(f32[96,4,128]{2,1,0:T(4,128)S(1)} %get-tuple-element.24), channel_id=1, source_target_pairs={{0,32},{1,33},{2,34},{3,35},{4,36},{5,37},{6,38},{7,39},{8,40},{9,... | collective-permute-start | bytes 589832 | tf_op jit(solution)/shard_map/ppermute | solution.py:335
  39.5 18.0 %collective-permute-start.6 = (f32[384,128]{1,0:T(8,128)S(1)}, f32[384,128]{1,0:T(8,128)S(1)}, u32[]{:S(2)}, u32[]{:S(2)}) collective-permute-start(f32[384,128]{1,0:T(8,128)S(1)} %get-tuple-element.25), channel_id=1, source_target_pairs={{0,1},{1,2},{2,3},{3,4},{4,5},{5,6},{6,7},{7,8},{8,9},{9,10},{10,1... | collective-permute-start | bytes 589832 | tf_op jit(solution)/shard_map/ppermute | solution.py:392
  43.0 14.5 %collective-permute-start.7 = (f32[384,128]{1,0:T(8,128)S(1)}, f32[384,128]{1,0:T(8,128)S(1)}, u32[]{:S(2)}, u32[]{:S(2)}) collective-permute-start(f32[384,128]{1,0:T(8,128)S(1)} %get-tuple-element.26), channel_id=1, source_target_pairs={{1,0},{2,1},{3,2},{4,3},{5,4},{6,5},{7,6},{8,7},{9,8},{10,9},{11,1... | collective-permute-start | bytes 589832 | tf_op jit(solution)/shard_map/ppermute | solution.py:393
  48.4 19.5 %all-to-all-start.1 = ((f32[32,3,4,128]{3,2,1,0:T(4,128)}), f32[32,3,4,128]{3,2,1,0:T(4,128)S(1)}, u32[]{:S(2)}, u32[]{:S(2)}) async-start(f32[32,3,4,128]{3,2,1,0:T(4,128)} %bitcast.4), calls=%async_computation.1 | async-start | bytes 393216 | tf_op jit(solution)/shard_map/all_to_all | solution.py:339
  57.5 10.5 %copy-start.2 = (f32[2,1024,128]{2,1,0:T(8,128)S(1)}, f32[2,1024,128]{2,1,0:T(8,128)}, u32[]{:S(2)}) copy-start(f32[2,1024,128]{2,1,0:T(8,128)} %rad_ref.1) | copy-start | bytes 3145732
  57.5 10.4 %copy-start.3 = (f32[8,1024]{1,0:T(8,128)S(1)}, f32[8,1024]{1,0:T(8,128)}, u32[]{:S(2)}) copy-start(f32[8,1024]{1,0:T(8,128)} %phase_ref.1) | copy-start | bytes 98308

commit v7 on v4

--- a/solution.py
+++ b/solution.py
@@ -103,7 +103,7 @@
 
 def aggregate_kernel(
     cur_hbm, rad_hbm, phase_hbm, out_ref, down_ref, up_ref, cur_ref, rad_ref, phase_ref, sems,
-    unroll=4, groups=(4, 4),
+    unroll=8, groups=(8,),
 ):
     cur_copy = pltpu.make_async_copy(cur_hbm, cur_ref, sems.at[4])
     phase_copy = pltpu.make_async_copy(phase_hbm, phase_ref, sems.at[5])
@@ -151,7 +151,7 @@
         first += count
 
 
-def disaggregate_kernel(in_ref, rad_ref, phase_ref, near_ref, out_ref, acc_ref, unroll=4):
+def disaggregate_kernel(in_ref, rad_ref, phase_ref, near_ref, out_ref, acc_ref, unroll=8):
     acc_ref[...] = near_ref[...]
 
     def directions(step, carry):

time: 69.9 us -> 69.4 us (level)
  no operation moved by 1% of the time
where the time goes in v7:
time: 69.4 us; the launch traced here: 69 us
  starting transfers between devices  32.5 us (47%)
  waiting for transfers between devices  17.1 us (25%)
  Pallas kernels  16.9 us (24%)
  local copies, waits for them, and re-layouts  2.04 us (3%)
    all_to_all x2, starting transfers between devices, spread(): lax.all_to_all(block, AXES, split_axis=0, concat_axis=0, axis_index_group...  19.5 us
    all_to_all x2, waiting for transfers between devices, spread(): lax.all_to_all(block, AXES, split_axis=0, concat_axis=0, axis_index_group...  8.1 us
    ppermute x5, waiting for transfers between devices, moved_by(): return lax.ppermute(block, AXES, route_of(move))  5.64 us
    pallas_call x1, Pallas kernels, per_device(): call(translate_kernel, (f32(3, 96, 4, 128), f32(3, 96, 4, 128), f32(96, 4...  5.62 us
    pallas_call x1, Pallas kernels, per_device(): call(near_kernel, f32(192, 256), [pltpu.VMEM((27, 2, 128, 128), F32), plt...  5.3 us
    ppermute x5, starting transfers between devices, moved_by(): return lax.ppermute(block, AXES, route_of(move))  4.62 us
    ppermute x1, starting transfers between devices, per_device(): down = lax.ppermute(down, 'dir', [(d, d + 1) for d in range(15)])  3.7 us
    pallas_call x1, Pallas kernels, per_device(): call(aggregate_kernel, (f32(32, 3, 4, 128), f32(192, 128), f32(192, 128))...  3.42 us
  transfers between devices with their start and end apart: 10, of which 6 were waited for; matrix products, arithmetic and copies ran while one was open for 3% of the time, Pallas kernels for 9%

profile of v7, /device:TPU:8, one launch (start us, length us, event | category | flops | bytes accessed | tf_op | source)
XLA Modules:
  0.0 69.0 jit_solution(12242053024132939349)
XLA Ops:
  0.0 0.0 copy-start
  0.0 3.4 %shard_map.73 = (f32[32,3,4,128]{3,2,1,0:T(4,128)}, f32[192,128]{1,0:T(8,128)}, f32[192,128]{1,0:T(8,128)}) custom-call(f32[384,128]{1,0:T(8,128)} %bitcast.8, f32[2,1024,128]{2,1,0:T(8,128)} %rad_ref.1, f32[8,1024]{1,0:T(8,128)} %phase_ref.1), custom_call_target="tpu_custom_call" | custom-call | flops 600000000 | bytes 2000000 | tf_op jit(solution)/shard_map/pallas_call | solution.py:355
  3.4 11.3 %all-to-all-start = ((f32[32,3,4,128]{3,2,1,0:T(4,128)}), f32[32,3,4,128]{3,2,1,0:T(4,128)S(1)}, u32[]{:S(2)}, u32[]{:S(2)}) async-start(f32[32,3,4,128]{3,2,1,0:T(4,128)} %get-tuple-element.16), calls=%async_computation | async-start | bytes 393216 | tf_op jit(solution)/shard_map/all_to_all | solution.py:340
  14.8 3.7 %collective-permute-start = (f32[192,128]{1,0:T(8,128)}, f32[192,128]{1,0:T(8,128)S(1)}, u32[]{:S(2)}, u32[]{:S(2)}) collective-permute-start(f32[192,128]{1,0:T(8,128)} %get-tuple-element.17), channel_id=1, source_target_pairs={{0,1},{1,2},{2,3},{3,4},{4,5},{5,6},{6,7},{7,8},{8,9},{9,10},{10,1... | collective-permute-start | bytes 294920 | tf_op jit(solution)/shard_map/ppermute | solution.py:370
  18.5 1.3 %collective-permute-start.1 = (f32[192,128]{1,0:T(8,128)}, f32[192,128]{1,0:T(8,128)S(1)}, u32[]{:S(2)}, u32[]{:S(2)}) collective-permute-start(f32[192,128]{1,0:T(8,128)} %get-tuple-element.18), channel_id=1, source_target_pairs={{1,0},{2,1},{3,2},{4,3},{5,4},{6,5},{7,6},{8,7},{9,8},{10,9},{11,1... | collective-permute-start | bytes 294920 | tf_op jit(solution)/shard_map/ppermute | solution.py:371
  19.8 0.9 %constant_dynamic-slice_fusion.2 = (s32[48,16]{0,1:T(8,128)S(1)}, s32[48,16]{0,1:T(8,128)S(1)}, s32[48,16]{0,1:T(8,128)S(1)}, s32[48,16]{0,1:T(8,128)S(1)}) fusion(s32[768,16]{0,1:T(8,128)} %param.13, s32[]{:T(128)S(6)} %select_n.86, s32[]{:T(128)S(6)} %select_n.87, s32[768,16]{0,1:T(8,128)} %param.12), kind=kLoop, calls=%fused_computation.43 | loop fusion | bytes 24584 | tf_op jit(solution)/shard_map/dynamic_slice | solution.py:314
  20.7 0.1 add_multiply_fusion
  20.7 0.1 broadcast_divide_fusion
  20.8 0.0 copy-done
  20.8 0.1 sign_compare_fusion.2
  20.9 0.1 copy.9
  21.0 0.1 ne.103
  21.2 0.1 copy.11
  21.2 0.1 div.42
  21.3 0.1 copy.12
  21.4 0.1 mul.41.kinds_ref
  21.5 0.1 copy.10
  21.6 0.1 rem.141
  21.7 0.1 fusion.9.slots_ref
  21.8 0.2 copy.13
  22.0 0.0 collective-permute-done.down_ref
  22.0 3.3 %collective-permute-done.1.up_ref = f32[192,128]{1,0:T(8,128)S(1)} collective-permute-done((f32[192,128]{1,0:T(8,128)}, f32[192,128]{1,0:T(8,128)S(1)}, u32[]{:S(2)}, u32[]{:S(2)}) %collective-permute-start.1) | collective-permute-done | bytes 98336 | tf_op jit(solution)/shard_map/ppermute | solution.py:371
  25.3 2.0 %all-to-all-done = f32[32,3,4,128]{3,2,1,0:T(4,128)S(1)} async-done(((f32[32,3,4,128]{3,2,1,0:T(4,128)}), f32[32,3,4,128]{3,2,1,0:T(4,128)S(1)}, u32[]{:S(2)}, u32[]{:S(2)}) %all-to-all-start) | async-done | bytes 196640 | tf_op jit(solution)/shard_map/all_to_all | solution.py:340
  27.4 0.2 broadcast_in_dim.15
  27.6 5.6 %shard_map.74 = (f32[3,96,4,128]{3,2,1,0:T(4,128)S(1)}, f32[3,96,4,128]{3,2,1,0:T(4,128)S(1)}, f32[96,4,128]{2,1,0:T(4,128)S(1)}) custom-call(s32[1536]{0:T(1024)S(1)} %fusion.9.slots_ref, s32[1536]{0:T(1024)S(1)} %mul.41.kinds_ref, f32[2528,128]{1,0:T(8,128)S(1)} %bitcast.6, f32[96,4,128]{2,1,0:T(4,128)S(1)} %bitcast.7, ...), custom_call_target="tpu_custom_call" | custom-call | flops 100000000 | bytes 3000000 | tf_op jit(solution)/shard_map/pallas_call | solution.py:373
  33.2 0.1 collective-permute-start.2
  33.3 2.4 %collective-permute-start.3 = (f32[96,4,128]{2,1,0:T(4,128)S(1)}, f32[96,4,128]{2,1,0:T(4,128)S(1)}, u32[]{:S(2)}, u32[]{:S(2)}) collective-permute-start(f32[96,4,128]{2,1,0:T(4,128)S(1)} %get-tuple-element.22), channel_id=1, source_target_pairs={{0,80},{1,81},{2,82},{3,83},{4,84},{5,85},{6,86},{7,87},{8,88},{9,... | collective-permute-start | bytes 589832 | tf_op jit(solution)/shard_map/ppermute | solution.py:336
  35.7 0.0 collective-permute-done.2.got_ref
  35.8 0.0 copy-done.1
  35.8 0.2 shard_map.75
  35.9 1.4 %collective-permute-start.4 = (f32[96,4,128]{2,1,0:T(4,128)S(1)}, f32[96,4,128]{2,1,0:T(4,128)S(1)}, u32[]{:S(2)}, u32[]{:S(2)}) collective-permute-start(f32[96,4,128]{2,1,0:T(4,128)S(1)} %get-tuple-element.23), channel_id=1, source_target_pairs={{0,96},{1,97},{2,98},{3,99},{4,100},{5,101},{6,102},{7,103},{8,104... | collective-permute-start | bytes 589832 | tf_op jit(solution)/shard_map/ppermute | solution.py:336
  37.4 0.7 collective-permute-start.5
  38.0 0.0 collective-permute-start.6
  38.0 3.4 %collective-permute-start.7 = (f32[384,128]{1,0:T(8,128)S(1)}, f32[384,128]{1,0:T(8,128)S(1)}, u32[]{:S(2)}, u32[]{:S(2)}) collective-permute-start(f32[384,128]{1,0:T(8,128)S(1)} %get-tuple-element.26), channel_id=1, source_target_pairs={{16,32},{32,16},{48,64},{64,48},{80,96},{96,80},{112,128},{128,112... | collective-permute-start | bytes 589832 | tf_op jit(solution)/shard_map/ppermute | solution.py:393
  41.4 0.3 collective-permute-done.3.far_ref
  41.7 4.7 %collective-permute-done.4.back_ref = f32[96,4,128]{2,1,0:T(4,128)S(1)} collective-permute-done((f32[96,4,128]{2,1,0:T(4,128)S(1)}, f32[96,4,128]{2,1,0:T(4,128)S(1)}, u32[]{:S(2)}, u32[]{:S(2)}) %collective-permute-start.4) | collective-permute-done | bytes 196640 | tf_op jit(solution)/shard_map/ppermute | solution.py:336
  46.3 0.7 %collective-permute-done.5.ahead_ref = f32[96,4,128]{2,1,0:T(4,128)S(1)} collective-permute-done((f32[96,4,128]{2,1,0:T(4,128)S(1)}, f32[96,4,128]{2,1,0:T(4,128)S(1)}, u32[]{:S(2)}, u32[]{:S(2)}) %collective-permute-start.5) | collective-permute-done | bytes 196640 | tf_op jit(solution)/shard_map/ppermute | solution.py:336
  47.0 0.8 %shard_map.76 = f32[96,4,128]{2,1,0:T(4,128)} custom-call(f32[96,4,128]{2,1,0:T(4,128)S(1)} %get-tuple-element.21.mid_ref, f32[96,4,128]{2,1,0:T(4,128)S(1)} %collective-permute-done.3.far_ref, f32[96,4,128]{2,1,0:T(4,128)S(1)} %collective-permute-done.4.back_ref, f32[96,4,128]{2,1,0:T(4,128)S(1)} %collective-permute-done.5.ahead_ref), custom_call_target="tpu_custom_call" | custom-call | flops 1000000 | bytes 1000000 | tf_op jit(solution)/shard_map/pallas_call | solution.py:396
  47.8 8.2 %all-to-all-start.1 = ((f32[32,3,4,128]{3,2,1,0:T(4,128)}), f32[32,3,4,128]{3,2,1,0:T(4,128)S(1)}, u32[]{:S(2)}, u32[]{:S(2)}) async-start(f32[32,3,4,128]{3,2,1,0:T(4,128)} %bitcast.4), calls=%async_computation.1 | async-start | bytes 393216 | tf_op jit(solution)/shard_map/all_to_all | solution.py:340
  56.0 0.0 copy-start.2
  56.0 0.0 copy-start.3
  56.0 0.0 collective-permute-done.6.beside_ref
  56.0 0.0 collective-permute-done.7.away_ref
  56.1 5.3 %shard_map.77.near_ref = f32[192,256]{1,0:T(8,128)S(1)} custom-call(s32[1]{0:T(128)} %bitcast.core_ref, f32[384,128]{1,0:T(8,128)S(1)} %bitcast.10, f32[384,128]{1,0:T(8,128)S(1)} %collective-permute-done.6.beside_ref, f32[384,128]{1,0:T(8,128)S(1)} %collective-permute-done.7.away_ref, f32[192,128]{1,0:T(8,128)S(1)} %collective-permute-done.down_ref, ...), custom_call_target="tpu_custom_call" | custom-call | flops 2000000000 | bytes 5000000 | tf_op jit(solution)/shard_map/pallas_call | solution.py:401
  61.4 6.0 %all-to-all-done.1.in_ref = f32[32,3,4,128]{3,2,1,0:T(4,128)S(1)} async-done(((f32[32,3,4,128]{3,2,1,0:T(4,128)}), f32[32,3,4,128]{3,2,1,0:T(4,128)S(1)}, u32[]{:S(2)}, u32[]{:S(2)}) %all-to-all-start.1) | async-done | bytes 196640 | tf_op jit(solution)/shard_map/all_to_all | solution.py:340
  67.4 0.0 copy-done.2
  67.4 0.0 copy-done.3
  67.4 1.6 %shard_map.78 = f32[384,128]{1,0:T(8,128)} custom-call(f32[32,3,4,128]{3,2,1,0:T(4,128)S(1)} %all-to-all-done.1.in_ref, f32[2,1024,128]{2,1,0:T(8,128)S(1)} %copy-done.2, f32[8,1024]{1,0:T(8,128)S(1)} %copy-done.3, f32[192,256]{1,0:T(8,128)S(1)} %shard_map.77.near_ref), custom_call_target="tpu_custom_call" | custom-call | flops 600000000 | bytes 2000000 | tf_op jit(solution)/shard_map/pallas_call | solution.py:417
  (3 shorter events, 0.0 us)
Async XLA Ops:
  0.0 20.8 %copy-start = (f32[316,2,64]{0,2,1:T(8,128)S(1)}, f32[316,2,64]{0,2,1:T(8,128)}, u32[]{:S(2)}) copy-start(f32[316,2,64]{0,2,1:T(8,128)} %param.11) | copy-start | bytes 485380
  0.0 35.7 %copy-start.1 = (f32[2,2,6,8,2,128]{5,4,3,2,1,0:T(2,128)S(1)}, f32[2,2,6,8,2,128]{5,4,3,2,1,0:T(2,128)}, u32[]{:S(2)}) copy-start(f32[2,2,6,8,2,128]{5,4,3,2,1,0:T(2,128)} %param.7) | copy-start | bytes 589828
  3.4 23.9 %all-to-all-start = ((f32[32,3,4,128]{3,2,1,0:T(4,128)}), f32[32,3,4,128]{3,2,1,0:T(4,128)S(1)}, u32[]{:S(2)}, u32[]{:S(2)}) async-start(f32[32,3,4,128]{3,2,1,0:T(4,128)} %get-tuple-element.16), calls=%async_computation | async-start | bytes 393216 | tf_op jit(solution)/shard_map/all_to_all | solution.py:340
  14.8 7.2 %collective-permute-start = (f32[192,128]{1,0:T(8,128)}, f32[192,128]{1,0:T(8,128)S(1)}, u32[]{:S(2)}, u32[]{:S(2)}) collective-permute-start(f32[192,128]{1,0:T(8,128)} %get-tuple-element.17), channel_id=1, source_target_pairs={{0,1},{1,2},{2,3},{3,4},{4,5},{5,6},{6,7},{7,8},{8,9},{9,10},{10,1... | collective-permute-start | bytes 294920 | tf_op jit(solution)/shard_map/ppermute | solution.py:370
  18.5 6.9 %collective-permute-start.1 = (f32[192,128]{1,0:T(8,128)}, f32[192,128]{1,0:T(8,128)S(1)}, u32[]{:S(2)}, u32[]{:S(2)}) collective-permute-start(f32[192,128]{1,0:T(8,128)} %get-tuple-element.18), channel_id=1, source_target_pairs={{1,0},{2,1},{3,2},{4,3},{5,4},{6,5},{7,6},{8,7},{9,8},{10,9},{11,1... | collective-permute-start | bytes 294920 | tf_op jit(solution)/shard_map/ppermute | solution.py:371
  33.2 2.5 %collective-permute-start.2 = (f32[3,96,4,128]{3,2,1,0:T(4,128)S(1)}, f32[3,96,4,128]{3,2,1,0:T(4,128)S(1)}, u32[]{:S(2)}, u32[]{:S(2)}) collective-permute-start(f32[3,96,4,128]{3,2,1,0:T(4,128)S(1)} %get-tuple-element.20), channel_id=1, source_target_pairs={{0,16},{1,17},{2,18},{3,19},{4,20},{5,21},{6,22},{7,23},{8,24},{9,... | collective-permute-start | bytes 1769480 | tf_op jit(solution)/shard_map/ppermute | solution.py:336
  33.3 8.3 %collective-permute-start.3 = (f32[96,4,128]{2,1,0:T(4,128)S(1)}, f32[96,4,128]{2,1,0:T(4,128)S(1)}, u32[]{:S(2)}, u32[]{:S(2)}) collective-permute-start(f32[96,4,128]{2,1,0:T(4,128)S(1)} %get-tuple-element.22), channel_id=1, source_target_pairs={{0,80},{1,81},{2,82},{3,83},{4,84},{5,85},{6,86},{7,87},{8,88},{9,... | collective-permute-start | bytes 589832 | tf_op jit(solution)/shard_map/ppermute | solution.py:336
  35.9 10.4 %collective-permute-start.4 = (f32[96,4,128]{2,1,0:T(4,128)S(1)}, f32[96,4,128]{2,1,0:T(4,128)S(1)}, u32[]{:S(2)}, u32[]{:S(2)}) collective-permute-start(f32[96,4,128]{2,1,0:T(4,128)S(1)} %get-tuple-element.23), channel_id=1, source_target_pairs={{0,96},{1,97},{2,98},{3,99},{4,100},{5,101},{6,102},{7,103},{8,104... | collective-permute-start | bytes 589832 | tf_op jit(solution)/shard_map/ppermute | solution.py:336
  37.4 9.7 %collective-permute-start.5 = (f32[96,4,128]{2,1,0:T(4,128)S(1)}, f32[96,4,128]{2,1,0:T(4,128)S(1)}, u32[]{:S(2)}, u32[]{:S(2)}) collective-permute-start(f32[96,4,128]{2,1,0:T(4,128)S(1)} %get-tuple-element.24), channel_id=1, source_target_pairs={{0,32},{1,33},{2,34},{3,35},{4,36},{5,37},{6,38},{7,39},{8,40},{9,... | collective-permute-start | bytes 589832 | tf_op jit(solution)/shard_map/ppermute | solution.py:336
  38.0 18.0 %collective-permute-start.6 = (f32[384,128]{1,0:T(8,128)S(1)}, f32[384,128]{1,0:T(8,128)S(1)}, u32[]{:S(2)}, u32[]{:S(2)}) collective-permute-start(f32[384,128]{1,0:T(8,128)S(1)} %get-tuple-element.25), channel_id=1, source_target_pairs={{0,16},{1,17},{2,18},{3,19},{4,20},{5,21},{6,22},{7,23},{8,24},{9,... | collective-permute-start | bytes 589832 | tf_op jit(solution)/shard_map/ppermute | solution.py:336
  38.0 18.0 %collective-permute-start.7 = (f32[384,128]{1,0:T(8,128)S(1)}, f32[384,128]{1,0:T(8,128)S(1)}, u32[]{:S(2)}, u32[]{:S(2)}) collective-permute-start(f32[384,128]{1,0:T(8,128)S(1)} %get-tuple-element.26), channel_id=1, source_target_pairs={{16,32},{32,16},{48,64},{64,48},{80,96},{96,80},{112,128},{128,112... | collective-permute-start | bytes 589832 | tf_op jit(solution)/shard_map/ppermute | solution.py:393
  47.8 19.6 %all-to-all-start.1 = ((f32[32,3,4,128]{3,2,1,0:T(4,128)}), f32[32,3,4,128]{3,2,1,0:T(4,128)S(1)}, u32[]{:S(2)}, u32[]{:S(2)}) async-start(f32[32,3,4,128]{3,2,1,0:T(4,128)} %bitcast.4), calls=%async_computation.1 | async-start | bytes 393216 | tf_op jit(solution)/shard_map/all_to_all | solution.py:340
  56.0 11.4 %copy-start.2 = (f32[2,1024,128]{2,1,0:T(8,128)S(1)}, f32[2,1024,128]{2,1,0:T(8,128)}, u32[]{:S(2)}) copy-start(f32[2,1024,128]{2,1,0:T(8,128)} %rad_ref.1) | copy-start | bytes 3145732
  56.0 11.4 %copy-start.3 = (f32[8,1024]{1,0:T(8,128)S(1)}, f32[8,1024]{1,0:T(8,128)}, u32[]{:S(2)}) copy-start(f32[8,1024]{1,0:T(8,128)} %phase_ref.1) | copy-start | bytes 98308

commit v8 on v7

--- a/solution.py
+++ b/solution.py
@@ -284,7 +284,7 @@
         ref[pl.ds(288, 96), :] = up_ref[pl.ds(pl.multiple_of(row * 96, 8), 96), :]
 
 
-def join_kernel(mid_ref, far_ref, back_ref, ahead_ref, out_ref):
+def join_kernel(mid_ref, far_ref, back_ref, ahead_ref, near_ref, out_ref):
     out_ref[...] = (mid_ref[...] + far_ref[...]) + (back_ref[...] + ahead_ref[...])
 
 
@@ -393,11 +393,6 @@
     away = lax.ppermute(
         away, "slab", [(s, s + 2 * (s % 2) - 1) for s in range(16) if 0 <= s + 2 * (s % 2) - 1 < 16]
     )
-    incoming = call(
-        join_kernel, f32(96, 4, 128), flops=1_000_000, moved=1_000_000
-    )(mid, far_in, back_in, ahead_in)
-    returned = spread(incoming.reshape(32, 3, 4, 128), groups)
-
     near = call(
         near_kernel,
         f32(192, 256),
@@ -414,6 +409,15 @@
         vmem_bytes=50 * 1024 * 1024,
     )(core, rows, beside, away, down, up, near_tiles)
 
+    incoming = call(
+        join_kernel,
+        f32(96, 4, 128),
+        in_specs=[vmem] * 4 + [hbm],
+        flops=1_000_000,
+        moved=1_000_000,
+    )(mid, far_in, back_in, ahead_in, near)
+    returned = spread(incoming.reshape(32, 3, 4, 128), groups)
+
     applied = call(
         disaggregate_kernel,
         f32(384, 128),

time: 69.4 us -> 76.9 us (1.11)
  the two profiles are of different devices: /device:TPU:8 before, /device:TPU:1 now
where the time goes in v8:
time: 76.9 us; the launch traced here: 76.6 us
  starting transfers between devices  27.9 us (36%)
  blocking collectives  20.2 us (26%)
  Pallas kernels  16.2 us (21%)
  waiting for transfers between devices  9.66 us (13%)
  local copies, waits for them, and re-layouts  2.03 us (3%)
    all_to_all x1, blocking collectives, spread(): lax.all_to_all(block, AXES, split_axis=0, concat_axis=0, axis_index_group...  20.2 us
    all_to_all x1, starting transfers between devices, spread(): lax.all_to_all(block, AXES, split_axis=0, concat_axis=0, axis_index_group...  11.9 us
    ppermute x5, starting transfers between devices, moved_by(): return lax.ppermute(block, AXES, route_of(move))  8.39 us
    ppermute x5, waiting for transfers between devices, moved_by(): return lax.ppermute(block, AXES, route_of(move))  6.39 us
    pallas_call x1, Pallas kernels, per_device(): call(translate_kernel, (f32(3, 96, 4, 128), f32(3, 96, 4, 128), f32(96, 4...  5.62 us
    pallas_call x1, Pallas kernels, per_device(): call(near_kernel, f32(192, 256), [pltpu.VMEM((27, 2, 128, 128), F32), plt...  5.31 us
    pallas_call x1, Pallas kernels, per_device(): call(aggregate_kernel, (f32(32, 3, 4, 128), f32(192, 128), f32(192, 128))...  3.41 us
    ppermute x1, starting transfers between devices, per_device(): lax.ppermute(away, 'slab', [(s, s + 2 * (s % 2) - 1) for s in range(16) i...  3.22 us
  transfers between devices with their start and end apart: 9, of which 5 were waited for; matrix products, arithmetic and copies ran while one was open for 3% of the time, Pallas kernels for 7%

profile of v8, /device:TPU:1, one launch (start us, length us, event | category | flops | bytes accessed | tf_op | source)
XLA Modules:
  0.0 76.6 jit_solution(16524378267072360847)
XLA Ops:
  0.0 0.0 copy-start
  0.0 0.0 copy-start.1
  0.0 3.4 %shard_map.73 = (f32[32,3,4,128]{3,2,1,0:T(4,128)}, f32[192,128]{1,0:T(8,128)}, f32[192,128]{1,0:T(8,128)}) custom-call(f32[384,128]{1,0:T(8,128)} %bitcast.9, f32[2,1024,128]{2,1,0:T(8,128)} %rad_ref.1, f32[8,1024]{1,0:T(8,128)} %phase_ref.1), custom_call_target="tpu_custom_call" | custom-call | flops 600000000 | bytes 2000000 | tf_op jit(solution)/shard_map/pallas_call | solution.py:355
  3.4 11.9 %all-to-all-start = ((f32[32,3,4,128]{3,2,1,0:T(4,128)}), f32[32,3,4,128]{3,2,1,0:T(4,128)S(1)}, u32[]{:S(2)}, u32[]{:S(2)}) async-start(f32[32,3,4,128]{3,2,1,0:T(4,128)} %get-tuple-element.16), calls=%async_computation | async-start | bytes 393216 | tf_op jit(solution)/shard_map/all_to_all | solution.py:340
  15.3 3.1 %collective-permute-start = (f32[192,128]{1,0:T(8,128)}, f32[192,128]{1,0:T(8,128)S(1)}, u32[]{:S(2)}, u32[]{:S(2)}) collective-permute-start(f32[192,128]{1,0:T(8,128)} %get-tuple-element.17), channel_id=1, source_target_pairs={{0,1},{1,2},{2,3},{3,4},{4,5},{5,6},{6,7},{7,8},{8,9},{9,10},{10,1... | collective-permute-start | bytes 294920 | tf_op jit(solution)/shard_map/ppermute | solution.py:370
  18.5 1.3 %collective-permute-start.1 = (f32[192,128]{1,0:T(8,128)}, f32[192,128]{1,0:T(8,128)S(1)}, u32[]{:S(2)}, u32[]{:S(2)}) collective-permute-start(f32[192,128]{1,0:T(8,128)} %get-tuple-element.18), channel_id=1, source_target_pairs={{1,0},{2,1},{3,2},{4,3},{5,4},{6,5},{7,6},{8,7},{9,8},{10,9},{11,1... | collective-permute-start | bytes 294920 | tf_op jit(solution)/shard_map/ppermute | solution.py:371
  19.8 0.9 %constant_dynamic-slice_fusion.2 = (s32[48,16]{0,1:T(8,128)S(1)}, s32[48,16]{0,1:T(8,128)S(1)}, s32[48,16]{0,1:T(8,128)S(1)}, s32[48,16]{0,1:T(8,128)S(1)}) fusion(s32[768,16]{0,1:T(8,128)} %param.13, s32[]{:T(128)S(6)} %select_n.86, s32[]{:T(128)S(6)} %select_n.87, s32[768,16]{0,1:T(8,128)} %param.12), kind=kLoop, calls=%fused_computation.43 | loop fusion | bytes 24584 | tf_op jit(solution)/shard_map/dynamic_slice | solution.py:314
  20.6 0.1 add_multiply_fusion
  20.7 0.1 broadcast_divide_fusion
  20.8 0.0 copy-done
  20.8 0.1 sign_compare_fusion.2
  20.9 0.1 copy.9
  21.0 0.1 ne.103
  21.1 0.1 copy.11
  21.2 0.1 div.42
  21.3 0.1 copy.12
  21.4 0.1 mul.41.kinds_ref
  21.5 0.1 copy.10
  21.6 0.1 rem.141
  21.7 0.1 fusion.9.slots_ref
  21.8 0.2 copy.13
  22.0 0.0 collective-permute-done.down_ref
  22.0 2.7 %collective-permute-done.1.up_ref = f32[192,128]{1,0:T(8,128)S(1)} collective-permute-done((f32[192,128]{1,0:T(8,128)}, f32[192,128]{1,0:T(8,128)S(1)}, u32[]{:S(2)}, u32[]{:S(2)}) %collective-permute-start.1) | collective-permute-done | bytes 98336 | tf_op jit(solution)/shard_map/ppermute | solution.py:371
  24.7 0.5 all-to-all-done
  25.2 0.2 broadcast_in_dim.15
  25.5 5.6 %shard_map.74 = (f32[3,96,4,128]{3,2,1,0:T(4,128)S(1)}, f32[3,96,4,128]{3,2,1,0:T(4,128)S(1)}, f32[96,4,128]{2,1,0:T(4,128)S(1)}) custom-call(s32[1536]{0:T(1024)S(1)} %fusion.9.slots_ref, s32[1536]{0:T(1024)S(1)} %mul.41.kinds_ref, f32[2528,128]{1,0:T(8,128)S(1)} %bitcast.6, f32[96,4,128]{2,1,0:T(4,128)S(1)} %bitcast.8, ...), custom_call_target="tpu_custom_call" | custom-call | flops 100000000 | bytes 3000000 | tf_op jit(solution)/shard_map/pallas_call | solution.py:373
  31.1 3.7 %collective-permute-start.2 = (f32[3,96,4,128]{3,2,1,0:T(4,128)S(1)}, f32[3,96,4,128]{3,2,1,0:T(4,128)S(1)}, u32[]{:S(2)}, u32[]{:S(2)}) collective-permute-start(f32[3,96,4,128]{3,2,1,0:T(4,128)S(1)} %get-tuple-element.20), channel_id=1, source_target_pairs={{0,16},{1,17},{2,18},{3,19},{4,20},{5,21},{6,22},{7,23},{8,24},{9,... | collective-permute-start | bytes 1769480 | tf_op jit(solution)/shard_map/ppermute | solution.py:336
  34.8 1.6 %collective-permute-done.2.got_ref = f32[3,96,4,128]{3,2,1,0:T(4,128)S(1)} collective-permute-done((f32[3,96,4,128]{3,2,1,0:T(4,128)S(1)}, f32[3,96,4,128]{3,2,1,0:T(4,128)S(1)}, u32[]{:S(2)}, u32[]{:S(2)}) %collective-permute-start.2) | collective-permute-done | bytes 589856 | tf_op jit(solution)/shard_map/ppermute | solution.py:336
  36.4 0.0 copy-done.1
  36.4 0.2 shard_map.75
  36.6 0.5 collective-permute-start.6
  37.1 3.2 %collective-permute-start.7 = (f32[384,128]{1,0:T(8,128)S(1)}, f32[384,128]{1,0:T(8,128)S(1)}, u32[]{:S(2)}, u32[]{:S(2)}) collective-permute-start(f32[384,128]{1,0:T(8,128)S(1)} %get-tuple-element.26), channel_id=1, source_target_pairs={{16,32},{32,16},{48,64},{64,48},{80,96},{96,80},{112,128},{128,112... | collective-permute-start | bytes 589832 | tf_op jit(solution)/shard_map/ppermute | solution.py:393
  40.3 2.1 %collective-permute-start.3 = (f32[96,4,128]{2,1,0:T(4,128)S(1)}, f32[96,4,128]{2,1,0:T(4,128)S(1)}, u32[]{:S(2)}, u32[]{:S(2)}) collective-permute-start(f32[96,4,128]{2,1,0:T(4,128)S(1)} %get-tuple-element.22), channel_id=1, source_target_pairs={{0,80},{1,81},{2,82},{3,83},{4,84},{5,85},{6,86},{7,87},{8,88},{9,... | collective-permute-start | bytes 589832 | tf_op jit(solution)/shard_map/ppermute | solution.py:336
  42.4 2.1 %collective-permute-start.4 = (f32[96,4,128]{2,1,0:T(4,128)S(1)}, f32[96,4,128]{2,1,0:T(4,128)S(1)}, u32[]{:S(2)}, u32[]{:S(2)}) collective-permute-start(f32[96,4,128]{2,1,0:T(4,128)S(1)} %get-tuple-element.23), channel_id=1, source_target_pairs={{0,96},{1,97},{2,98},{3,99},{4,100},{5,101},{6,102},{7,103},{8,104... | collective-permute-start | bytes 589832 | tf_op jit(solution)/shard_map/ppermute | solution.py:336
  44.5 0.0 copy-start.2
  44.5 0.0 copy-start.3
  44.5 0.0 collective-permute-start.5
  44.5 0.0 collective-permute-done.6.beside_ref
  44.5 0.0 collective-permute-done.7.away_ref
  44.5 5.3 %shard_map.76.near_ref = f32[192,256]{1,0:T(8,128)S(1)} custom-call(s32[1]{0:T(128)} %bitcast.core_ref, f32[384,128]{1,0:T(8,128)S(1)} %bitcast.11, f32[384,128]{1,0:T(8,128)S(1)} %collective-permute-done.6.beside_ref, f32[384,128]{1,0:T(8,128)S(1)} %collective-permute-done.7.away_ref, f32[192,128]{1,0:T(8,128)S(1)} %collective-permute-done.down_ref, ...), custom_call_target="tpu_custom_call" | custom-call | flops 2000000000 | bytes 5000000 | tf_op jit(solution)/shard_map/pallas_call | solution.py:396
  49.9 0.0 collective-permute-done.3.far_ref
  49.9 4.0 %collective-permute-done.4.back_ref = f32[96,4,128]{2,1,0:T(4,128)S(1)} collective-permute-done((f32[96,4,128]{2,1,0:T(4,128)S(1)}, f32[96,4,128]{2,1,0:T(4,128)S(1)}, u32[]{:S(2)}, u32[]{:S(2)}) %collective-permute-start.4) | collective-permute-done | bytes 196640 | tf_op jit(solution)/shard_map/ppermute | solution.py:336
  53.9 0.8 collective-permute-done.5.ahead_ref
  54.6 0.1 shard_map.77
  54.7 20.2 %all_to_all.10.in_ref = f32[32,3,4,128]{3,2,1,0:T(4,128)S(1)} all-to-all(f32[32,3,4,128]{3,2,1,0:T(4,128)S(1)} %bitcast.7), channel_id=1, replica_groups={{0,1,2,3,4,5,6,7,8,9,10,11,12,13,14,15,128,129,130,131,132,133,134,135,..., dimensions={0} | all-to-all | bytes 393216 | tf_op jit(solution)/shard_map/all_to_all | solution.py:340
  74.9 0.0 copy-done.2
  74.9 0.0 copy-done.3
  74.9 1.6 %shard_map.78 = f32[384,128]{1,0:T(8,128)} custom-call(f32[32,3,4,128]{3,2,1,0:T(4,128)S(1)} %all_to_all.10.in_ref, f32[2,1024,128]{2,1,0:T(8,128)S(1)} %copy-done.2, f32[8,1024]{1,0:T(8,128)S(1)} %copy-done.3, f32[192,256]{1,0:T(8,128)S(1)} %shard_map.76.near_ref), custom_call_target="tpu_custom_call" | custom-call | flops 600000000 | bytes 2000000 | tf_op jit(solution)/shard_map/pallas_call | solution.py:421
  (2 shorter events, 0.0 us)
Async XLA Ops:
  0.0 20.8 %copy-start = (f32[316,2,64]{0,2,1:T(8,128)S(1)}, f32[316,2,64]{0,2,1:T(8,128)}, u32[]{:S(2)}) copy-start(f32[316,2,64]{0,2,1:T(8,128)} %param.11) | copy-start | bytes 485380
  0.0 36.4 %copy-start.1 = (f32[2,2,6,8,2,128]{5,4,3,2,1,0:T(2,128)S(1)}, f32[2,2,6,8,2,128]{5,4,3,2,1,0:T(2,128)}, u32[]{:S(2)}) copy-start(f32[2,2,6,8,2,128]{5,4,3,2,1,0:T(2,128)} %param.7) | copy-start | bytes 589828
  3.4 21.8 %all-to-all-start = ((f32[32,3,4,128]{3,2,1,0:T(4,128)}), f32[32,3,4,128]{3,2,1,0:T(4,128)S(1)}, u32[]{:S(2)}, u32[]{:S(2)}) async-start(f32[32,3,4,128]{3,2,1,0:T(4,128)} %get-tuple-element.16), calls=%async_computation | async-start | bytes 393216 | tf_op jit(solution)/shard_map/all_to_all | solution.py:340
  15.3 6.7 %collective-permute-start = (f32[192,128]{1,0:T(8,128)}, f32[192,128]{1,0:T(8,128)S(1)}, u32[]{:S(2)}, u32[]{:S(2)}) collective-permute-start(f32[192,128]{1,0:T(8,128)} %get-tuple-element.17), channel_id=1, source_target_pairs={{0,1},{1,2},{2,3},{3,4},{4,5},{5,6},{6,7},{7,8},{8,9},{9,10},{10,1... | collective-permute-start | bytes 294920 | tf_op jit(solution)/shard_map/ppermute | solution.py:370
  18.5 6.2 %collective-permute-start.1 = (f32[192,128]{1,0:T(8,128)}, f32[192,128]{1,0:T(8,128)S(1)}, u32[]{:S(2)}, u32[]{:S(2)}) collective-permute-start(f32[192,128]{1,0:T(8,128)} %get-tuple-element.18), channel_id=1, source_target_pairs={{1,0},{2,1},{3,2},{4,3},{5,4},{6,5},{7,6},{8,7},{9,8},{10,9},{11,1... | collective-permute-start | bytes 294920 | tf_op jit(solution)/shard_map/ppermute | solution.py:371
  31.1 5.3 %collective-permute-start.2 = (f32[3,96,4,128]{3,2,1,0:T(4,128)S(1)}, f32[3,96,4,128]{3,2,1,0:T(4,128)S(1)}, u32[]{:S(2)}, u32[]{:S(2)}) collective-permute-start(f32[3,96,4,128]{3,2,1,0:T(4,128)S(1)} %get-tuple-element.20), channel_id=1, source_target_pairs={{0,16},{1,17},{2,18},{3,19},{4,20},{5,21},{6,22},{7,23},{8,24},{9,... | collective-permute-start | bytes 1769480 | tf_op jit(solution)/shard_map/ppermute | solution.py:336
  36.6 7.9 %collective-permute-start.6 = (f32[384,128]{1,0:T(8,128)S(1)}, f32[384,128]{1,0:T(8,128)S(1)}, u32[]{:S(2)}, u32[]{:S(2)}) collective-permute-start(f32[384,128]{1,0:T(8,128)S(1)} %get-tuple-element.25), channel_id=1, source_target_pairs={{0,16},{1,17},{2,18},{3,19},{4,20},{5,21},{6,22},{7,23},{8,24},{9,... | collective-permute-start | bytes 589832 | tf_op jit(solution)/shard_map/ppermute | solution.py:336
  37.1 7.4 %collective-permute-start.7 = (f32[384,128]{1,0:T(8,128)S(1)}, f32[384,128]{1,0:T(8,128)S(1)}, u32[]{:S(2)}, u32[]{:S(2)}) collective-permute-start(f32[384,128]{1,0:T(8,128)S(1)} %get-tuple-element.26), channel_id=1, source_target_pairs={{16,32},{32,16},{48,64},{64,48},{80,96},{96,80},{112,128},{128,112... | collective-permute-start | bytes 589832 | tf_op jit(solution)/shard_map/ppermute | solution.py:393
  40.3 9.6 %collective-permute-start.3 = (f32[96,4,128]{2,1,0:T(4,128)S(1)}, f32[96,4,128]{2,1,0:T(4,128)S(1)}, u32[]{:S(2)}, u32[]{:S(2)}) collective-permute-start(f32[96,4,128]{2,1,0:T(4,128)S(1)} %get-tuple-element.22), channel_id=1, source_target_pairs={{0,80},{1,81},{2,82},{3,83},{4,84},{5,85},{6,86},{7,87},{8,88},{9,... | collective-permute-start | bytes 589832 | tf_op jit(solution)/shard_map/ppermute | solution.py:336
  42.4 11.4 %collective-permute-start.4 = (f32[96,4,128]{2,1,0:T(4,128)S(1)}, f32[96,4,128]{2,1,0:T(4,128)S(1)}, u32[]{:S(2)}, u32[]{:S(2)}) collective-permute-start(f32[96,4,128]{2,1,0:T(4,128)S(1)} %get-tuple-element.23), channel_id=1, source_target_pairs={{0,96},{1,97},{2,98},{3,99},{4,100},{5,101},{6,102},{7,103},{8,104... | collective-permute-start | bytes 589832 | tf_op jit(solution)/shard_map/ppermute | solution.py:336
  44.5 30.4 %copy-start.2 = (f32[2,1024,128]{2,1,0:T(8,128)S(1)}, f32[2,1024,128]{2,1,0:T(8,128)}, u32[]{:S(2)}) copy-start(f32[2,1024,128]{2,1,0:T(8,128)} %rad_ref.1) | copy-start | bytes 3145732
  44.5 30.4 %copy-start.3 = (f32[8,1024]{1,0:T(8,128)S(1)}, f32[8,1024]{1,0:T(8,128)}, u32[]{:S(2)}) copy-start(f32[8,1024]{1,0:T(8,128)} %phase_ref.1) | copy-start | bytes 98308
  44.5 10.1 %collective-permute-start.5 = (f32[96,4,128]{2,1,0:T(4,128)S(1)}, f32[96,4,128]{2,1,0:T(4,128)S(1)}, u32[]{:S(2)}, u32[]{:S(2)}) collective-permute-start(f32[96,4,128]{2,1,0:T(4,128)S(1)} %get-tuple-element.24), channel_id=1, source_target_pairs={{0,32},{1,33},{2,34},{3,35},{4,36},{5,37},{6,38},{7,39},{8,40},{9,... | collective-permute-start | bytes 589832 | tf_op jit(solution)/shard_map/ppermute | solution.py:336

commit v9 on v7

--- a/solution.py
+++ b/solution.py
@@ -102,7 +102,7 @@
 
 
 def aggregate_kernel(
-    cur_hbm, rad_hbm, phase_hbm, out_ref, down_ref, up_ref, cur_ref, rad_ref, phase_ref, sems,
+    core_ref, cur_hbm, rad_hbm, phase_hbm, out_ref, one_ref, two_ref, cur_ref, rad_ref, phase_ref, sems,
     unroll=8, groups=(8,),
 ):
     cur_copy = pltpu.make_async_copy(cur_hbm, cur_ref, sems.at[4])
@@ -113,9 +113,11 @@
         if i == 1:
             phase_copy.start()
     cur_copy.wait()
-    for i in range(2):
-        down_ref[pl.ds(i * 96, 96), :] = cur_ref[pl.ds(i * 192 + 96, 96), :]
-        up_ref[pl.ds(i * 96, 96), :] = cur_ref[pl.ds(i * 192, 96), :]
+    core = core_ref[0]
+    for ref, j in ((one_ref, 1 - core), (two_ref, core)):
+        for i in range(2):
+            first = pl.multiple_of(i * 192 + j * 96, 8)
+            ref[pl.ds(i * 96, 96), :] = cur_ref[pl.ds(first, 96), :]
     rows = cur_ref.shape[0] // 2
     x = jnp.concatenate(
         [cur_ref[pl.ds(0, rows, stride=2), :], cur_ref[pl.ds(1, rows, stride=2), :]], axis=1
@@ -184,7 +186,7 @@
 
 
 def near_kernel(
-    core_ref, own_ref, beside_ref, away_ref, down_ref, up_ref, tiles_hbm,
+    core_ref, own_ref, beside_ref, away_ref, one_ref, two_ref, tiles_hbm,
     out_ref, tiles_ref, hi_ref, lo_ref, acc_ref, sems,
 ):
     for i in range(3):
@@ -204,8 +206,8 @@
     for i in range(2):
         for j in range(2):
             put(own_ref, i * 2 + j, 1 + i, 1 + j)
-        put(down_ref, i, 1 + i, 0)
-        put(up_ref, i, 1 + i, 3)
+        put(one_ref, i, 1 + i, 3 * core_ref[0])
+        put(two_ref, i, 1 + i, 3 - 3 * core_ref[0])
     for i, to_y in enumerate((1, 2, 0, 3)):
         put(beside_ref, i, to_beside, to_y)
         put(away_ref, i, to_away, to_y)
@@ -235,7 +237,7 @@
 
 
 def translate_kernel(
-    slots_ref, kinds_ref, table_ref, src_ref, down_ref, up_ref,
+    slots_ref, kinds_ref, table_ref, src_ref, one_ref, two_ref,
     keep_ref, swap_ref, far_ref, acc_ref,
 ):
     acc_ref[...] = jnp.zeros_like(acc_ref)
@@ -271,17 +273,18 @@
 
 
 def fold_kernel(
-    core_ref, keep_ref, got_ref, cur_ref, down_ref, up_ref,
-    back_ref, mid_ref, ahead_ref, beside_ref, away_ref,
+    core_ref, keep_ref, got_ref, cur_ref, one_ref, two_ref,
+    first_ref, mid_ref, second_ref, beside_ref, away_ref,
 ):
-    back_ref[...] = keep_ref[0] + got_ref[0]
+    core = core_ref[0]
+    first_ref[...] = keep_ref[2 - 2 * core] + got_ref[2 - 2 * core]
     mid_ref[...] = keep_ref[1] + got_ref[1]
-    ahead_ref[...] = keep_ref[2] + got_ref[2]
-    core = core_ref[0]
+    second_ref[...] = keep_ref[2 * core] + got_ref[2 * core]
     for ref, row in ((beside_ref, 1 - core), (away_ref, core)):
+        side = pl.ds(pl.multiple_of(row * 96, 8), 96)
         ref[pl.ds(0, 192), :] = cur_ref[pl.ds(pl.multiple_of(row * 192, 8), 192), :]
-        ref[pl.ds(192, 96), :] = down_ref[pl.ds(pl.multiple_of(row * 96, 8), 96), :]
-        ref[pl.ds(288, 96), :] = up_ref[pl.ds(pl.multiple_of(row * 96, 8), 96), :]
+        ref[pl.ds(pl.multiple_of(192 + core * 96, 8), 96), :] = one_ref[side, :]
+        ref[pl.ds(pl.multiple_of(288 - core * 96, 8), 96), :] = two_ref[side, :]
 
 
 def join_kernel(mid_ref, far_ref, back_ref, ahead_ref, out_ref):
@@ -352,7 +355,7 @@
     smem = pl.BlockSpec(memory_space=pltpu.SMEM)
     hbm = pl.BlockSpec(memory_space=pl.ANY)
 
-    patterns, down, up = call(
+    patterns, one, two = call(
         aggregate_kernel,
         (f32(32, 3, 4, 128), f32(192, 128), f32(192, 128)),
         [
@@ -361,14 +364,21 @@
             pltpu.VMEM((8, 1024), F32),
             pltpu.SemaphoreType.DMA((6,)),
         ],
-        in_specs=[hbm] * 3,
+        in_specs=[smem] + [hbm] * 3,
         flops=600_000_000,
         moved=2_000_000,
         vmem_bytes=62 * 1024 * 1024,
-    )(rows, radiation, child_phase)
+    )(core, rows, radiation, child_phase)
     moved = spread(patterns, groups)
-    down = lax.ppermute(down, "dir", [(d, d + 1) for d in range(15)])
-    up = lax.ppermute(up, "dir", [(d + 1, d) for d in range(15)])
+
+    def along_dir(block, sign):
+        def move(z_hi, y, core, d):
+            to = d + sign * (1 - 2 * core)
+            return (z_hi, y, core, to) if 0 <= to < 16 else None
+
+        return moved_by(block, move)
+
+    one, two = along_dir(one, 1), along_dir(two, -1)
 
     keep, swap, far = call(
         translate_kernel,
@@ -377,25 +387,25 @@
         in_specs=[smem, smem, vmem, vmem, hbm, hbm],
         flops=100_000_000,
         moved=3_000_000,
-    )(slots, kinds, table, moved.reshape(96, 4, 128), down, up)
+    )(slots, kinds, table, moved.reshape(96, 4, 128), one, two)
     far_in = moved_by(far, lambda z_hi, y, core, d: (z_hi, (y + 2) % 4, 1 - core, d))
     swap_in = moved_by(swap, lambda z_hi, y, core, d: (z_hi, y, 1 - core, d))
-    back, mid, ahead, beside, away = call(
+    first, mid, second, beside, away = call(
         fold_kernel,
         (f32(96, 4, 128),) * 3 + (f32(384, 128),) * 2,
         in_specs=[smem] + [vmem] * 5,
         flops=1_000_000,
         moved=2_000_000,
-    )(core, keep, swap_in, rows, down, up)
-    back_in = moved_by(back, lambda z_hi, y, core, d: (z_hi, (y + 3) % 4, core, d))
-    ahead_in = moved_by(ahead, lambda z_hi, y, core, d: (z_hi, (y + 1) % 4, core, d))
+    )(core, keep, swap_in, rows, one, two)
+    first_in = moved_by(first, lambda z_hi, y, core, d: (z_hi, (y + 1 + 2 * core) % 4, core, d))
+    second_in = moved_by(second, lambda z_hi, y, core, d: (z_hi, (y + 3 - 2 * core) % 4, core, d))
     beside = moved_by(beside, lambda z_hi, y, core, d: (z_hi, y, 1 - core, d))
     away = lax.ppermute(
         away, "slab", [(s, s + 2 * (s % 2) - 1) for s in range(16) if 0 <= s + 2 * (s % 2) - 1 < 16]
     )
     incoming = call(
         join_kernel, f32(96, 4, 128), flops=1_000_000, moved=1_000_000
-    )(mid, far_in, back_in, ahead_in)
+    )(mid, far_in, first_in, second_in)
     returned = spread(incoming.reshape(32, 3, 4, 128), groups)
 
     near = call(
@@ -412,7 +422,7 @@
         flops=2_000_000_000,
         moved=5_000_000,
         vmem_bytes=50 * 1024 * 1024,
-    )(core, rows, beside, away, down, up, near_tiles)
+    )(core, rows, beside, away, one, two, near_tiles)
 
     applied = call(
         disaggregate_kernel,

time: 69.4 us -> 69.4 us (level)
  waiting for transfers between devices: 17.1 us -> 14.9 us
  starting transfers between devices: 32.5 us -> 34.6 us
    ppermute x5 -> x7, starting transfers between devices: 4.62 us -> 9.61 us  [moved_by(): return lax.ppermute(block, AXES, route_of(move))]
    ppermute x2 -> x0, starting transfers between devices: 4.99 us -> none  [the longest x1 3.7 us: per_device(): down = lax.ppermute(down, 'dir', [(d, d + 1) for d in range(15)])]
    ppermute x2 -> x0, waiting for transfers between devices: 3.34 us -> none  [the longest x1 3.34 us: per_device(): up = lax.ppermute(up, 'dir', [(d + 1, d) for d in range(15)])]
    ppermute x5 -> x7, waiting for transfers between devices: 5.64 us -> 7.77 us  [moved_by(): return lax.ppermute(block, AXES, route_of(move))]
    ppermute x1, starting transfers between devices: 3.36 us -> 4.57 us  [per_device(): lax.ppermute(away, 'slab', [(s, s + 2 * (s % 2) - 1) for s in range(16) i...]
    all_to_all x2, waiting for transfers between devices: 8.1 us -> 7.16 us  [spread(): lax.all_to_all(block, AXES, split_axis=0, concat_axis=0, axis_index_group...]
    all_to_all x2, starting transfers between devices: 19.5 us -> 20.4 us  [spread(): lax.all_to_all(block, AXES, split_axis=0, concat_axis=0, axis_index_group...]
  transfers between devices with their start and end apart: 10 -> 10, of which waited for: 6 -> 5; matrix products, arithmetic and copies ran while one was open for 3% -> 3% of each run, Pallas kernels for 9% -> 9%
where the time goes in v9:
time: 69.4 us; the launch traced here: 69 us
  starting transfers between devices  34.6 us (50%)
  Pallas kernels  16.9 us (24%)
  waiting for transfers between devices  14.9 us (21%)
  local copies, waits for them, and re-layouts  2.04 us (3%)
    all_to_all x2, starting transfers between devices, spread(): lax.all_to_all(block, AXES, split_axis=0, concat_axis=0, axis_index_group...  20.4 us
    ppermute x7, starting transfers between devices, moved_by(): return lax.ppermute(block, AXES, route_of(move))  9.61 us
    ppermute x7, waiting for transfers between devices, moved_by(): return lax.ppermute(block, AXES, route_of(move))  7.77 us
    all_to_all x2, waiting for transfers between devices, spread(): lax.all_to_all(block, AXES, split_axis=0, concat_axis=0, axis_index_group...  7.16 us
    pallas_call x1, Pallas kernels, per_device(): call(translate_kernel, (f32(3, 96, 4, 128), f32(3, 96, 4, 128), f32(96, 4...  5.62 us
    pallas_call x1, Pallas kernels, per_device(): call(near_kernel, f32(192, 256), [pltpu.VMEM((27, 2, 128, 128), F32), plt...  5.31 us
    ppermute x1, starting transfers between devices, per_device(): lax.ppermute(away, 'slab', [(s, s + 2 * (s % 2) - 1) for s in range(16) i...  4.57 us
    pallas_call x1, Pallas kernels, per_device(): call(aggregate_kernel, (f32(32, 3, 4, 128), f32(192, 128), f32(192, 128))...  3.42 us
  transfers between devices with their start and end apart: 10, of which 5 were waited for; matrix products, arithmetic and copies ran while one was open for 3% of the time, Pallas kernels for 9%

profile of v9, /device:TPU:8, one launch (start us, length us, event | category | flops | bytes accessed | tf_op | source)
XLA Modules:
  0.0 69.0 jit_solution(14777429678739821953)
XLA Ops:
  0.0 0.0 copy-start
  0.0 3.4 %shard_map.73 = (f32[32,3,4,128]{3,2,1,0:T(4,128)}, f32[192,128]{1,0:T(8,128)}, f32[192,128]{1,0:T(8,128)}) custom-call(s32[1]{0:T(128)} %bitcast.core_ref, f32[384,128]{1,0:T(8,128)} %bitcast.8, f32[2,1024,128]{2,1,0:T(8,128)} %rad_ref.1, f32[8,1024]{1,0:T(8,128)} %phase_ref.1), custom_call_target="tpu_custom_call" | custom-call | flops 600000000 | bytes 2000000 | tf_op jit(solution)/shard_map/pallas_call | solution.py:358
  3.4 11.3 %all-to-all-start = ((f32[32,3,4,128]{3,2,1,0:T(4,128)}), f32[32,3,4,128]{3,2,1,0:T(4,128)S(1)}, u32[]{:S(2)}, u32[]{:S(2)}) async-start(f32[32,3,4,128]{3,2,1,0:T(4,128)} %get-tuple-element.16), calls=%async_computation | async-start | bytes 393216 | tf_op jit(solution)/shard_map/all_to_all | solution.py:343
  14.8 3.7 %collective-permute-start = (f32[192,128]{1,0:T(8,128)}, f32[192,128]{1,0:T(8,128)S(1)}, u32[]{:S(2)}, u32[]{:S(2)}) collective-permute-start(f32[192,128]{1,0:T(8,128)} %get-tuple-element.17), channel_id=1, source_target_pairs={{0,1},{1,2},{2,3},{3,4},{4,5},{5,6},{6,7},{7,8},{8,9},{9,10},{10,1... | collective-permute-start | bytes 294920 | tf_op jit(solution)/shard_map/ppermute | solution.py:339
  18.5 1.3 %collective-permute-start.1 = (f32[192,128]{1,0:T(8,128)}, f32[192,128]{1,0:T(8,128)S(1)}, u32[]{:S(2)}, u32[]{:S(2)}) collective-permute-start(f32[192,128]{1,0:T(8,128)} %get-tuple-element.18), channel_id=1, source_target_pairs={{1,0},{2,1},{3,2},{4,3},{5,4},{6,5},{7,6},{8,7},{9,8},{10,9},{11,1... | collective-permute-start | bytes 294920 | tf_op jit(solution)/shard_map/ppermute | solution.py:339
  19.8 0.9 %constant_dynamic-slice_fusion.2 = (s32[48,16]{0,1:T(8,128)S(1)}, s32[48,16]{0,1:T(8,128)S(1)}, s32[48,16]{0,1:T(8,128)S(1)}, s32[48,16]{0,1:T(8,128)S(1)}) fusion(s32[768,16]{0,1:T(8,128)} %param.13, s32[]{:T(128)S(6)} %select_n.86, s32[]{:T(128)S(6)} %select_n.87, s32[768,16]{0,1:T(8,128)} %param.12), kind=kLoop, calls=%fused_computation.43 | loop fusion | bytes 24584 | tf_op jit(solution)/shard_map/dynamic_slice | solution.py:317
  20.7 0.1 add_multiply_fusion
  20.7 0.1 broadcast_divide_fusion
  20.8 0.0 copy-done
  20.8 0.1 sign_compare_fusion.2
  20.9 0.1 copy.9
  21.0 0.1 ne.103
  21.1 0.1 copy.11
  21.2 0.1 div.42
  21.3 0.1 copy.12
  21.4 0.1 mul.41.kinds_ref
  21.5 0.1 copy.10
  21.6 0.1 rem.141
  21.7 0.1 fusion.9.slots_ref
  21.8 0.2 copy.13
  22.0 0.2 collective-permute-done.one_ref
  22.2 3.1 %collective-permute-done.1.two_ref = f32[192,128]{1,0:T(8,128)S(1)} collective-permute-done((f32[192,128]{1,0:T(8,128)}, f32[192,128]{1,0:T(8,128)S(1)}, u32[]{:S(2)}, u32[]{:S(2)}) %collective-permute-start.1) | collective-permute-done | bytes 98336 | tf_op jit(solution)/shard_map/ppermute | solution.py:339
  25.3 1.1 %all-to-all-done = f32[32,3,4,128]{3,2,1,0:T(4,128)S(1)} async-done(((f32[32,3,4,128]{3,2,1,0:T(4,128)}), f32[32,3,4,128]{3,2,1,0:T(4,128)S(1)}, u32[]{:S(2)}, u32[]{:S(2)}) %all-to-all-start) | async-done | bytes 196640 | tf_op jit(solution)/shard_map/all_to_all | solution.py:343
  26.5 0.2 broadcast_in_dim.15
  26.7 5.6 %shard_map.74 = (f32[3,96,4,128]{3,2,1,0:T(4,128)S(1)}, f32[3,96,4,128]{3,2,1,0:T(4,128)S(1)}, f32[96,4,128]{2,1,0:T(4,128)S(1)}) custom-call(s32[1536]{0:T(1024)S(1)} %fusion.9.slots_ref, s32[1536]{0:T(1024)S(1)} %mul.41.kinds_ref, f32[2528,128]{1,0:T(8,128)S(1)} %bitcast.6, f32[96,4,128]{2,1,0:T(4,128)S(1)} %bitcast.7, ...), custom_call_target="tpu_custom_call" | custom-call | flops 100000000 | bytes 3000000 | tf_op jit(solution)/shard_map/pallas_call | solution.py:383
  32.3 0.1 collective-permute-start.2
  32.4 2.4 %collective-permute-start.3 = (f32[96,4,128]{2,1,0:T(4,128)S(1)}, f32[96,4,128]{2,1,0:T(4,128)S(1)}, u32[]{:S(2)}, u32[]{:S(2)}) collective-permute-start(f32[96,4,128]{2,1,0:T(4,128)S(1)} %get-tuple-element.22), channel_id=1, source_target_pairs={{0,80},{1,81},{2,82},{3,83},{4,84},{5,85},{6,86},{7,87},{8,88},{9,... | collective-permute-start | bytes 589832 | tf_op jit(solution)/shard_map/ppermute | solution.py:339
  34.8 0.0 collective-permute-done.2.got_ref
  34.8 0.0 copy-done.1
  34.8 0.2 shard_map.75
  35.0 1.2 %collective-permute-start.4 = (f32[96,4,128]{2,1,0:T(4,128)S(1)}, f32[96,4,128]{2,1,0:T(4,128)S(1)}, u32[]{:S(2)}, u32[]{:S(2)}) collective-permute-start(f32[96,4,128]{2,1,0:T(4,128)S(1)} %get-tuple-element.23), channel_id=1, source_target_pairs={{0,32},{1,33},{2,34},{3,35},{4,36},{5,37},{6,38},{7,39},{8,40},{9,... | collective-permute-start | bytes 589832 | tf_op jit(solution)/shard_map/ppermute | solution.py:339
  36.2 0.9 %collective-permute-start.5 = (f32[96,4,128]{2,1,0:T(4,128)S(1)}, f32[96,4,128]{2,1,0:T(4,128)S(1)}, u32[]{:S(2)}, u32[]{:S(2)}) collective-permute-start(f32[96,4,128]{2,1,0:T(4,128)S(1)} %get-tuple-element.24), channel_id=1, source_target_pairs={{0,96},{1,97},{2,98},{3,99},{4,100},{5,101},{6,102},{7,103},{8,104... | collective-permute-start | bytes 589832 | tf_op jit(solution)/shard_map/ppermute | solution.py:339
  37.1 0.0 collective-permute-start.6
  37.1 4.6 %collective-permute-start.7 = (f32[384,128]{1,0:T(8,128)S(1)}, f32[384,128]{1,0:T(8,128)S(1)}, u32[]{:S(2)}, u32[]{:S(2)}) collective-permute-start(f32[384,128]{1,0:T(8,128)S(1)} %get-tuple-element.26), channel_id=1, source_target_pairs={{16,32},{32,16},{48,64},{64,48},{80,96},{96,80},{112,128},{128,112... | collective-permute-start | bytes 589832 | tf_op jit(solution)/shard_map/ppermute | solution.py:403
  41.7 0.0 collective-permute-done.3.far_ref
  41.7 4.4 %collective-permute-done.4.back_ref = f32[96,4,128]{2,1,0:T(4,128)S(1)} collective-permute-done((f32[96,4,128]{2,1,0:T(4,128)S(1)}, f32[96,4,128]{2,1,0:T(4,128)S(1)}, u32[]{:S(2)}, u32[]{:S(2)}) %collective-permute-start.4) | collective-permute-done | bytes 196640 | tf_op jit(solution)/shard_map/ppermute | solution.py:339
  46.1 0.0 collective-permute-done.5.ahead_ref
  46.1 0.8 %shard_map.76 = f32[96,4,128]{2,1,0:T(4,128)} custom-call(f32[96,4,128]{2,1,0:T(4,128)S(1)} %get-tuple-element.21.mid_ref, f32[96,4,128]{2,1,0:T(4,128)S(1)} %collective-permute-done.3.far_ref, f32[96,4,128]{2,1,0:T(4,128)S(1)} %collective-permute-done.4.back_ref, f32[96,4,128]{2,1,0:T(4,128)S(1)} %collective-permute-done.5.ahead_ref), custom_call_target="tpu_custom_call" | custom-call | flops 1000000 | bytes 1000000 | tf_op jit(solution)/shard_map/pallas_call | solution.py:406
  46.9 9.1 %all-to-all-start.1 = ((f32[32,3,4,128]{3,2,1,0:T(4,128)}), f32[32,3,4,128]{3,2,1,0:T(4,128)S(1)}, u32[]{:S(2)}, u32[]{:S(2)}) async-start(f32[32,3,4,128]{3,2,1,0:T(4,128)} %bitcast.4), calls=%async_computation.1 | async-start | bytes 393216 | tf_op jit(solution)/shard_map/all_to_all | solution.py:343
  56.0 0.0 copy-start.2
  56.0 0.0 copy-start.3
  56.0 0.0 collective-permute-done.6.beside_ref
  56.0 0.0 collective-permute-done.7.away_ref
  56.1 5.3 %shard_map.77.near_ref = f32[192,256]{1,0:T(8,128)S(1)} custom-call(s32[1]{0:T(128)} %bitcast.core_ref, f32[384,128]{1,0:T(8,128)S(1)} %bitcast.10, f32[384,128]{1,0:T(8,128)S(1)} %collective-permute-done.6.beside_ref, f32[384,128]{1,0:T(8,128)S(1)} %collective-permute-done.7.away_ref, f32[192,128]{1,0:T(8,128)S(1)} %collective-permute-done.one_ref, ...), custom_call_target="tpu_custom_call" | custom-call | flops 2000000000 | bytes 5000000 | tf_op jit(solution)/shard_map/pallas_call | solution.py:411
  61.4 6.0 %all-to-all-done.1.in_ref = f32[32,3,4,128]{3,2,1,0:T(4,128)S(1)} async-done(((f32[32,3,4,128]{3,2,1,0:T(4,128)}), f32[32,3,4,128]{3,2,1,0:T(4,128)S(1)}, u32[]{:S(2)}, u32[]{:S(2)}) %all-to-all-start.1) | async-done | bytes 196640 | tf_op jit(solution)/shard_map/all_to_all | solution.py:343
  67.4 0.0 copy-done.2
  67.4 0.0 copy-done.3
  67.4 1.6 %shard_map.78 = f32[384,128]{1,0:T(8,128)} custom-call(f32[32,3,4,128]{3,2,1,0:T(4,128)S(1)} %all-to-all-done.1.in_ref, f32[2,1024,128]{2,1,0:T(8,128)S(1)} %copy-done.2, f32[8,1024]{1,0:T(8,128)S(1)} %copy-done.3, f32[192,256]{1,0:T(8,128)S(1)} %shard_map.77.near_ref), custom_call_target="tpu_custom_call" | custom-call | flops 600000000 | bytes 2000000 | tf_op jit(solution)/shard_map/pallas_call | solution.py:427
  (3 shorter events, 0.0 us)
Async XLA Ops:
  0.0 20.8 %copy-start = (f32[316,2,64]{0,2,1:T(8,128)S(1)}, f32[316,2,64]{0,2,1:T(8,128)}, u32[]{:S(2)}) copy-start(f32[316,2,64]{0,2,1:T(8,128)} %param.11) | copy-start | bytes 485380
  0.0 34.8 %copy-start.1 = (f32[2,2,6,8,2,128]{5,4,3,2,1,0:T(2,128)S(1)}, f32[2,2,6,8,2,128]{5,4,3,2,1,0:T(2,128)}, u32[]{:S(2)}) copy-start(f32[2,2,6,8,2,128]{5,4,3,2,1,0:T(2,128)} %param.7) | copy-start | bytes 589828
  3.4 23.0 %all-to-all-start = ((f32[32,3,4,128]{3,2,1,0:T(4,128)}), f32[32,3,4,128]{3,2,1,0:T(4,128)S(1)}, u32[]{:S(2)}, u32[]{:S(2)}) async-start(f32[32,3,4,128]{3,2,1,0:T(4,128)} %get-tuple-element.16), calls=%async_computation | async-start | bytes 393216 | tf_op jit(solution)/shard_map/all_to_all | solution.py:343
  14.8 7.4 %collective-permute-start = (f32[192,128]{1,0:T(8,128)}, f32[192,128]{1,0:T(8,128)S(1)}, u32[]{:S(2)}, u32[]{:S(2)}) collective-permute-start(f32[192,128]{1,0:T(8,128)} %get-tuple-element.17), channel_id=1, source_target_pairs={{0,1},{1,2},{2,3},{3,4},{4,5},{5,6},{6,7},{7,8},{8,9},{9,10},{10,1... | collective-permute-start | bytes 294920 | tf_op jit(solution)/shard_map/ppermute | solution.py:339
  18.5 6.9 %collective-permute-start.1 = (f32[192,128]{1,0:T(8,128)}, f32[192,128]{1,0:T(8,128)S(1)}, u32[]{:S(2)}, u32[]{:S(2)}) collective-permute-start(f32[192,128]{1,0:T(8,128)} %get-tuple-element.18), channel_id=1, source_target_pairs={{1,0},{2,1},{3,2},{4,3},{5,4},{6,5},{7,6},{8,7},{9,8},{10,9},{11,1... | collective-permute-start | bytes 294920 | tf_op jit(solution)/shard_map/ppermute | solution.py:339
  32.3 2.5 %collective-permute-start.2 = (f32[3,96,4,128]{3,2,1,0:T(4,128)S(1)}, f32[3,96,4,128]{3,2,1,0:T(4,128)S(1)}, u32[]{:S(2)}, u32[]{:S(2)}) collective-permute-start(f32[3,96,4,128]{3,2,1,0:T(4,128)S(1)} %get-tuple-element.20), channel_id=1, source_target_pairs={{0,16},{1,17},{2,18},{3,19},{4,20},{5,21},{6,22},{7,23},{8,24},{9,... | collective-permute-start | bytes 1769480 | tf_op jit(solution)/shard_map/ppermute | solution.py:339
  32.4 9.3 %collective-permute-start.3 = (f32[96,4,128]{2,1,0:T(4,128)S(1)}, f32[96,4,128]{2,1,0:T(4,128)S(1)}, u32[]{:S(2)}, u32[]{:S(2)}) collective-permute-start(f32[96,4,128]{2,1,0:T(4,128)S(1)} %get-tuple-element.22), channel_id=1, source_target_pairs={{0,80},{1,81},{2,82},{3,83},{4,84},{5,85},{6,86},{7,87},{8,88},{9,... | collective-permute-start | bytes 589832 | tf_op jit(solution)/shard_map/ppermute | solution.py:339
  35.0 11.1 %collective-permute-start.4 = (f32[96,4,128]{2,1,0:T(4,128)S(1)}, f32[96,4,128]{2,1,0:T(4,128)S(1)}, u32[]{:S(2)}, u32[]{:S(2)}) collective-permute-start(f32[96,4,128]{2,1,0:T(4,128)S(1)} %get-tuple-element.23), channel_id=1, source_target_pairs={{0,32},{1,33},{2,34},{3,35},{4,36},{5,37},{6,38},{7,39},{8,40},{9,... | collective-permute-start | bytes 589832 | tf_op jit(solution)/shard_map/ppermute | solution.py:339
  36.2 9.9 %collective-permute-start.5 = (f32[96,4,128]{2,1,0:T(4,128)S(1)}, f32[96,4,128]{2,1,0:T(4,128)S(1)}, u32[]{:S(2)}, u32[]{:S(2)}) collective-permute-start(f32[96,4,128]{2,1,0:T(4,128)S(1)} %get-tuple-element.24), channel_id=1, source_target_pairs={{0,96},{1,97},{2,98},{3,99},{4,100},{5,101},{6,102},{7,103},{8,104... | collective-permute-start | bytes 589832 | tf_op jit(solution)/shard_map/ppermute | solution.py:339
  37.1 18.9 %collective-permute-start.6 = (f32[384,128]{1,0:T(8,128)S(1)}, f32[384,128]{1,0:T(8,128)S(1)}, u32[]{:S(2)}, u32[]{:S(2)}) collective-permute-start(f32[384,128]{1,0:T(8,128)S(1)} %get-tuple-element.25), channel_id=1, source_target_pairs={{0,16},{1,17},{2,18},{3,19},{4,20},{5,21},{6,22},{7,23},{8,24},{9,... | collective-permute-start | bytes 589832 | tf_op jit(solution)/shard_map/ppermute | solution.py:339
  37.1 18.9 %collective-permute-start.7 = (f32[384,128]{1,0:T(8,128)S(1)}, f32[384,128]{1,0:T(8,128)S(1)}, u32[]{:S(2)}, u32[]{:S(2)}) collective-permute-start(f32[384,128]{1,0:T(8,128)S(1)} %get-tuple-element.26), channel_id=1, source_target_pairs={{16,32},{32,16},{48,64},{64,48},{80,96},{96,80},{112,128},{128,112... | collective-permute-start | bytes 589832 | tf_op jit(solution)/shard_map/ppermute | solution.py:403
  46.9 20.5 %all-to-all-start.1 = ((f32[32,3,4,128]{3,2,1,0:T(4,128)}), f32[32,3,4,128]{3,2,1,0:T(4,128)S(1)}, u32[]{:S(2)}, u32[]{:S(2)}) async-start(f32[32,3,4,128]{3,2,1,0:T(4,128)} %bitcast.4), calls=%async_computation.1 | async-start | bytes 393216 | tf_op jit(solution)/shard_map/all_to_all | solution.py:343
  56.0 11.4 %copy-start.2 = (f32[2,1024,128]{2,1,0:T(8,128)S(1)}, f32[2,1024,128]{2,1,0:T(8,128)}, u32[]{:S(2)}) copy-start(f32[2,1024,128]{2,1,0:T(8,128)} %rad_ref.1) | copy-start | bytes 3145732
  56.0 11.4 %copy-start.3 = (f32[8,1024]{1,0:T(8,128)S(1)}, f32[8,1024]{1,0:T(8,128)}, u32[]{:S(2)}) copy-start(f32[8,1024]{1,0:T(8,128)} %phase_ref.1) | copy-start | bytes 98308

commit v10 on v7

--- a/solution.py
+++ b/solution.py
@@ -261,8 +261,9 @@
     lax.fori_loop(0, 96, source, 0, unroll=4)
 
     def folded(block):
-        part = acc_ref[pl.ds(block * 768, 768), :].reshape(96, 8, 128)
-        return part[:, :4] + part[:, 4:]
+        tiles = acc_ref.reshape(672, 8, 128)
+        rows = pl.ds(block * 96, 96)
+        return tiles[rows, 0:4, :] + tiles[rows, 4:8, :]
 
     for block in range(3):
         keep_ref[block] = folded(block)

time: 69.4 us -> 69.5 us (level)
  no operation moved by 1% of the time
where the time goes in v10:
time: 69.5 us; the launch traced here: 69.2 us
  starting transfers between devices  32.5 us (47%)
  waiting for transfers between devices  17.1 us (25%)
  Pallas kernels  17 us (24%)
  local copies, waits for them, and re-layouts  2.04 us (3%)
    all_to_all x2, starting transfers between devices, spread(): lax.all_to_all(block, AXES, split_axis=0, concat_axis=0, axis_index_group...  19.5 us
    all_to_all x2, waiting for transfers between devices, spread(): lax.all_to_all(block, AXES, split_axis=0, concat_axis=0, axis_index_group...  8.1 us
    pallas_call x1, Pallas kernels, per_device(): call(translate_kernel, (f32(3, 96, 4, 128), f32(3, 96, 4, 128), f32(96, 4...  5.73 us
    ppermute x5, waiting for transfers between devices, moved_by(): return lax.ppermute(block, AXES, route_of(move))  5.64 us
    pallas_call x1, Pallas kernels, per_device(): call(near_kernel, f32(192, 256), [pltpu.VMEM((27, 2, 128, 128), F32), plt...  5.3 us
    ppermute x5, starting transfers between devices, moved_by(): return lax.ppermute(block, AXES, route_of(move))  4.62 us
    ppermute x1, starting transfers between devices, per_device(): down = lax.ppermute(down, 'dir', [(d, d + 1) for d in range(15)])  3.7 us
    pallas_call x1, Pallas kernels, per_device(): call(aggregate_kernel, (f32(32, 3, 4, 128), f32(192, 128), f32(192, 128))...  3.42 us
  transfers between devices with their start and end apart: 10, of which 6 were waited for; matrix products, arithmetic and copies ran while one was open for 3% of the time, Pallas kernels for 9%

profile of v10, /device:TPU:8, one launch (start us, length us, event | category | flops | bytes accessed | tf_op | source)
XLA Modules:
  0.0 69.2 jit_solution(882396090419810955)
XLA Ops:
  0.0 0.0 copy-start
  0.0 3.4 %shard_map.73 = (f32[32,3,4,128]{3,2,1,0:T(4,128)}, f32[192,128]{1,0:T(8,128)}, f32[192,128]{1,0:T(8,128)}) custom-call(f32[384,128]{1,0:T(8,128)} %bitcast.8, f32[2,1024,128]{2,1,0:T(8,128)} %rad_ref.1, f32[8,1024]{1,0:T(8,128)} %phase_ref.1), custom_call_target="tpu_custom_call" | custom-call | flops 600000000 | bytes 2000000 | tf_op jit(solution)/shard_map/pallas_call | solution.py:356
  3.4 11.3 %all-to-all-start = ((f32[32,3,4,128]{3,2,1,0:T(4,128)}), f32[32,3,4,128]{3,2,1,0:T(4,128)S(1)}, u32[]{:S(2)}, u32[]{:S(2)}) async-start(f32[32,3,4,128]{3,2,1,0:T(4,128)} %get-tuple-element.16), calls=%async_computation | async-start | bytes 393216 | tf_op jit(solution)/shard_map/all_to_all | solution.py:341
  14.8 3.7 %collective-permute-start = (f32[192,128]{1,0:T(8,128)}, f32[192,128]{1,0:T(8,128)S(1)}, u32[]{:S(2)}, u32[]{:S(2)}) collective-permute-start(f32[192,128]{1,0:T(8,128)} %get-tuple-element.17), channel_id=1, source_target_pairs={{0,1},{1,2},{2,3},{3,4},{4,5},{5,6},{6,7},{7,8},{8,9},{9,10},{10,1... | collective-permute-start | bytes 294920 | tf_op jit(solution)/shard_map/ppermute | solution.py:371
  18.5 1.3 %collective-permute-start.1 = (f32[192,128]{1,0:T(8,128)}, f32[192,128]{1,0:T(8,128)S(1)}, u32[]{:S(2)}, u32[]{:S(2)}) collective-permute-start(f32[192,128]{1,0:T(8,128)} %get-tuple-element.18), channel_id=1, source_target_pairs={{1,0},{2,1},{3,2},{4,3},{5,4},{6,5},{7,6},{8,7},{9,8},{10,9},{11,1... | collective-permute-start | bytes 294920 | tf_op jit(solution)/shard_map/ppermute | solution.py:372
  19.8 0.9 %constant_dynamic-slice_fusion.2 = (s32[48,16]{0,1:T(8,128)S(1)}, s32[48,16]{0,1:T(8,128)S(1)}, s32[48,16]{0,1:T(8,128)S(1)}, s32[48,16]{0,1:T(8,128)S(1)}) fusion(s32[768,16]{0,1:T(8,128)} %param.13, s32[]{:T(128)S(6)} %select_n.86, s32[]{:T(128)S(6)} %select_n.87, s32[768,16]{0,1:T(8,128)} %param.12), kind=kLoop, calls=%fused_computation.43 | loop fusion | bytes 24584 | tf_op jit(solution)/shard_map/dynamic_slice | solution.py:315
  20.7 0.1 add_multiply_fusion
  20.7 0.1 broadcast_divide_fusion
  20.8 0.0 copy-done
  20.8 0.1 sign_compare_fusion.2
  20.9 0.1 copy.9
  21.0 0.1 ne.103
  21.2 0.1 copy.11
  21.2 0.1 div.42
  21.3 0.1 copy.12
  21.4 0.1 mul.41.kinds_ref
  21.5 0.1 copy.10
  21.6 0.1 rem.141
  21.7 0.1 fusion.9.slots_ref
  21.8 0.2 copy.13
  22.0 0.0 collective-permute-done.down_ref
  22.0 3.3 %collective-permute-done.1.up_ref = f32[192,128]{1,0:T(8,128)S(1)} collective-permute-done((f32[192,128]{1,0:T(8,128)}, f32[192,128]{1,0:T(8,128)S(1)}, u32[]{:S(2)}, u32[]{:S(2)}) %collective-permute-start.1) | collective-permute-done | bytes 98336 | tf_op jit(solution)/shard_map/ppermute | solution.py:372
  25.3 2.0 %all-to-all-done = f32[32,3,4,128]{3,2,1,0:T(4,128)S(1)} async-done(((f32[32,3,4,128]{3,2,1,0:T(4,128)}), f32[32,3,4,128]{3,2,1,0:T(4,128)S(1)}, u32[]{:S(2)}, u32[]{:S(2)}) %all-to-all-start) | async-done | bytes 196640 | tf_op jit(solution)/shard_map/all_to_all | solution.py:341
  27.4 0.2 broadcast_in_dim.15
  27.6 5.7 %shard_map.74 = (f32[3,96,4,128]{3,2,1,0:T(4,128)S(1)}, f32[3,96,4,128]{3,2,1,0:T(4,128)S(1)}, f32[96,4,128]{2,1,0:T(4,128)S(1)}) custom-call(s32[1536]{0:T(1024)S(1)} %fusion.9.slots_ref, s32[1536]{0:T(1024)S(1)} %mul.41.kinds_ref, f32[2528,128]{1,0:T(8,128)S(1)} %bitcast.6, f32[96,4,128]{2,1,0:T(4,128)S(1)} %bitcast.7, ...), custom_call_target="tpu_custom_call" | custom-call | flops 100000000 | bytes 3000000 | tf_op jit(solution)/shard_map/pallas_call | solution.py:374
  33.3 0.1 collective-permute-start.2
  33.4 2.4 %collective-permute-start.3 = (f32[96,4,128]{2,1,0:T(4,128)S(1)}, f32[96,4,128]{2,1,0:T(4,128)S(1)}, u32[]{:S(2)}, u32[]{:S(2)}) collective-permute-start(f32[96,4,128]{2,1,0:T(4,128)S(1)} %get-tuple-element.22), channel_id=1, source_target_pairs={{0,80},{1,81},{2,82},{3,83},{4,84},{5,85},{6,86},{7,87},{8,88},{9,... | collective-permute-start | bytes 589832 | tf_op jit(solution)/shard_map/ppermute | solution.py:337
  35.9 0.0 collective-permute-done.2.got_ref
  35.9 0.0 copy-done.1
  35.9 0.2 shard_map.75
  36.1 1.4 %collective-permute-start.4 = (f32[96,4,128]{2,1,0:T(4,128)S(1)}, f32[96,4,128]{2,1,0:T(4,128)S(1)}, u32[]{:S(2)}, u32[]{:S(2)}) collective-permute-start(f32[96,4,128]{2,1,0:T(4,128)S(1)} %get-tuple-element.23), channel_id=1, source_target_pairs={{0,96},{1,97},{2,98},{3,99},{4,100},{5,101},{6,102},{7,103},{8,104... | collective-permute-start | bytes 589832 | tf_op jit(solution)/shard_map/ppermute | solution.py:337
  37.5 0.7 collective-permute-start.5
  38.2 0.0 collective-permute-start.6
  38.2 3.4 %collective-permute-start.7 = (f32[384,128]{1,0:T(8,128)S(1)}, f32[384,128]{1,0:T(8,128)S(1)}, u32[]{:S(2)}, u32[]{:S(2)}) collective-permute-start(f32[384,128]{1,0:T(8,128)S(1)} %get-tuple-element.26), channel_id=1, source_target_pairs={{16,32},{32,16},{48,64},{64,48},{80,96},{96,80},{112,128},{128,112... | collective-permute-start | bytes 589832 | tf_op jit(solution)/shard_map/ppermute | solution.py:394
  41.5 0.3 collective-permute-done.3.far_ref
  41.8 4.7 %collective-permute-done.4.back_ref = f32[96,4,128]{2,1,0:T(4,128)S(1)} collective-permute-done((f32[96,4,128]{2,1,0:T(4,128)S(1)}, f32[96,4,128]{2,1,0:T(4,128)S(1)}, u32[]{:S(2)}, u32[]{:S(2)}) %collective-permute-start.4) | collective-permute-done | bytes 196640 | tf_op jit(solution)/shard_map/ppermute | solution.py:337
  46.5 0.7 %collective-permute-done.5.ahead_ref = f32[96,4,128]{2,1,0:T(4,128)S(1)} collective-permute-done((f32[96,4,128]{2,1,0:T(4,128)S(1)}, f32[96,4,128]{2,1,0:T(4,128)S(1)}, u32[]{:S(2)}, u32[]{:S(2)}) %collective-permute-start.5) | collective-permute-done | bytes 196640 | tf_op jit(solution)/shard_map/ppermute | solution.py:337
  47.2 0.8 %shard_map.76 = f32[96,4,128]{2,1,0:T(4,128)} custom-call(f32[96,4,128]{2,1,0:T(4,128)S(1)} %get-tuple-element.21.mid_ref, f32[96,4,128]{2,1,0:T(4,128)S(1)} %collective-permute-done.3.far_ref, f32[96,4,128]{2,1,0:T(4,128)S(1)} %collective-permute-done.4.back_ref, f32[96,4,128]{2,1,0:T(4,128)S(1)} %collective-permute-done.5.ahead_ref), custom_call_target="tpu_custom_call" | custom-call | flops 1000000 | bytes 1000000 | tf_op jit(solution)/shard_map/pallas_call | solution.py:397
  47.9 8.2 %all-to-all-start.1 = ((f32[32,3,4,128]{3,2,1,0:T(4,128)}), f32[32,3,4,128]{3,2,1,0:T(4,128)S(1)}, u32[]{:S(2)}, u32[]{:S(2)}) async-start(f32[32,3,4,128]{3,2,1,0:T(4,128)} %bitcast.4), calls=%async_computation.1 | async-start | bytes 393216 | tf_op jit(solution)/shard_map/all_to_all | solution.py:341
  56.1 0.0 copy-start.2
  56.1 0.0 copy-start.3
  56.2 0.0 collective-permute-done.6.beside_ref
  56.2 0.0 collective-permute-done.7.away_ref
  56.2 5.3 %shard_map.77.near_ref = f32[192,256]{1,0:T(8,128)S(1)} custom-call(s32[1]{0:T(128)} %bitcast.core_ref, f32[384,128]{1,0:T(8,128)S(1)} %bitcast.10, f32[384,128]{1,0:T(8,128)S(1)} %collective-permute-done.6.beside_ref, f32[384,128]{1,0:T(8,128)S(1)} %collective-permute-done.7.away_ref, f32[192,128]{1,0:T(8,128)S(1)} %collective-permute-done.down_ref, ...), custom_call_target="tpu_custom_call" | custom-call | flops 2000000000 | bytes 5000000 | tf_op jit(solution)/shard_map/pallas_call | solution.py:402
  61.5 6.0 %all-to-all-done.1.in_ref = f32[32,3,4,128]{3,2,1,0:T(4,128)S(1)} async-done(((f32[32,3,4,128]{3,2,1,0:T(4,128)}), f32[32,3,4,128]{3,2,1,0:T(4,128)S(1)}, u32[]{:S(2)}, u32[]{:S(2)}) %all-to-all-start.1) | async-done | bytes 196640 | tf_op jit(solution)/shard_map/all_to_all | solution.py:341
  67.5 0.0 copy-done.2
  67.5 0.0 copy-done.3
  67.5 1.6 %shard_map.78 = f32[384,128]{1,0:T(8,128)} custom-call(f32[32,3,4,128]{3,2,1,0:T(4,128)S(1)} %all-to-all-done.1.in_ref, f32[2,1024,128]{2,1,0:T(8,128)S(1)} %copy-done.2, f32[8,1024]{1,0:T(8,128)S(1)} %copy-done.3, f32[192,256]{1,0:T(8,128)S(1)} %shard_map.77.near_ref), custom_call_target="tpu_custom_call" | custom-call | flops 600000000 | bytes 2000000 | tf_op jit(solution)/shard_map/pallas_call | solution.py:418
  (3 shorter events, 0.0 us)
Async XLA Ops:
  0.0 20.8 %copy-start = (f32[316,2,64]{0,2,1:T(8,128)S(1)}, f32[316,2,64]{0,2,1:T(8,128)}, u32[]{:S(2)}) copy-start(f32[316,2,64]{0,2,1:T(8,128)} %param.11) | copy-start | bytes 485380
  0.0 35.9 %copy-start.1 = (f32[2,2,6,8,2,128]{5,4,3,2,1,0:T(2,128)S(1)}, f32[2,2,6,8,2,128]{5,4,3,2,1,0:T(2,128)}, u32[]{:S(2)}) copy-start(f32[2,2,6,8,2,128]{5,4,3,2,1,0:T(2,128)} %param.7) | copy-start | bytes 589828
  3.4 23.9 %all-to-all-start = ((f32[32,3,4,128]{3,2,1,0:T(4,128)}), f32[32,3,4,128]{3,2,1,0:T(4,128)S(1)}, u32[]{:S(2)}, u32[]{:S(2)}) async-start(f32[32,3,4,128]{3,2,1,0:T(4,128)} %get-tuple-element.16), calls=%async_computation | async-start | bytes 393216 | tf_op jit(solution)/shard_map/all_to_all | solution.py:341
  14.8 7.2 %collective-permute-start = (f32[192,128]{1,0:T(8,128)}, f32[192,128]{1,0:T(8,128)S(1)}, u32[]{:S(2)}, u32[]{:S(2)}) collective-permute-start(f32[192,128]{1,0:T(8,128)} %get-tuple-element.17), channel_id=1, source_target_pairs={{0,1},{1,2},{2,3},{3,4},{4,5},{5,6},{6,7},{7,8},{8,9},{9,10},{10,1... | collective-permute-start | bytes 294920 | tf_op jit(solution)/shard_map/ppermute | solution.py:371
  18.5 6.9 %collective-permute-start.1 = (f32[192,128]{1,0:T(8,128)}, f32[192,128]{1,0:T(8,128)S(1)}, u32[]{:S(2)}, u32[]{:S(2)}) collective-permute-start(f32[192,128]{1,0:T(8,128)} %get-tuple-element.18), channel_id=1, source_target_pairs={{1,0},{2,1},{3,2},{4,3},{5,4},{6,5},{7,6},{8,7},{9,8},{10,9},{11,1... | collective-permute-start | bytes 294920 | tf_op jit(solution)/shard_map/ppermute | solution.py:372
  33.3 2.5 %collective-permute-start.2 = (f32[3,96,4,128]{3,2,1,0:T(4,128)S(1)}, f32[3,96,4,128]{3,2,1,0:T(4,128)S(1)}, u32[]{:S(2)}, u32[]{:S(2)}) collective-permute-start(f32[3,96,4,128]{3,2,1,0:T(4,128)S(1)} %get-tuple-element.20), channel_id=1, source_target_pairs={{0,16},{1,17},{2,18},{3,19},{4,20},{5,21},{6,22},{7,23},{8,24},{9,... | collective-permute-start | bytes 1769480 | tf_op jit(solution)/shard_map/ppermute | solution.py:337
  33.4 8.3 %collective-permute-start.3 = (f32[96,4,128]{2,1,0:T(4,128)S(1)}, f32[96,4,128]{2,1,0:T(4,128)S(1)}, u32[]{:S(2)}, u32[]{:S(2)}) collective-permute-start(f32[96,4,128]{2,1,0:T(4,128)S(1)} %get-tuple-element.22), channel_id=1, source_target_pairs={{0,80},{1,81},{2,82},{3,83},{4,84},{5,85},{6,86},{7,87},{8,88},{9,... | collective-permute-start | bytes 589832 | tf_op jit(solution)/shard_map/ppermute | solution.py:337
  36.1 10.4 %collective-permute-start.4 = (f32[96,4,128]{2,1,0:T(4,128)S(1)}, f32[96,4,128]{2,1,0:T(4,128)S(1)}, u32[]{:S(2)}, u32[]{:S(2)}) collective-permute-start(f32[96,4,128]{2,1,0:T(4,128)S(1)} %get-tuple-element.23), channel_id=1, source_target_pairs={{0,96},{1,97},{2,98},{3,99},{4,100},{5,101},{6,102},{7,103},{8,104... | collective-permute-start | bytes 589832 | tf_op jit(solution)/shard_map/ppermute | solution.py:337
  37.5 9.7 %collective-permute-start.5 = (f32[96,4,128]{2,1,0:T(4,128)S(1)}, f32[96,4,128]{2,1,0:T(4,128)S(1)}, u32[]{:S(2)}, u32[]{:S(2)}) collective-permute-start(f32[96,4,128]{2,1,0:T(4,128)S(1)} %get-tuple-element.24), channel_id=1, source_target_pairs={{0,32},{1,33},{2,34},{3,35},{4,36},{5,37},{6,38},{7,39},{8,40},{9,... | collective-permute-start | bytes 589832 | tf_op jit(solution)/shard_map/ppermute | solution.py:337
  38.2 18.0 %collective-permute-start.6 = (f32[384,128]{1,0:T(8,128)S(1)}, f32[384,128]{1,0:T(8,128)S(1)}, u32[]{:S(2)}, u32[]{:S(2)}) collective-permute-start(f32[384,128]{1,0:T(8,128)S(1)} %get-tuple-element.25), channel_id=1, source_target_pairs={{0,16},{1,17},{2,18},{3,19},{4,20},{5,21},{6,22},{7,23},{8,24},{9,... | collective-permute-start | bytes 589832 | tf_op jit(solution)/shard_map/ppermute | solution.py:337
  38.2 18.0 %collective-permute-start.7 = (f32[384,128]{1,0:T(8,128)S(1)}, f32[384,128]{1,0:T(8,128)S(1)}, u32[]{:S(2)}, u32[]{:S(2)}) collective-permute-start(f32[384,128]{1,0:T(8,128)S(1)} %get-tuple-element.26), channel_id=1, source_target_pairs={{16,32},{32,16},{48,64},{64,48},{80,96},{96,80},{112,128},{128,112... | collective-permute-start | bytes 589832 | tf_op jit(solution)/shard_map/ppermute | solution.py:394
  47.9 19.6 %all-to-all-start.1 = ((f32[32,3,4,128]{3,2,1,0:T(4,128)}), f32[32,3,4,128]{3,2,1,0:T(4,128)S(1)}, u32[]{:S(2)}, u32[]{:S(2)}) async-start(f32[32,3,4,128]{3,2,1,0:T(4,128)} %bitcast.4), calls=%async_computation.1 | async-start | bytes 393216 | tf_op jit(solution)/shard_map/all_to_all | solution.py:341
  56.1 11.4 %copy-start.2 = (f32[2,1024,128]{2,1,0:T(8,128)S(1)}, f32[2,1024,128]{2,1,0:T(8,128)}, u32[]{:S(2)}) copy-start(f32[2,1024,128]{2,1,0:T(8,128)} %rad_ref.1) | copy-start | bytes 3145732
  56.1 11.4 %copy-start.3 = (f32[8,1024]{1,0:T(8,128)S(1)}, f32[8,1024]{1,0:T(8,128)}, u32[]{:S(2)}) copy-start(f32[8,1024]{1,0:T(8,128)} %phase_ref.1) | copy-start | bytes 98308
